TPU v7x, 128 devices: a whole 4x4x4 slice. The times are simulated.
128 devices in a mesh: blocks: 32 (over y, x, core), depth: 4 (over z).
Axes of the slice: x: 4, y: 4, z: 4, core: 2. Of those that a mesh axis runs over, the one named last changes fastest.
Arguments:
- features: bfloat16 [131072, 128], P(('blocks', 'depth')), may hold values from -6 to 6
- row_owner_index: int32 [131072, 1], P(('blocks', 'depth')), may hold values from 0 to 127; in each aligned block of 1024 rows (0 to 1023, 1024 to 2047, ...) at most 16 rows name the same one
- kernel_map: int32 [128, 27, 2048], P(('blocks', 'depth')), may hold values from 0 to 2560, as said below
- coarse_to_fine_slots: int32 [128, 8, 512], P(('blocks', 'depth')), may hold values from 0 to 2560, as said below
- conv_weight: bfloat16 [27, 128, 128], replicated, may hold values from -0.109375 to 0.109375
- norm_gain: float32 [128], replicated, may hold values from 0.5 to 1.5
- norm_shift: float32 [128], replicated, may hold values from -3 to 3
- down_weight: bfloat16 [8, 128, 256], replicated, may hold values from -0.1875 to 0.1875
Outputs:
- hidden: bfloat16 [262144, 128], P(('blocks', 'depth'))
- coarse: bfloat16 [65536, 256], P(('blocks', 'depth'))
Inputs may be any that keep to these rules, and one draw needn't show every extreme that they name: `kernel_map`: indices into extended; 2560 marks a missing neighbour, offset 13 is the slot itself; otherwise the entry for output slot i lies in i to i + 512. `coarse_to_fine_slots`: indices into hidden_ext; 2560 marks a missing child; otherwise the entry for coarse slot j lies in 4 * j to 4 * j + 512. `row_owner_index`: no shard sends more than 16 rows to one owner.
All inputs are finite; a program needn't handle non-finite values.
Results may differ from a plain program's by a relative error of at most 0.005.
Values may be sent and summed in bfloat16 or wider, within the bound.
No kernel may reach another device: no remote copies, remote signals or barrier semaphores. Data moves between devices by JAX's collectives and lax.ppermute only.
A program may use at most 64 MiB of HBM per device.

v0:
```python
import jax
import jax.numpy as jnp
from jax import lax
from jax.sharding import PartitionSpec as P


def extended_2(cells, sides, width):
    for axis, dim in sides:
        count = lax.axis_size(axis)
        ends = count - 1
        head = lax.slice_in_dim(cells, 0, width, axis=dim)
        tail = lax.slice_in_dim(cells, cells.shape[dim] - width, cells.shape[dim], axis=dim)
        cells = jnp.concatenate(
            [
                lax.ppermute(tail, axis, [(i, (i + 1) % count) for i in range(ends)]),
                cells,
                lax.ppermute(head, axis, [((i + 1) % count, i) for i in range(ends)]),
            ],
            axis=dim,
        )
    return cells


def blocked_select(table, index_map, block_rows, stride, weights):
    offsets_count, out_rows = index_map.shape
    reach_rows = table.shape[0] - stride * out_rows
    window_rows = stride * block_rows + reach_rows
    block_count = out_rows // block_rows
    columns = jnp.arange(window_rows, dtype=jnp.int32)[None, None, :]

    def one_block(block_id):
        start = block_id * block_rows
        picked = lax.dynamic_slice_in_dim(index_map, start, block_rows, 1)
        local = picked - stride * start
        selector = (local[:, :, None] == columns).astype(jnp.bfloat16)
        window = lax.dynamic_slice_in_dim(table, stride * start, window_rows, 0)
        chosen = jnp.einsum(
            "kbw,wc->kbc", selector, window, preferred_element_type=jnp.float32
        ).astype(jnp.bfloat16)
        return jnp.einsum("kbc,kcd->bd", chosen, weights, preferred_element_type=jnp.float32)

    blocks_out = lax.map(one_block, jnp.arange(block_count, dtype=jnp.int32))
    return blocks_out.reshape(out_rows, weights.shape[2])


def shards(
    features,
    row_owner_index,
    kernel_map,
    coarse_to_fine_slots,
    conv_weight,
    norm_gain,
    norm_shift,
    down_weight,
):
    n_blocks = lax.axis_size("blocks")
    n_depth = lax.axis_size("depth")
    ndev = n_blocks * n_depth
    rows, channels = features.shape
    slots_per = 2 * rows // ndev
    owned_rows = ndev * slots_per
    reach = owned_rows // 8
    owners = row_owner_index[:, 0]
    onehot = (owners[:, None] == jnp.arange(ndev, dtype=jnp.int32)[None, :]).astype(jnp.bfloat16)
    row_ids = jnp.arange(rows, dtype=jnp.int32)
    earlier = (row_ids[:, None] > row_ids[None, :]).astype(jnp.bfloat16)
    before_counts = jnp.dot(earlier, onehot, preferred_element_type=jnp.float32)
    ranks = jnp.sum(before_counts * onehot.astype(jnp.float32), axis=1).astype(jnp.int32)
    where_to = owners * slots_per + ranks
    placement = (where_to[:, None] == jnp.arange(owned_rows, dtype=jnp.int32)[None, :]).astype(
        jnp.bfloat16
    )
    buffer = jnp.einsum(
        "rs,rc->sc", placement, features, preferred_element_type=jnp.float32
    ).astype(jnp.bfloat16)
    marks = jnp.sum(placement.astype(jnp.float32), axis=0).astype(jnp.bfloat16)
    owned, occupied = (
        lax.all_to_all(
            buffer.reshape(ndev, slots_per, channels),
            ("blocks", "depth"),
            split_axis=0,
            concat_axis=0,
            tiled=True,
        ),
        lax.all_to_all(
            marks.reshape(ndev, slots_per),
            ("blocks", "depth"),
            split_axis=0,
            concat_axis=0,
            tiled=True,
        ),
    )
    owned = owned.reshape(owned_rows, channels)
    occupied = occupied.reshape(owned_rows).astype(jnp.float32)
    extended = extended_2(owned, ((("blocks", "depth"), 0),), reach)
    conv = blocked_select(extended, kernel_map[0], 256, 1, conv_weight)
    weighted = conv * occupied[:, None]
    first_sum, second_sum = lax.psum(
        (jnp.sum(weighted, axis=0), jnp.sum(weighted * conv, axis=0)), ("blocks", "depth")
    )
    count = jnp.float32(ndev * rows)
    mean = first_sum / count
    squared_moment = second_sum / count
    scale = norm_gain / jnp.sqrt(squared_moment - mean * mean + 1e-05)
    hidden = (occupied[:, None] * jax.nn.relu((conv - mean) * scale + norm_shift)).astype(
        jnp.bfloat16
    )
    hidden_padded = extended_2(hidden, ((("blocks", "depth"), 0),), reach)
    coarse = blocked_select(hidden_padded, coarse_to_fine_slots[0], 64, 4, down_weight)
    return (hidden, coarse.astype(jnp.bfloat16))


def solution(mesh):
    placed = (
        P(("blocks", "depth"), None),
        P(("blocks", "depth"), None),
        P(("blocks", "depth"), None, None),
        P(("blocks", "depth"), None, None),
        P(),
        P(),
        P(),
        P(),
    )
    return jax.shard_map(
        shards,
        mesh=mesh,
        in_specs=placed,
        out_specs=(P(("blocks", "depth"), None), P(("blocks", "depth"), None)),
        check_vma=False,
    )
```

profile of v0, /device:TPU:1, one launch (start us, length us, event | category | flops | bytes accessed | tf_op | source)
XLA Modules:
  0.0 212.1 jit_solution(10417120250083720927)
XLA Ops:
  0.7 1.4 fusion.40
  3.9 11.5 %all-to-all-start = ((bf16[128,1,16]{2,1,0:T(2,128)(2,1)}), bf16[128,1,16]{2,1,0:T(2,128)(2,1)S(1)}, u32[]{:S(2)}, u32[]{:S(2)}) async-start(bf16[128,1,16]{2,1,0:T(2,128)(2,1)} %all_to_all.12), calls=%async_computation | async-start | bytes 131072 | tf_op jit(solution)/shard_map/all_to_all | solution.py:85
  15.4 3.3 %fusion.38 = bf16[2048,128]{1,0:T(8,128)(2,1)} fusion(bf16[1024,128]{1,0:T(8,128)(2,1)S(1)} %copy-done, s32[1024]{0:T(1024)S(1)} %bitcast.76), kind=kOutput, calls=%fused_computation.31 | convolution fusion | flops 539230208 | bytes 790528 | tf_op jit(solution)/shard_map/rs,rc->sc/dot_general | solution.py:73
  18.7 6.3 %all-to-all-done = bf16[128,1,16]{2,1,0:T(2,128)(2,1)S(1)} async-done(((bf16[128,1,16]{2,1,0:T(2,128)(2,1)}), bf16[128,1,16]{2,1,0:T(2,128)(2,1)S(1)}, u32[]{:S(2)}, u32[]{:S(2)}) %all-to-all-start) | async-done | bytes 4128 | tf_op jit(solution)/shard_map/all_to_all | solution.py:85
  25.0 4.3 %all-to-all-start.1 = ((bf16[128,16,128]{2,1,0:T(8,128)(2,1)}), bf16[128,16,128]{2,1,0:T(8,128)(2,1)S(1)}, u32[]{:S(2)}, u32[]{:S(2)}) async-start(bf16[128,16,128]{2,1,0:T(8,128)(2,1)} %bitcast.3), calls=%async_computation.1 | async-start | bytes 1048576 | tf_op jit(solution)/shard_map/all_to_all | solution.py:78
  29.5 13.5 %all-to-all-done.1 = bf16[128,16,128]{2,1,0:T(8,128)(2,1)S(1)} async-done(((bf16[128,16,128]{2,1,0:T(8,128)(2,1)}), bf16[128,16,128]{2,1,0:T(8,128)(2,1)S(1)}, u32[]{:S(2)}, u32[]{:S(2)}) %all-to-all-start.1) | async-done | bytes 524320 | tf_op jit(solution)/shard_map/all_to_all | solution.py:78
  43.0 2.6 %collective-permute-start = (bf16[256,128]{1,0:T(8,128)(2,1)S(1)}, bf16[256,128]{1,0:T(8,128)(2,1)S(1)}, u32[]{:S(2)}, u32[]{:S(2)}) collective-permute-start(bf16[256,128]{1,0:T(8,128)(2,1)S(1)} %bitcast.71), channel_id=1, source_target_pairs={{0,1},{1,2},{2,3},{3,4},{4,5},{5,6},{6,7},{7,8},{8,9},{9,10},{10,1... | collective-permute-start | bytes 196616 | tf_op jit(solution)/shard_map/ppermute | solution.py:15
  45.6 4.2 %collective-permute-start.1 = (bf16[256,128]{1,0:T(8,128)(2,1)S(1)}, bf16[256,128]{1,0:T(8,128)(2,1)S(1)}, u32[]{:S(2)}, u32[]{:S(2)}) collective-permute-start(bf16[256,128]{1,0:T(8,128)(2,1)S(1)} %bitcast.70), channel_id=1, source_target_pairs={{1,0},{2,1},{3,2},{4,3},{5,4},{6,5},{7,6},{8,7},{9,8},{10,9},{11,1... | collective-permute-start | bytes 196616 | tf_op jit(solution)/shard_map/ppermute | solution.py:17
  51.2 52.6 %while.24 = (s32[]{:T(128)}, f32[8,256,128]{2,1,0:T(8,128)S(1)}, s32[8]{0:T(128)S(1)}, s32[27,2048]{1,0:T(8,128)S(1)}, bf16[2560,128]{1,0:T(8,128)(2,1)S(1)}, /*...) while((s32[]{:T(128)}, f32[8,256,128]{2,1,0:T(8,128)S(1)}, ...), condition=%wide.region_3.4_spmd.clone, body=%wide.region_2.3_spmd.clone.sunk | while | flops 1591646976 | bytes 1300688 | solution.py:42
  52.5 5.3 %fusion.64 = f32[8,256,128]{2,1,0:T(8,128)S(1)} fusion(f32[8,256,128]{2,1,0:T(8,128)S(1)} %get-tuple-element.278, s32[]{:T(128)} %get-tuple-element.277, bf16[27,128,128]{2,1,0:T(8,128)(2,1)} %get-tuple-element.293, s32[27,256]{1,0:T(8,128)S(1)} %dynamic-slice_subtract_fusion.4, bf16[2560,128]{1,0:T(8,128)(2,1)S(1)} %get-tuple-element.292, ...), kind=kOutput, calls=%fused_computation.8.clone.1 | convolution fusion | flops 1591640064 | bytes 1245192 | tf_op jit(solution)/shard_map/while/body/eval_jaxpr/kbc,kcd->bd/dot_general | solution.py:40
  59.0 5.3 %fusion.64 = f32[8,256,128]{2,1,0:T(8,128)S(1)} fusion(f32[8,256,128]{2,1,0:T(8,128)S(1)} %get-tuple-element.278, s32[]{:T(128)} %get-tuple-element.277, bf16[27,128,128]{2,1,0:T(8,128)(2,1)} %get-tuple-element.293, s32[27,256]{1,0:T(8,128)S(1)} %dynamic-slice_subtract_fusion.4, bf16[2560,128]{1,0:T(8,128)(2,1)S(1)} %get-tuple-element.292, ...), kind=kOutput, calls=%fused_computation.8.clone.1 | convolution fusion | flops 1591640064 | bytes 1245192 | tf_op jit(solution)/shard_map/while/body/eval_jaxpr/kbc,kcd->bd/dot_general | solution.py:40
  65.6 5.3 %fusion.64 = f32[8,256,128]{2,1,0:T(8,128)S(1)} fusion(f32[8,256,128]{2,1,0:T(8,128)S(1)} %get-tuple-element.278, s32[]{:T(128)} %get-tuple-element.277, bf16[27,128,128]{2,1,0:T(8,128)(2,1)} %get-tuple-element.293, s32[27,256]{1,0:T(8,128)S(1)} %dynamic-slice_subtract_fusion.4, bf16[2560,128]{1,0:T(8,128)(2,1)S(1)} %get-tuple-element.292, ...), kind=kOutput, calls=%fused_computation.8.clone.1 | convolution fusion | flops 1591640064 | bytes 1245192 | tf_op jit(solution)/shard_map/while/body/eval_jaxpr/kbc,kcd->bd/dot_general | solution.py:40
  72.2 5.3 %fusion.64 = f32[8,256,128]{2,1,0:T(8,128)S(1)} fusion(f32[8,256,128]{2,1,0:T(8,128)S(1)} %get-tuple-element.278, s32[]{:T(128)} %get-tuple-element.277, bf16[27,128,128]{2,1,0:T(8,128)(2,1)} %get-tuple-element.293, s32[27,256]{1,0:T(8,128)S(1)} %dynamic-slice_subtract_fusion.4, bf16[2560,128]{1,0:T(8,128)(2,1)S(1)} %get-tuple-element.292, ...), kind=kOutput, calls=%fused_computation.8.clone.1 | convolution fusion | flops 1591640064 | bytes 1245192 | tf_op jit(solution)/shard_map/while/body/eval_jaxpr/kbc,kcd->bd/dot_general | solution.py:40
  78.8 5.3 %fusion.64 = f32[8,256,128]{2,1,0:T(8,128)S(1)} fusion(f32[8,256,128]{2,1,0:T(8,128)S(1)} %get-tuple-element.278, s32[]{:T(128)} %get-tuple-element.277, bf16[27,128,128]{2,1,0:T(8,128)(2,1)} %get-tuple-element.293, s32[27,256]{1,0:T(8,128)S(1)} %dynamic-slice_subtract_fusion.4, bf16[2560,128]{1,0:T(8,128)(2,1)S(1)} %get-tuple-element.292, ...), kind=kOutput, calls=%fused_computation.8.clone.1 | convolution fusion | flops 1591640064 | bytes 1245192 | tf_op jit(solution)/shard_map/while/body/eval_jaxpr/kbc,kcd->bd/dot_general | solution.py:40
  85.3 5.3 %fusion.64 = f32[8,256,128]{2,1,0:T(8,128)S(1)} fusion(f32[8,256,128]{2,1,0:T(8,128)S(1)} %get-tuple-element.278, s32[]{:T(128)} %get-tuple-element.277, bf16[27,128,128]{2,1,0:T(8,128)(2,1)} %get-tuple-element.293, s32[27,256]{1,0:T(8,128)S(1)} %dynamic-slice_subtract_fusion.4, bf16[2560,128]{1,0:T(8,128)(2,1)S(1)} %get-tuple-element.292, ...), kind=kOutput, calls=%fused_computation.8.clone.1 | convolution fusion | flops 1591640064 | bytes 1245192 | tf_op jit(solution)/shard_map/while/body/eval_jaxpr/kbc,kcd->bd/dot_general | solution.py:40
  91.9 5.3 %fusion.64 = f32[8,256,128]{2,1,0:T(8,128)S(1)} fusion(f32[8,256,128]{2,1,0:T(8,128)S(1)} %get-tuple-element.278, s32[]{:T(128)} %get-tuple-element.277, bf16[27,128,128]{2,1,0:T(8,128)(2,1)} %get-tuple-element.293, s32[27,256]{1,0:T(8,128)S(1)} %dynamic-slice_subtract_fusion.4, bf16[2560,128]{1,0:T(8,128)(2,1)S(1)} %get-tuple-element.292, ...), kind=kOutput, calls=%fused_computation.8.clone.1 | convolution fusion | flops 1591640064 | bytes 1245192 | tf_op jit(solution)/shard_map/while/body/eval_jaxpr/kbc,kcd->bd/dot_general | solution.py:40
  98.5 5.3 %fusion.64 = f32[8,256,128]{2,1,0:T(8,128)S(1)} fusion(f32[8,256,128]{2,1,0:T(8,128)S(1)} %get-tuple-element.278, s32[]{:T(128)} %get-tuple-element.277, bf16[27,128,128]{2,1,0:T(8,128)(2,1)} %get-tuple-element.293, s32[27,256]{1,0:T(8,128)S(1)} %dynamic-slice_subtract_fusion.4, bf16[2560,128]{1,0:T(8,128)(2,1)S(1)} %get-tuple-element.292, ...), kind=kOutput, calls=%fused_computation.8.clone.1 | convolution fusion | flops 1591640064 | bytes 1245192 | tf_op jit(solution)/shard_map/while/body/eval_jaxpr/kbc,kcd->bd/dot_general | solution.py:40
  104.1 68.6 %all-reduce = (f32[128]{0:T(128)S(1)}, f32[128]{0:T(128)S(1)}) all-reduce(f32[128]{0:T(128)S(1)} %get-tuple-element.159, f32[128]{0:T(128)S(1)} %get-tuple-element.158), channel_id=1, replica_groups=mesh['blocks'=32,'depth'=4] {'blocks','depth'}, use_global_device_ids=true, to_apply=%region_7.8 | all-reduce | flops 256 | bytes 2048 | tf_op jit(solution)/shard_map/psum | solution.py:98
  173.1 3.0 %collective-permute-start.2 = (bf16[256,128]{1,0:T(8,128)(2,1)S(1)}, bf16[256,128]{1,0:T(8,128)(2,1)S(1)}, u32[]{:S(2)}, u32[]{:S(2)}) collective-permute-start(bf16[256,128]{1,0:T(8,128)(2,1)S(1)} %get-tuple-element.186), channel_id=1, source_target_pairs={{0,1},{1,2},{2,3},{3,4},{4,5},{5,6},{6,7},{7,8},{8,9},{9,10},{10,1... | collective-permute-start | bytes 196616 | tf_op jit(solution)/shard_map/ppermute | solution.py:15
  176.1 3.9 %collective-permute-start.3 = (bf16[256,128]{1,0:T(8,128)(2,1)S(1)}, bf16[256,128]{1,0:T(8,128)(2,1)S(1)}, u32[]{:S(2)}, u32[]{:S(2)}) collective-permute-start(bf16[256,128]{1,0:T(8,128)(2,1)S(1)} %get-tuple-element.187), channel_id=1, source_target_pairs={{1,0},{2,1},{3,2},{4,3},{5,4},{6,5},{7,6},{8,7},{9,8},{10,9},{11,1... | collective-permute-start | bytes 196616 | tf_op jit(solution)/shard_map/ppermute | solution.py:17
  180.1 1.3 collective-permute-done.3
  181.4 30.7 %while.25 = (s32[]{:T(128)}, bf16[8,64,256]{2,1,0:T(8,128)(2,1)}, s32[8]{0:T(128)S(1)}, s32[8,512]{1,0:T(8,128)}, bf16[2560,128]{1,0:T(8,128)(2,1)S(1)}, /*index...) while((s32[]{:T(128)}, bf16[8,64,256]{2,1,0:T(8,128)(2,1)}, ...), condition=%wide.region_9.10_spmd.clone, body=%wide.region_8.9_spmd.clone.sunk | while | flops 134677008 | bytes 795369 | solution.py:42
  199.4 1.2 fusion.67
  203.2 1.2 fusion.67
  (75 shorter events, 27.2 us)
Async XLA Ops:
  0.6 14.8 %copy-start = (bf16[1024,128]{1,0:T(8,128)(2,1)S(1)}, bf16[1024,128]{1,0:T(8,128)(2,1)}, u32[]{:S(2)}) copy-start(bf16[1024,128]{1,0:T(8,128)(2,1)} %param.12) | copy-start | bytes 786436
  0.6 1.4 copy-start.3
  3.9 21.1 %all-to-all-start = ((bf16[128,1,16]{2,1,0:T(2,128)(2,1)}), bf16[128,1,16]{2,1,0:T(2,128)(2,1)S(1)}, u32[]{:S(2)}, u32[]{:S(2)}) async-start(bf16[128,1,16]{2,1,0:T(2,128)(2,1)} %all_to_all.12), calls=%async_computation | async-start | bytes 131072 | tf_op jit(solution)/shard_map/all_to_all | solution.py:85
  18.7 10.6 %copy-start.2 = (s32[1,27,2048]{2,0,1:T(1,128)S(1)}, s32[1,27,2048]{2,0,1:T(1,128)}, u32[]{:S(2)}) copy-start(s32[1,27,2048]{2,0,1:T(1,128)} %param.14) | copy-start | bytes 663556
  25.0 18.1 %all-to-all-start.1 = ((bf16[128,16,128]{2,1,0:T(8,128)(2,1)}), bf16[128,16,128]{2,1,0:T(8,128)(2,1)S(1)}, u32[]{:S(2)}, u32[]{:S(2)}) async-start(bf16[128,16,128]{2,1,0:T(8,128)(2,1)} %bitcast.3), calls=%async_computation.1 | async-start | bytes 1048576 | tf_op jit(solution)/shard_map/all_to_all | solution.py:78
  43.0 7.1 %collective-permute-start = (bf16[256,128]{1,0:T(8,128)(2,1)S(1)}, bf16[256,128]{1,0:T(8,128)(2,1)S(1)}, u32[]{:S(2)}, u32[]{:S(2)}) collective-permute-start(bf16[256,128]{1,0:T(8,128)(2,1)S(1)} %bitcast.71), channel_id=1, source_target_pairs={{0,1},{1,2},{2,3},{3,4},{4,5},{5,6},{6,7},{7,8},{8,9},{9,10},{10,1... | collective-permute-start | bytes 196616 | tf_op jit(solution)/shard_map/ppermute | solution.py:15
  45.6 5.5 %collective-permute-start.1 = (bf16[256,128]{1,0:T(8,128)(2,1)S(1)}, bf16[256,128]{1,0:T(8,128)(2,1)S(1)}, u32[]{:S(2)}, u32[]{:S(2)}) collective-permute-start(bf16[256,128]{1,0:T(8,128)(2,1)S(1)} %bitcast.70), channel_id=1, source_target_pairs={{1,0},{2,1},{3,2},{4,3},{5,4},{6,5},{7,6},{8,7},{9,8},{10,9},{11,1... | collective-permute-start | bytes 196616 | tf_op jit(solution)/shard_map/ppermute | solution.py:17
  103.8 69.0 %copy-start.5 = (f32[128]{0:T(128)S(1)}, f32[128]{0:T(128)}, u32[]{:S(2)}) copy-start(f32[128]{0:T(128)} %param.17) | copy-start | bytes 1540
  103.8 69.0 %copy-start.4 = (f32[128]{0:T(128)S(1)}, f32[128]{0:T(128)}, u32[]{:S(2)}) copy-start(f32[128]{0:T(128)} %param.18) | copy-start | bytes 1540
  173.1 8.3 %copy-start.1 = (bf16[2048,128]{1,0:T(8,128)(2,1)}, bf16[2048,128]{1,0:T(8,128)(2,1)S(1)}, u32[]{:S(2)}) copy-start(bf16[2048,128]{1,0:T(8,128)(2,1)S(1)} %fusion.46) | copy-start | bytes 1572868
  173.1 8.3 %copy-start.6 = (bf16[8,128,256]{2,1,0:T(8,128)(2,1)S(1)}, bf16[8,128,256]{2,1,0:T(8,128)(2,1)}, u32[]{:S(2)}) copy-start(bf16[8,128,256]{2,1,0:T(8,128)(2,1)} %param.19) | copy-start | bytes 1572868
  173.1 6.9 %collective-permute-start.2 = (bf16[256,128]{1,0:T(8,128)(2,1)S(1)}, bf16[256,128]{1,0:T(8,128)(2,1)S(1)}, u32[]{:S(2)}, u32[]{:S(2)}) collective-permute-start(bf16[256,128]{1,0:T(8,128)(2,1)S(1)} %get-tuple-element.186), channel_id=1, source_target_pairs={{0,1},{1,2},{2,3},{3,4},{4,5},{5,6},{6,7},{7,8},{8,9},{9,10},{10,1... | collective-permute-start | bytes 196616 | tf_op jit(solution)/shard_map/ppermute | solution.py:15
  176.1 5.3 %collective-permute-start.3 = (bf16[256,128]{1,0:T(8,128)(2,1)S(1)}, bf16[256,128]{1,0:T(8,128)(2,1)S(1)}, u32[]{:S(2)}, u32[]{:S(2)}) collective-permute-start(bf16[256,128]{1,0:T(8,128)(2,1)S(1)} %get-tuple-element.187), channel_id=1, source_target_pairs={{1,0},{2,1},{3,2},{4,3},{5,4},{6,5},{7,6},{8,7},{9,8},{10,9},{11,1... | collective-permute-start | bytes 196616 | tf_op jit(solution)/shard_map/ppermute | solution.py:17
where the time goes:
time: 216 us; the launch traced here: 212 us
  blocking collectives  68.6 us (32%)
  matrix products  56.8 us (26%)
  starting transfers between devices  29.5 us (14%)
  waiting for transfers between devices  22.1 us (10%)
  loops' own time  15.5 us (7%)
  local copies, waits for them, and re-layouts  10.5 us (5%)
  other arithmetic  8.29 us (4%)
    psum x1, blocking collectives, shards(): lax.psum((jnp.sum(weighted, axis=0), jnp.sum(weighted * conv, axis=0)), (...  68.6 us
    dot_general x16, matrix products, one_block(): jnp.einsum('kbc,kcd->bd', chosen, weights, preferred_element_type=jnp.flo...  52.1 us
    another operation x2, loops' own time, blocked_select(): blocks_out = lax.map(one_block, jnp.arange(block_count, dtype=jnp.int32))  15.5 us
    all_to_all x1, waiting for transfers between devices, shards(): lax.all_to_all(buffer.reshape(ndev, slots_per, channels), ('blocks', 'dep...  13.5 us
    all_to_all x1, starting transfers between devices, shards(): lax.all_to_all(marks.reshape(ndev, slots_per), ('blocks', 'depth'), split...  11.5 us
    dynamic_slice x16, local copies, waits for them, and re-layouts, blocked_select(): blocks_out = lax.map(one_block, jnp.arange(block_count, dtype=jnp.int32))  9.42 us
    ppermute x2, starting transfers between devices, extended_2(): lax.ppermute(head, axis, [((i + 1) % count, i) for i in range(ends)])  8.11 us
    all_to_all x1, waiting for transfers between devices, shards(): lax.all_to_all(marks.reshape(ndev, slots_per), ('blocks', 'depth'), split...  6.25 us
  transfers between devices with their start and end apart: 6, of which 4 were waited for; matrix products, arithmetic and copies ran while one was open for 2% of the time, Pallas kernels for 0%

commit v1 on v0

v1 whole, which is shorter than its diff:
```python
import jax
import jax.numpy as jnp
from jax import lax
from jax.experimental import pallas as pl
from jax.experimental.pallas import tpu as pltpu
from jax.sharding import PartitionSpec as P

AXES = ("blocks", "depth")
CH = 128
SEG = 256
VMEM = pl.BlockSpec(memory_space=pltpu.VMEM)
BF16 = jnp.bfloat16
F32 = jnp.float32


def params():
    return pltpu.CompilerParams(vmem_limit_bytes=40 << 20)


def onehot(where, size, first):
    rows = lax.broadcasted_iota(jnp.int16, (size, where.shape[1]), 0)
    local = jnp.broadcast_to((where - first).astype(jnp.int16), (size, where.shape[1]))
    return jnp.where(rows == local, BF16(1), BF16(0))


def route_body(features_ref, owners_ref, out_ref):
    upper = (
        lax.broadcasted_iota(jnp.int32, (SEG, SEG), 0)
        < lax.broadcasted_iota(jnp.int32, (SEG, SEG), 1)
    ).astype(BF16)
    ones = jnp.ones((SEG, SEG), BF16)
    carry = jnp.zeros((128, SEG), F32)
    where = []
    for c in range(4):
        owners = jnp.concatenate(
            [owners_ref[2 * c : 2 * c + 1, :], owners_ref[2 * c + 1 : 2 * c + 2, :]], axis=1
        )
        hot = onehot(owners, 128, 0)
        before = jnp.dot(hot, upper, preferred_element_type=F32) + carry
        carry = carry + jnp.dot(hot, ones, preferred_element_type=F32)
        rank = jnp.sum(before * hot.astype(F32), axis=0, keepdims=True)
        where.append(owners * 16 + rank.astype(jnp.int32))
    table = jnp.concatenate([features_ref[...], jnp.ones((1024, CH), BF16)], axis=1)
    for s in range(8):
        placed = jnp.concatenate([onehot(w, SEG, SEG * s) for w in where], axis=1)
        found = jnp.dot(placed, table, preferred_element_type=F32)
        out_ref[SEG * s : SEG * (s + 1), :] = jnp.where(
            found[:, CH:] > 0.5, found[:, :CH], jnp.inf
        ).astype(BF16)


def route(features, owners):
    return pl.pallas_call(
        route_body,
        name="route",
        out_shape=jax.ShapeDtypeStruct((2048, CH), BF16),
        in_specs=[VMEM] * 2,
        out_specs=VMEM,
        compiler_params=params(),
    )(features, owners)


def pick(window, local):
    segments = window.shape[0] // CH
    low = jnp.dot(window, onehot(local & (SEG - 1), SEG, 0), preferred_element_type=F32)
    high = jnp.broadcast_to(local >> 8, (CH, SEG))
    out = jnp.zeros((CH, SEG), F32)
    for s in range(segments):
        out = jnp.where(high == s, low[CH * s : CH * (s + 1)], out)
    return out.astype(BF16)


def conv_block(window, index_ref, block, weights_ref, gathered_ref):
    for k in range(27):
        row = k * 16 + 2 * block
        index = jnp.concatenate(
            [index_ref[pl.ds(row, 1), :], index_ref[pl.ds(row + 1, 1), :]], axis=1
        )
        gathered_ref[CH * k : CH * (k + 1), :] = pick(window, index - SEG * block)
    return jnp.dot(weights_ref[...], gathered_ref[...], preferred_element_type=F32)


def turned(raw):
    flat = raw.astype(F32).T
    filled = flat < jnp.inf
    return jnp.where(filled, flat, 0.0).astype(BF16), filled[:1].astype(F32)


def inner_body(raw_ref, index_ref, weights_ref, table_ref, filled_ref, conv_ref, sums_ref, gathered_ref):
    for c in range(8):
        table, filled = turned(raw_ref[SEG * c : SEG * (c + 1), :])
        table_ref[CH * c : CH * (c + 1), :] = table
        filled_ref[:, SEG * c : SEG * (c + 1)] = filled
    sums_ref[...] = jnp.zeros_like(sums_ref)

    def block(b, _):
        window = table_ref[pl.ds(pl.multiple_of(CH * (b - 1), CH), 3 * CH), :]
        conv = conv_block(window, index_ref, b, weights_ref, gathered_ref)
        conv_ref[:, pl.ds(pl.multiple_of(SEG * (b - 1), SEG), SEG)] = conv
        weighted = conv * filled_ref[:, pl.ds(pl.multiple_of(SEG * b, SEG), SEG)]
        sums_ref[:CH] += weighted
        sums_ref[CH:] += weighted * conv
        return 0

    lax.fori_loop(1, 7, block, 0)


def inner(raw, index, weights):
    return pl.pallas_call(
        inner_body,
        name="inner",
        out_shape=(
            jax.ShapeDtypeStruct((8 * CH, SEG), BF16),
            jax.ShapeDtypeStruct((1, 2048), F32),
            jax.ShapeDtypeStruct((CH, 6 * SEG), F32),
            jax.ShapeDtypeStruct((2 * CH, SEG), F32),
        ),
        in_specs=[VMEM] * 3,
        out_specs=(VMEM,) * 4,
        scratch_shapes=[pltpu.VMEM((27 * CH, SEG), BF16)],
        compiler_params=params(),
        cost_estimate=pl.CostEstimate(
            flops=6 * 27 * 2 * 384 * 256 * 256, bytes_accessed=4 << 20, transcendentals=0
        ),
    )(raw, index, weights)


def outer_body(
    ends_ref, before_ref, after_ref, table_ref, filled_ref, sums_ref, index_ref, weights_ref,
    head_ref, tail_ref, rims_ref, send_ref, window_ref, gathered_ref,
):
    table, filled = turned(before_ref[...])
    window_ref[:CH] = table
    rims_ref[:1] = jnp.where(ends_ref[0] > 0, filled, 0.0)
    table, filled = turned(after_ref[...])
    window_ref[5 * CH :] = table
    rims_ref[1:] = jnp.where(ends_ref[1] > 0, filled, 0.0)
    window_ref[CH : 3 * CH] = table_ref[: 2 * CH]
    window_ref[3 * CH : 5 * CH] = table_ref[6 * CH :]
    first = sums_ref[:CH]
    second = sums_ref[CH:]
    for side, out_ref in ((0, head_ref), (1, tail_ref)):
        block = 7 * side
        window = window_ref[3 * CH * side : 3 * CH * (side + 1), :]
        conv = conv_block(window, index_ref, block, weights_ref, gathered_ref)
        out_ref[...] = conv
        weighted = conv * filled_ref[:, SEG * block : SEG * (block + 1)]
        first = first + weighted
        second = second + weighted * conv
    for n, total in ((0, first), (1, second)):
        row = jnp.sum((total[:, :CH] + total[:, CH:]).T, axis=0, keepdims=True)
        send_ref[:, n : n + 1, :] = jnp.broadcast_to(row[None], (128, 1, CH))


def outer(ends, before, after, table, filled, sums, index, weights):
    return pl.pallas_call(
        outer_body,
        name="outer",
        out_shape=(
            jax.ShapeDtypeStruct((CH, SEG), F32),
            jax.ShapeDtypeStruct((CH, SEG), F32),
            jax.ShapeDtypeStruct((2, SEG), F32),
            jax.ShapeDtypeStruct((128, 2, CH), F32),
        ),
        in_specs=[pl.BlockSpec(memory_space=pltpu.SMEM)] + [VMEM] * 7,
        out_specs=(VMEM,) * 4,
        scratch_shapes=[pltpu.VMEM((6 * CH, SEG), BF16), pltpu.VMEM((27 * CH, SEG), BF16)],
        compiler_params=params(),
        cost_estimate=pl.CostEstimate(
            flops=2 * 27 * 2 * 384 * 256 * 256, bytes_accessed=4 << 20, transcendentals=0
        ),
    )(ends, before, after, table, filled, sums, index, weights)


def final_body(
    sums_ref, gain_ref, shift_ref, before_ref, head_ref, conv_ref, tail_ref, after_ref,
    filled_ref, rims_ref, index_ref, weights_ref, hidden_ref, coarse_ref, table_ref, gathered_ref,
):
    totals = jnp.sum(sums_ref[...], axis=0) / 131072.0
    mean = totals[:1]
    scale = gain_ref[...] / jnp.sqrt(totals[1:] - mean * mean + 1e-05)

    def column(row):
        turned_row = jnp.broadcast_to(row, (CH, CH)).T
        return jnp.concatenate([turned_row, turned_row], axis=1)

    mean, scale, shift = column(mean), column(scale), column(shift_ref[...])

    def normal(conv, filled):
        return filled * jnp.maximum((conv - mean) * scale + shift, 0.0)

    table_ref[:CH] = normal(before_ref[...], rims_ref[:1]).astype(BF16)
    table_ref[9 * CH :] = normal(after_ref[...], rims_ref[1:]).astype(BF16)
    for c in range(8):
        if c == 0:
            conv = head_ref[...]
        elif c == 7:
            conv = tail_ref[...]
        else:
            conv = conv_ref[:, SEG * (c - 1) : SEG * c]
        hidden = normal(conv, filled_ref[:, SEG * c : SEG * (c + 1)])
        table_ref[CH * (c + 1) : CH * (c + 2)] = hidden.astype(BF16)
        hidden_ref[SEG * c : SEG * (c + 1), :] = hidden.T.astype(BF16)
    for b in range(4):
        window = table_ref[2 * CH * b : 2 * CH * b + 4 * CH, :]
        for k in range(0, 8, 2):
            index = jnp.concatenate(
                [index_ref[k : k + 1, CH * b : CH * (b + 1)], index_ref[k + 1 : k + 2, CH * b : CH * (b + 1)]],
                axis=1,
            )
            chosen = pick(window, index - 2 * SEG * b)
            gathered_ref[CH * k : CH * (k + 1), CH * b : CH * (b + 1)] = chosen[:, :CH]
            gathered_ref[CH * (k + 1) : CH * (k + 2), CH * b : CH * (b + 1)] = chosen[:, CH:]
    for b in range(2):
        out = jnp.dot(
            weights_ref[...], gathered_ref[:, SEG * b : SEG * (b + 1)], preferred_element_type=F32
        )
        coarse_ref[SEG * b : SEG * (b + 1), :] = out.T.astype(BF16)


def final(sums, gain, shift, before, head, conv, tail, after, filled, rims, index, weights):
    return pl.pallas_call(
        final_body,
        name="final",
        out_shape=(
            jax.ShapeDtypeStruct((2048, CH), BF16),
            jax.ShapeDtypeStruct((512, 2 * CH), BF16),
        ),
        in_specs=[VMEM] * 12,
        out_specs=(VMEM,) * 2,
        scratch_shapes=[pltpu.VMEM((10 * CH, SEG), BF16), pltpu.VMEM((8 * CH, 512), BF16)],
        compiler_params=params(),
    )(sums, gain, shift, before, head, conv, tail, after, filled, rims, index, weights)


def shards(features, owners, kernel_map, fine_slots, conv_weight, gain, shift, down_weight):
    ndev = lax.axis_size("blocks") * lax.axis_size("depth")
    me = lax.axis_index(AXES)
    ends = jnp.stack([me, ndev - 1 - me]).astype(jnp.int32)
    up = [(i, i + 1) for i in range(ndev - 1)]
    down = [(i + 1, i) for i in range(ndev - 1)]
    index = kernel_map.reshape(27 * 16, 128)
    weights = jnp.transpose(conv_weight, (2, 0, 1)).reshape(CH, 27 * CH)
    down_weights = jnp.transpose(down_weight, (2, 0, 1)).reshape(2 * CH, 8 * CH)

    sent = route(features, owners.reshape(8, 128))
    raw = lax.all_to_all(
        sent.reshape(ndev, 16, CH), AXES, split_axis=0, concat_axis=0, tiled=True
    ).reshape(2048, CH)
    raw_before = lax.ppermute(raw[2048 - SEG :], AXES, up)
    raw_after = lax.ppermute(raw[:SEG], AXES, down)
    table, filled, conv, sums = inner(raw, index, weights)
    head, tail, rims, send = outer(ends, raw_before, raw_after, table, filled, sums, index, weights)
    before = lax.ppermute(tail, AXES, up)
    after = lax.ppermute(head, AXES, down)
    totals = lax.all_to_all(send, AXES, split_axis=0, concat_axis=0, tiled=True)
    return final(
        totals, gain.reshape(1, CH), shift.reshape(1, CH), before, head, conv, tail, after,
        filled, rims, fine_slots.reshape(8, 512), down_weights,
    )


def solution(mesh):
    split = P(AXES, None)
    placed = (split, split, P(AXES, None, None), P(AXES, None, None), P(), P(), P(), P())
    return jax.shard_map(
        shards, mesh=mesh, in_specs=placed, out_specs=(split, split), check_vma=False
    )
```

time: 216 us -> 83 us (0.38); the launches traced: 212 us -> 82.6 us
  blocking collectives: 68.6 us -> 0 us
  matrix products: 56.8 us -> 0 us
  Pallas kernels: 0 us -> 22.1 us
  loops' own time: 15.5 us -> 0 us
  other arithmetic: 8.29 us -> 0.08 us
  local copies, waits for them, and re-layouts: 10.5 us -> 3.52 us
  starting transfers between devices: 29.5 us -> 33.8 us
    psum x1 -> x0, blocking collectives: 68.6 us -> none  [shards(): lax.psum((jnp.sum(weighted, axis=0), jnp.sum(weighted * conv, axis=0)), (...]
    dot_general x18 -> x0, matrix products: 56.8 us -> none  [the longest x16 52.1 us: one_block(): jnp.einsum('kbc,kcd->bd', chosen, weights, preferred_element_type=jnp.flo...]
    pallas_call x0 -> x4, Pallas kernels: none -> 22.1 us  [the longest x1 12.1 us: inner(): pl.pallas_call(inner_body, name='inner', out_shape=(jax.ShapeDtypeStruct(...]
    another operation x2 -> x0, loops' own time: 15.5 us -> none  [blocked_select(): blocks_out = lax.map(one_block, jnp.arange(block_count, dtype=jnp.int32))]
    dynamic_slice x16 -> x0, local copies, waits for them, and re-layouts: 9.42 us -> none  [blocked_select(): blocks_out = lax.map(one_block, jnp.arange(block_count, dtype=jnp.int32))]
    sub x16 -> x0, other arithmetic: 6.19 us -> none  [one_block(): local = picked - stride * start]
    all_to_all x2, starting transfers between devices: 15.8 us -> 20.2 us  [the longest x1 11.5 us: shards(): lax.all_to_all(sent.reshape(ndev, 16, CH), AXES, split_axis=0, concat_axi...]
    all_to_all x2, waiting for transfers between devices: 19.7 us -> 22.3 us  [the longest x1 12.6 us: shards(): lax.all_to_all(sent.reshape(ndev, 16, CH), AXES, split_axis=0, concat_axi...]
  transfers between devices with their start and end apart: 6 -> 6, of which waited for: 4 -> 2; matrix products, arithmetic and copies ran while one was open for 2% -> 2% of each run, Pallas kernels for 0% -> 15%
where the time goes in v1:
time: 83 us; the launch traced here: 82.6 us
  starting transfers between devices  33.8 us (41%)
  waiting for transfers between devices  22.3 us (27%)
  Pallas kernels  22.1 us (27%)
  local copies, waits for them, and re-layouts  3.52 us (4%)
    all_to_all x1, waiting for transfers between devices, shards(): lax.all_to_all(sent.reshape(ndev, 16, CH), AXES, split_axis=0, concat_axi...  12.6 us
    pallas_call x1, Pallas kernels, inner(): pl.pallas_call(inner_body, name='inner', out_shape=(jax.ShapeDtypeStruct(...  12.1 us
    all_to_all x1, starting transfers between devices, shards(): lax.all_to_all(sent.reshape(ndev, 16, CH), AXES, split_axis=0, concat_axi...  11.5 us
    all_to_all x1, waiting for transfers between devices, shards(): totals = lax.all_to_all(send, AXES, split_axis=0, concat_axis=0, tiled=True)  9.7 us
    all_to_all x1, starting transfers between devices, shards(): totals = lax.all_to_all(send, AXES, split_axis=0, concat_axis=0, tiled=True)  8.72 us
    pallas_call x1, Pallas kernels, outer(): pl.pallas_call(outer_body, name='outer', out_shape=(jax.ShapeDtypeStruct(...  4.97 us
    ppermute x1, starting transfers between devices, shards(): after = lax.ppermute(head, AXES, down)  4.85 us
    ppermute x1, starting transfers between devices, shards(): raw_after = lax.ppermute(raw[:SEG], AXES, down)  4.18 us
  transfers between devices with their start and end apart: 6, of which 2 were waited for; matrix products, arithmetic and copies ran while one was open for 2% of the time, Pallas kernels for 15%

profile of v1, /device:TPU:1, one launch (start us, length us, event | category | flops | bytes accessed | tf_op | source)
XLA Modules:
  0.0 82.6 jit_solution(16821393477104190155)
XLA Ops:
  0.6 0.9 %copy-done = bf16[1024,128]{1,0:T(8,128)(2,1)S(1)} copy-done((bf16[1024,128]{1,0:T(8,128)(2,1)S(1)}, bf16[1024,128]{1,0:T(8,128)(2,1)}, u32[]{:S(2)}) %copy-start) | copy-done | bytes 262168
  1.6 0.7 copy-done.2
  2.3 2.3 %route.1 = bf16[2048,128]{1,0:T(8,128)(2,1)} custom-call(bf16[1024,128]{1,0:T(8,128)(2,1)S(1)} %copy-done, s32[8,128]{1,0:T(8,128)S(1)} %bitcast.19), custom_call_target="tpu_custom_call" | custom-call | tf_op jit(solution)/shard_map/route/pallas_call | solution.py:53
  4.5 11.5 %all-to-all-start = ((bf16[128,16,128]{2,1,0:T(8,128)(2,1)}), bf16[128,16,128]{2,1,0:T(8,128)(2,1)S(1)}, u32[]{:S(2)}, u32[]{:S(2)}) async-start(bf16[128,16,128]{2,1,0:T(8,128)(2,1)} %bitcast.3), calls=%async_computation | async-start | bytes 1048576 | tf_op jit(solution)/shard_map/all_to_all | solution.py:247
  16.1 1.0 %copy.12.weights_ref = bf16[128,3456]{1,0:T(8,128)(2,1)S(1)} copy(bf16[128,3456]{0,1:T(8,128)(2,1)S(1)} %bitcast.24) | data formatting | bytes 1769472 | tf_op jit(solution)/shard_map/reshape | solution.py:243
  17.1 0.0 copy-start.5
  17.1 0.1 pad_add_fusion.ends_ref
  17.2 12.6 %all-to-all-done = bf16[128,16,128]{2,1,0:T(8,128)(2,1)S(1)} async-done(((bf16[128,16,128]{2,1,0:T(8,128)(2,1)}), bf16[128,16,128]{2,1,0:T(8,128)(2,1)S(1)}, u32[]{:S(2)}, u32[]{:S(2)}) %all-to-all-start) | async-done | bytes 524320 | tf_op jit(solution)/shard_map/all_to_all | solution.py:247
  29.8 2.6 %collective-permute-start = (bf16[256,128]{1,0:T(8,128)(2,1)S(1)}, bf16[256,128]{1,0:T(8,128)(2,1)S(1)}, u32[]{:S(2)}, u32[]{:S(2)}) collective-permute-start(bf16[256,128]{1,0:T(8,128)(2,1)S(1)} %bitcast.27), channel_id=1, source_target_pairs={{0,1},{1,2},{2,3},{3,4},{4,5},{5,6},{6,7},{7,8},{8,9},{9,10},{10,1... | collective-permute-start | bytes 196616 | tf_op jit(solution)/shard_map/ppermute | solution.py:250
  32.4 4.2 %collective-permute-start.1 = (bf16[256,128]{1,0:T(8,128)(2,1)S(1)}, bf16[256,128]{1,0:T(8,128)(2,1)S(1)}, u32[]{:S(2)}, u32[]{:S(2)}) collective-permute-start(bf16[256,128]{1,0:T(8,128)(2,1)S(1)} %bitcast.26), channel_id=1, source_target_pairs={{1,0},{2,1},{3,2},{4,3},{5,4},{6,5},{7,6},{8,7},{9,8},{10,9},{11,1... | collective-permute-start | bytes 196616 | tf_op jit(solution)/shard_map/ppermute | solution.py:251
  36.6 12.1 %inner.1 = (bf16[1024,256]{1,0:T(8,128)(2,1)S(1)}, f32[1,2048]{1,0:T(1,128)S(1)}, f32[128,1536]{1,0:T(8,128)S(1)}, f32[256,256]{1,0:T(8,128)S(1)}) custom-call(bf16[2048,128]{1,0:T(8,128)(2,1)S(1)} %bitcast.17, s32[432,128]{1,0:T(8,128)S(1)} %bitcast.22, bf16[128,3456]{1,0:T(8,128)(2,1)S(1)} %copy.12.weights_ref), custom_call_target="tpu_custom_call" | custom-call | flops 8153726976 | bytes 4194304 | tf_op jit(solution)/shard_map/inner/pallas_call | solution.py:109
  48.7 0.0 collective-permute-done.1.after_ref
  48.7 0.0 copy-start.7
  48.7 5.0 %outer.1 = (f32[128,256]{1,0:T(8,128)S(1)}, f32[128,256]{1,0:T(8,128)S(1)}, f32[2,256]{1,0:T(2,128)S(1)}, f32[128,2,128]{2,1,0:T(2,128)}) custom-call(s32[2]{0:T(128)S(1)} %pad_add_fusion.ends_ref, bf16[256,128]{1,0:T(8,128)(2,1)S(1)} %collective-permute-done.before_ref, bf16[256,128]{1,0:T(8,128)(2,1)S(1)} %collective-permute-done.1.after_ref, ...), custom_call_target="tpu_custom_call" | custom-call | flops 2717908992 | bytes 4194304 | tf_op jit(solution)/shard_map/outer/pallas_call | solution.py:156
  53.7 1.9 %collective-permute-start.2 = (f32[128,256]{1,0:T(8,128)S(1)}, f32[128,256]{1,0:T(8,128)S(1)}, u32[]{:S(2)}, u32[]{:S(2)}) collective-permute-start(f32[128,256]{1,0:T(8,128)S(1)} %get-tuple-element.14.tail_ref), channel_id=1, source_target_pairs={{0,1},{1,2},{2,3},{3,4},{4,5},{5,6},{6,7},{7,8},{8,9},{9,10},{10,1... | collective-permute-start | bytes 393224 | tf_op jit(solution)/shard_map/ppermute | solution.py:254
  55.6 4.9 %collective-permute-start.3 = (f32[128,256]{1,0:T(8,128)S(1)}, f32[128,256]{1,0:T(8,128)S(1)}, u32[]{:S(2)}, u32[]{:S(2)}) collective-permute-start(f32[128,256]{1,0:T(8,128)S(1)} %get-tuple-element.15.head_ref), channel_id=1, source_target_pairs={{1,0},{2,1},{3,2},{4,3},{5,4},{6,5},{7,6},{8,7},{9,8},{10,9},{11,1... | collective-permute-start | bytes 393224 | tf_op jit(solution)/shard_map/ppermute | solution.py:255
  60.5 8.7 %all-to-all-start.1 = ((f32[128,2,128]{2,1,0:T(2,128)}), f32[128,2,128]{2,1,0:T(2,128)S(1)}, u32[]{:S(2)}, u32[]{:S(2)}) async-start(f32[128,2,128]{2,1,0:T(2,128)} %get-tuple-element.13), calls=%async_computation.1 | async-start | bytes 262144 | tf_op jit(solution)/shard_map/all_to_all | solution.py:256
  69.2 0.0 copy-start.1
  69.2 0.2 copy.15.weights_ref
  69.4 9.7 %all-to-all-done.1.sums_ref = f32[128,2,128]{2,1,0:T(2,128)S(1)} async-done(((f32[128,2,128]{2,1,0:T(2,128)}), f32[128,2,128]{2,1,0:T(2,128)S(1)}, u32[]{:S(2)}, u32[]{:S(2)}) %all-to-all-start.1) | async-done | bytes 131104 | tf_op jit(solution)/shard_map/all_to_all | solution.py:256
  79.2 0.0 copy-start.4
  79.2 0.6 copy-done.3
  79.8 0.0 copy-done.4
  79.8 2.8 %final.1 = (bf16[2048,128]{1,0:T(8,128)(2,1)}, bf16[512,256]{1,0:T(8,128)(2,1)}) custom-call(f32[128,2,128]{2,1,0:T(2,128)S(1)} %all-to-all-done.1.sums_ref, f32[1,128]{1,0:T(1,128)S(1)} %bitcast.20, f32[1,128]{1,0:T(1,128)S(1)} %bitcast.21, f32[128,256]{1,0:T(8,128)S(1)} %collective-permute-done.2.before_ref, f32[128,256]{1,0:T(8,128)S(1)} %get-tuple-element.15.head_ref, ...), custom_call_target="tpu_custom_call" | custom-call | tf_op jit(solution)/shard_map/final/pallas_call | solution.py:222
  (12 shorter events, 0.0 us)
Async XLA Ops:
  0.6 1.0 %copy-start = (bf16[1024,128]{1,0:T(8,128)(2,1)S(1)}, bf16[1024,128]{1,0:T(8,128)(2,1)}, u32[]{:S(2)}) copy-start(bf16[1024,128]{1,0:T(8,128)(2,1)} %features_ref.1) | copy-start | bytes 786436
  1.6 0.7 copy-start.2
  2.3 13.8 %copy-start.6 = (bf16[27,128,128]{2,1,0:T(8,128)(2,1)S(1)}, bf16[27,128,128]{2,1,0:T(8,128)(2,1)}, u32[]{:S(2)}) copy-start(bf16[27,128,128]{2,1,0:T(8,128)(2,1)} %param.12) | copy-start | bytes 2654212
  4.5 25.3 %all-to-all-start = ((bf16[128,16,128]{2,1,0:T(8,128)(2,1)}), bf16[128,16,128]{2,1,0:T(8,128)(2,1)S(1)}, u32[]{:S(2)}, u32[]{:S(2)}) async-start(bf16[128,16,128]{2,1,0:T(8,128)(2,1)} %bitcast.3), calls=%async_computation | async-start | bytes 1048576 | tf_op jit(solution)/shard_map/all_to_all | solution.py:247
  17.1 19.5 %copy-start.5 = (s32[1,27,2048]{2,0,1:T(1,128)S(1)}, s32[1,27,2048]{2,0,1:T(1,128)}, u32[]{:S(2)}) copy-start(s32[1,27,2048]{2,0,1:T(1,128)} %param.10) | copy-start | bytes 663556
  29.8 18.9 %collective-permute-start = (bf16[256,128]{1,0:T(8,128)(2,1)S(1)}, bf16[256,128]{1,0:T(8,128)(2,1)S(1)}, u32[]{:S(2)}, u32[]{:S(2)}) collective-permute-start(bf16[256,128]{1,0:T(8,128)(2,1)S(1)} %bitcast.27), channel_id=1, source_target_pairs={{0,1},{1,2},{2,3},{3,4},{4,5},{5,6},{6,7},{7,8},{8,9},{9,10},{10,1... | collective-permute-start | bytes 196616 | tf_op jit(solution)/shard_map/ppermute | solution.py:250
  32.4 16.3 %collective-permute-start.1 = (bf16[256,128]{1,0:T(8,128)(2,1)S(1)}, bf16[256,128]{1,0:T(8,128)(2,1)S(1)}, u32[]{:S(2)}, u32[]{:S(2)}) collective-permute-start(bf16[256,128]{1,0:T(8,128)(2,1)S(1)} %bitcast.26), channel_id=1, source_target_pairs={{1,0},{2,1},{3,2},{4,3},{5,4},{6,5},{7,6},{8,7},{9,8},{10,9},{11,1... | collective-permute-start | bytes 196616 | tf_op jit(solution)/shard_map/ppermute | solution.py:251
  48.7 20.5 %copy-start.7 = (bf16[8,128,256]{2,1,0:T(8,128)(2,1)S(1)}, bf16[8,128,256]{2,1,0:T(8,128)(2,1)}, u32[]{:S(2)}) copy-start(bf16[8,128,256]{2,1,0:T(8,128)(2,1)} %param.15) | copy-start | bytes 1572868
  53.7 25.4 %collective-permute-start.2 = (f32[128,256]{1,0:T(8,128)S(1)}, f32[128,256]{1,0:T(8,128)S(1)}, u32[]{:S(2)}, u32[]{:S(2)}) collective-permute-start(f32[128,256]{1,0:T(8,128)S(1)} %get-tuple-element.14.tail_ref), channel_id=1, source_target_pairs={{0,1},{1,2},{2,3},{3,4},{4,5},{5,6},{6,7},{7,8},{8,9},{9,10},{10,1... | collective-permute-start | bytes 393224 | tf_op jit(solution)/shard_map/ppermute | solution.py:254
  55.6 23.5 %collective-permute-start.3 = (f32[128,256]{1,0:T(8,128)S(1)}, f32[128,256]{1,0:T(8,128)S(1)}, u32[]{:S(2)}, u32[]{:S(2)}) collective-permute-start(f32[128,256]{1,0:T(8,128)S(1)} %get-tuple-element.15.head_ref), channel_id=1, source_target_pairs={{1,0},{2,1},{3,2},{4,3},{5,4},{6,5},{7,6},{8,7},{9,8},{10,9},{11,1... | collective-permute-start | bytes 393224 | tf_op jit(solution)/shard_map/ppermute | solution.py:255
  60.5 18.7 %all-to-all-start.1 = ((f32[128,2,128]{2,1,0:T(2,128)}), f32[128,2,128]{2,1,0:T(2,128)S(1)}, u32[]{:S(2)}, u32[]{:S(2)}) async-start(f32[128,2,128]{2,1,0:T(2,128)} %get-tuple-element.13), calls=%async_computation.1 | async-start | bytes 262144 | tf_op jit(solution)/shard_map/all_to_all | solution.py:256
  69.2 10.0 %copy-start.1 = (s32[1,8,512]{2,1,0:T(8,128)S(1)}, s32[1,8,512]{2,1,0:T(8,128)}, u32[]{:S(2)}) copy-start(s32[1,8,512]{2,1,0:T(8,128)} %param.11) | copy-start | bytes 49156
  79.2 0.7 copy-start.3
  79.2 0.7 copy-start.4

commit v2 on v1

v2 whole, which is shorter than its diff:
```python
import jax
import jax.numpy as jnp
from jax import lax
from jax.experimental import pallas as pl
from jax.experimental.pallas import tpu as pltpu
from jax.sharding import PartitionSpec as P

AXES = ("blocks", "depth")
CH = 128
SEG = 256
VMEM = pl.BlockSpec(memory_space=pltpu.VMEM)
HBM = pl.BlockSpec(memory_space=pltpu.HBM)
BF16 = jnp.bfloat16
F32 = jnp.float32


def params(mib=16):
    return pltpu.CompilerParams(vmem_limit_bytes=mib << 20)


def onehot(where, size, first):
    rows = lax.broadcasted_iota(jnp.int16, (size, where.shape[1]), 0)
    local = jnp.broadcast_to((where - first).astype(jnp.int16), (size, where.shape[1]))
    return jnp.where(rows == local, BF16(1), BF16(0))


def route_body(late_ref, features_hbm, owners_hbm, out_ref, features_ref, owners_ref, sems):
    get_owners = pltpu.make_async_copy(owners_hbm, owners_ref, sems.at[0])
    get_features = pltpu.make_async_copy(features_hbm, features_ref, sems.at[1])
    get_owners.start()
    get_features.start()
    upper = (
        lax.broadcasted_iota(jnp.int32, (SEG, SEG), 0)
        < lax.broadcasted_iota(jnp.int32, (SEG, SEG), 1)
    ).astype(BF16)
    ones = jnp.ones((SEG, SEG), BF16)
    carry = jnp.zeros((128, SEG), F32)
    where = []
    get_owners.wait()
    for c in range(4):
        owners = jnp.concatenate(
            [owners_ref[2 * c : 2 * c + 1, :], owners_ref[2 * c + 1 : 2 * c + 2, :]], axis=1
        )
        hot = onehot(owners, 128, 0)
        before = jnp.dot(hot, upper, preferred_element_type=F32) + carry
        carry = carry + jnp.dot(hot, ones, preferred_element_type=F32)
        rank = jnp.sum(before * hot.astype(F32), axis=0, keepdims=True)
        where.append(owners * 16 + rank.astype(jnp.int32))
    get_features.wait()
    table = jnp.concatenate([features_ref[...], jnp.ones((1024, CH), BF16)], axis=1)
    for s in range(8):
        placed = jnp.concatenate([onehot(w, SEG, SEG * s) for w in where], axis=1)
        found = jnp.dot(placed, table, preferred_element_type=F32)
        rows = jnp.where(found[:, CH:] > 0.5, found[:, :CH], jnp.inf).astype(BF16)
        out_ref[16 * s : 16 * (s + 1), :16, :] = rows.reshape(16, 16, CH)
    late = late_ref[0] > 0

    @pl.when(late)
    def _():
        out_ref[1:, 16:, :] = out_ref[:127, :16, :]
        out_ref[:1, 16:, :] = jnp.full((1, 16, CH), jnp.inf, BF16)

    @pl.when(jnp.logical_not(late))
    def _():
        out_ref[:127, 16:, :] = out_ref[1:, :16, :]
        out_ref[127:, 16:, :] = jnp.full((1, 16, CH), jnp.inf, BF16)


def route(late, features, owners):
    return pl.pallas_call(
        route_body,
        name="route",
        out_shape=jax.ShapeDtypeStruct((128, 32, CH), BF16),
        in_specs=[pl.BlockSpec(memory_space=pltpu.SMEM)] + [HBM] * 2,
        out_specs=VMEM,
        scratch_shapes=[
            pltpu.VMEM((1024, CH), BF16),
            pltpu.VMEM((8, 128), jnp.int32),
            pltpu.SemaphoreType.DMA((2,)),
        ],
        compiler_params=params(60),
    )(late, features, owners)


def prepare_body(index_ref, weights_ref, down_ref, local_ref, head_ref, tail_ref, turned_ref, down_turned_ref):
    for k in range(27):
        local = index_ref[16 * k : 16 * (k + 1), :] - SEG * (
            lax.broadcasted_iota(jnp.int32, (16, 128), 0) >> 1
        )
        local_ref[16 * k : 16 * (k + 1), :] = local
        head_ref[k : k + 1, :] = jnp.concatenate([local[:1], local[1:2]], axis=1)
        tail_ref[k : k + 1, :] = jnp.concatenate([local[14:15], local[15:]], axis=1)
        turned_ref[:, CH * k : CH * (k + 1)] = weights_ref[k].astype(F32).T.astype(BF16)
    for k in range(8):
        down_turned_ref[:, CH * k : CH * (k + 1)] = down_ref[k].astype(F32).T.astype(BF16)


def prepare(index, weights, down):
    return pl.pallas_call(
        prepare_body,
        name="prepare",
        out_shape=(
            jax.ShapeDtypeStruct((432, 128), jnp.int32),
            jax.ShapeDtypeStruct((27, SEG), jnp.int32),
            jax.ShapeDtypeStruct((27, SEG), jnp.int32),
            jax.ShapeDtypeStruct((CH, 27 * CH), BF16),
            jax.ShapeDtypeStruct((2 * CH, 8 * CH), BF16),
        ),
        in_specs=[VMEM] * 3,
        out_specs=(VMEM,) * 5,
        compiler_params=params(),
        cost_estimate=pl.CostEstimate(flops=0, bytes_accessed=8 << 20, transcendentals=0),
    )(index, weights, down)


def pick(window, local):
    segments = window.shape[0] // CH
    low = jnp.dot(window, onehot(local & (SEG - 1), SEG, 0), preferred_element_type=F32)
    high = jnp.broadcast_to(local >> 8, (CH, SEG))
    out = jnp.zeros((CH, SEG), F32)
    for s in range(segments):
        out = jnp.where(high == s, low[CH * s : CH * (s + 1)], out)
    return out.astype(BF16)


def conv_block(window, index_of, weights_ref, gathered_ref):
    for k in range(27):
        gathered_ref[CH * k : CH * (k + 1), :] = pick(window, index_of(k))
    return jnp.dot(weights_ref[...], gathered_ref[...], preferred_element_type=F32)


def turned(raw):
    flat = raw.astype(F32).T
    filled = flat < jnp.inf
    return jnp.where(filled, flat, 0.0).astype(BF16), filled[:1].astype(F32)


def chunk(rows_ref, c):
    part, first = (1, c + 6) if c < 2 else (0, c - 2) if c < 10 else (1, c - 10)
    raw = rows_ref[16 * first : 16 * (first + 1), 16 * part : 16 * (part + 1), :]
    return turned(raw.reshape(SEG, CH))


def conv_body(
    rows_ref, index_hbm, weights_hbm, filled_ref, conv_ref, send_ref,
    table_ref, sums_ref, gathered_ref, index_ref, weights_ref, sems,
):
    get_index = pltpu.make_async_copy(index_hbm, index_ref, sems.at[0])
    get_weights = pltpu.make_async_copy(weights_hbm, weights_ref, sems.at[1])
    get_index.start()
    get_weights.start()
    for c in range(1, 11):
        table, filled = chunk(rows_ref, c)
        table_ref[CH * (c - 1) : CH * c, :] = table
        if 1 < c < 10:
            filled_ref[:, SEG * (c - 2) : SEG * (c - 1)] = filled
    sums_ref[...] = jnp.zeros_like(sums_ref)
    get_index.wait()
    get_weights.wait()

    def block(b, _):
        window = table_ref[pl.ds(pl.multiple_of(CH * b, CH), 3 * CH), :]

        def index_of(k):
            row = k * 16 + 2 * b
            pair = [index_ref[pl.ds(row, 1), :], index_ref[pl.ds(row + 1, 1), :]]
            return jnp.concatenate(pair, axis=1)

        conv = conv_block(window, index_of, weights_ref, gathered_ref)
        lanes = pl.ds(pl.multiple_of(SEG * b, SEG), SEG)
        conv_ref[:, lanes] = conv
        weighted = conv * filled_ref[:, lanes]
        sums_ref[:CH] += weighted
        sums_ref[CH:] += weighted * conv
        return 0

    lax.fori_loop(0, 8, block, 0)
    for n in range(2):
        total = sums_ref[CH * n : CH * (n + 1)]
        row = jnp.sum((total[:, :CH] + total[:, CH:]).T, axis=0, keepdims=True)
        send_ref[:, n : n + 1, :] = jnp.broadcast_to(row[None], (128, 1, CH))


def convolve(rows, index, weights):
    return pl.pallas_call(
        conv_body,
        name="convolve",
        out_shape=(
            jax.ShapeDtypeStruct((1, 2048), F32),
            jax.ShapeDtypeStruct((CH, 2048), F32),
            jax.ShapeDtypeStruct((128, 2, CH), F32),
        ),
        in_specs=[VMEM, HBM, HBM],
        out_specs=(VMEM,) * 3,
        scratch_shapes=[
            pltpu.VMEM((10 * CH, SEG), BF16),
            pltpu.VMEM((2 * CH, SEG), F32),
            pltpu.VMEM((27 * CH, SEG), BF16),
            pltpu.VMEM((432, 128), jnp.int32),
            pltpu.VMEM((CH, 27 * CH), BF16),
            pltpu.SemaphoreType.DMA((2,)),
        ],
        compiler_params=params(52),
        cost_estimate=pl.CostEstimate(
            flops=8 * 27 * 2 * 384 * 256 * 256, bytes_accessed=4 << 20, transcendentals=0
        ),
    )(rows, index, weights)


def column(row):
    flat = jnp.broadcast_to(row, (CH, CH)).T
    return jnp.concatenate([flat, flat], axis=1)


def rims_body(
    rows_ref, before_ref, after_ref, weights_hbm, gain_ref, shift_ref,
    conv_ref, filled_ref, columns_ref, table_ref, gathered_ref, weights_ref, sem,
):
    get_weights = pltpu.make_async_copy(weights_hbm, weights_ref, sem)
    get_weights.start()
    columns_ref[:CH] = column(gain_ref[...])
    columns_ref[CH:] = column(shift_ref[...])
    for side, index_ref in ((0, before_ref), (1, after_ref)):
        for n in range(3):
            table, filled = chunk(rows_ref, 9 * side + n)
            table_ref[CH * n : CH * (n + 1), :] = table
            if n == 1:
                filled_ref[:, SEG * side : SEG * (side + 1)] = filled
        if side == 0:
            get_weights.wait()
        conv_ref[:, SEG * side : SEG * (side + 1)] = conv_block(
            table_ref[...], lambda k: index_ref[k : k + 1, :], weights_ref, gathered_ref
        )


def rims(rows, before, after, weights, gain, shift):
    return pl.pallas_call(
        rims_body,
        name="rims",
        out_shape=(
            jax.ShapeDtypeStruct((CH, 2 * SEG), F32),
            jax.ShapeDtypeStruct((1, 2 * SEG), F32),
            jax.ShapeDtypeStruct((2 * CH, SEG), F32),
        ),
        in_specs=[VMEM, VMEM, VMEM, HBM, VMEM, VMEM],
        out_specs=(VMEM,) * 3,
        scratch_shapes=[
            pltpu.VMEM((3 * CH, SEG), BF16),
            pltpu.VMEM((27 * CH, SEG), BF16),
            pltpu.VMEM((CH, 27 * CH), BF16),
            pltpu.SemaphoreType.DMA,
        ],
        compiler_params=params(52),
        cost_estimate=pl.CostEstimate(
            flops=2 * 27 * 2 * 384 * 256 * 256, bytes_accessed=4 << 20, transcendentals=0
        ),
    )(rows, before, after, weights, gain, shift)


def final_body(
    sums_ref, columns_ref, rims_ref, rims_filled_ref, conv_ref, filled_ref, index_ref, weights_hbm,
    hidden_ref, coarse_ref, table_ref, gathered_ref, weights_ref, sem,
):
    get_weights = pltpu.make_async_copy(weights_hbm, weights_ref, sem)
    get_weights.start()
    totals = jnp.sum(sums_ref[...], axis=0) / 131072.0
    mean = column(totals[:1])
    scale = columns_ref[:CH] / jnp.sqrt(column(totals[1:]) - mean * mean + 1e-05)
    shift = columns_ref[CH:]
    for c in range(10):
        if c in (0, 9):
            side = slice(SEG * (c // 9), SEG * (c // 9 + 1))
            conv, filled = rims_ref[:, side], rims_filled_ref[:, side]
        else:
            own = slice(SEG * (c - 1), SEG * c)
            conv, filled = conv_ref[:, own], filled_ref[:, own]
        hidden = filled * jnp.maximum((conv - mean) * scale + shift, 0.0)
        table_ref[CH * c : CH * (c + 1)] = hidden.astype(BF16)
        if 0 < c < 9:
            hidden_ref[own, :] = hidden.T.astype(BF16)
    for b in range(4):
        window = table_ref[2 * CH * b : 2 * CH * b + 4 * CH, :]
        for k in range(0, 8, 2):
            index = jnp.concatenate(
                [index_ref[k : k + 1, CH * b : CH * (b + 1)], index_ref[k + 1 : k + 2, CH * b : CH * (b + 1)]],
                axis=1,
            )
            chosen = pick(window, index - 2 * SEG * b)
            gathered_ref[CH * k : CH * (k + 1), CH * b : CH * (b + 1)] = chosen[:, :CH]
            gathered_ref[CH * (k + 1) : CH * (k + 2), CH * b : CH * (b + 1)] = chosen[:, CH:]
    get_weights.wait()
    for b in range(2):
        out = jnp.dot(
            weights_ref[...], gathered_ref[:, SEG * b : SEG * (b + 1)], preferred_element_type=F32
        )
        coarse_ref[SEG * b : SEG * (b + 1), :] = out.T.astype(BF16)


def final(sums, columns, rims_conv, rims_filled, conv, filled, index, weights):
    return pl.pallas_call(
        final_body,
        name="final",
        out_shape=(
            jax.ShapeDtypeStruct((2048, CH), BF16),
            jax.ShapeDtypeStruct((512, 2 * CH), BF16),
        ),
        in_specs=[VMEM] * 7 + [HBM],
        out_specs=(VMEM,) * 2,
        scratch_shapes=[
            pltpu.VMEM((10 * CH, SEG), BF16),
            pltpu.VMEM((8 * CH, 512), BF16),
            pltpu.VMEM((2 * CH, 8 * CH), BF16),
            pltpu.SemaphoreType.DMA,
        ],
        compiler_params=params(52),
    )(sums, columns, rims_conv, rims_filled, conv, filled, index, weights)


def shards(features, owners, kernel_map, fine_slots, conv_weight, gain, shift, down_weight):
    ndev = lax.axis_size("blocks") * lax.axis_size("depth")
    late = (lax.axis_index("blocks") >= lax.axis_size("blocks") // 2).astype(jnp.int32)
    up = [(i, i + 1) for i in range(ndev - 1)]
    down = [(i + 1, i) for i in range(ndev - 1)]

    sent = route(late[None], features, owners.reshape(8, 128))
    rows = lax.all_to_all(sent, AXES, split_axis=0, concat_axis=0, tiled=True)
    index, head, tail, weights, down_weights = prepare(
        kernel_map.reshape(27 * 16, 128), conv_weight, down_weight
    )
    before = lax.ppermute(tail, AXES, up)
    after = lax.ppermute(head, AXES, down)
    filled, conv, send = convolve(rows, index, weights)
    totals = lax.all_to_all(send, AXES, split_axis=0, concat_axis=0, tiled=True)
    rims_conv, rims_filled, columns = rims(
        rows, before, after, weights, gain.reshape(1, CH), shift.reshape(1, CH)
    )
    return final(
        totals, columns, rims_conv, rims_filled, conv, filled, fine_slots.reshape(8, 512), down_weights
    )


def solution(mesh):
    split = P(AXES, None)
    placed = (split, split, P(AXES, None, None), P(AXES, None, None), P(), P(), P(), P())
    return jax.shard_map(
        shards, mesh=mesh, in_specs=placed, out_specs=(split, split), check_vma=False
    )
```

time: 83 us -> 72.3 us (0.87)
  starting transfers between devices: 33.8 us -> 23.3 us
  Pallas kernels: 22.1 us -> 31.9 us
  waiting for transfers between devices: 22.3 us -> 15.2 us
  local copies, waits for them, and re-layouts: 3.52 us -> 0.68 us
    pallas_call x2 -> x3, Pallas kernels: 17.1 us -> 24.4 us  [the longest x1 18.7 us: convolve(): pl.pallas_call(conv_body, name='convolve', out_shape=(jax.ShapeDtypeStruc...]
    ppermute x2 -> x0, starting transfers between devices: 6.77 us -> none  [the longest x1 4.18 us: shards(): raw_after = lax.ppermute(raw[:SEG], AXES, down)]
    all_to_all x1, waiting for transfers between devices: 9.7 us -> 4.01 us  [shards(): totals = lax.all_to_all(send, AXES, split_axis=0, concat_axis=0, tiled=True)]
    all_to_all x1, starting transfers between devices: 8.72 us -> 4.05 us  [shards(): totals = lax.all_to_all(send, AXES, split_axis=0, concat_axis=0, tiled=True)]
    unnamed x16 -> x12, local copies, waits for them, and re-layouts: 2.3 us -> 0.68 us
    ppermute x1, starting transfers between devices: 1.91 us -> 3.42 us  [shards(): before = lax.ppermute(tail, AXES, up)]
    all_to_all x1, waiting for transfers between devices: 12.6 us -> 11.2 us  [shards(): rows = lax.all_to_all(sent, AXES, split_axis=0, concat_axis=0, tiled=True)]
    pallas_call x1, Pallas kernels: 2.81 us -> 4.17 us  [final(): pl.pallas_call(final_body, name='final', out_shape=(jax.ShapeDtypeStruct(...]
  transfers between devices with their start and end apart: 6 -> 4, of which waited for: 2 -> 2; matrix products, arithmetic and copies ran while one was open for 2% -> 0% of each run, Pallas kernels for 15% -> 34%
where the time goes in v2:
time: 72.3 us; the launch traced here: 71.9 us
  Pallas kernels  31.9 us (44%)
  starting transfers between devices  23.3 us (32%)
  waiting for transfers between devices  15.2 us (21%)
  between operations  0.78 us (1%)
    pallas_call x1, Pallas kernels, convolve(): pl.pallas_call(conv_body, name='convolve', out_shape=(jax.ShapeDtypeStruc...  18.7 us
    all_to_all x1, starting transfers between devices, shards(): rows = lax.all_to_all(sent, AXES, split_axis=0, concat_axis=0, tiled=True)  11.9 us
    all_to_all x1, waiting for transfers between devices, shards(): rows = lax.all_to_all(sent, AXES, split_axis=0, concat_axis=0, tiled=True)  11.2 us
    pallas_call x1, Pallas kernels, rims(): pl.pallas_call(rims_body, name='rims', out_shape=(jax.ShapeDtypeStruct((C...  5.22 us
    pallas_call x1, Pallas kernels, final(): pl.pallas_call(final_body, name='final', out_shape=(jax.ShapeDtypeStruct(...  4.17 us
    all_to_all x1, starting transfers between devices, shards(): totals = lax.all_to_all(send, AXES, split_axis=0, concat_axis=0, tiled=True)  4.05 us
    all_to_all x1, waiting for transfers between devices, shards(): totals = lax.all_to_all(send, AXES, split_axis=0, concat_axis=0, tiled=True)  4.01 us
    ppermute x1, starting transfers between devices, shards(): after = lax.ppermute(head, AXES, down)  3.92 us
  transfers between devices with their start and end apart: 4, of which 2 were waited for; matrix products, arithmetic and copies ran while one was open for 0% of the time, Pallas kernels for 34%

profile of v2, /device:TPU:1, one launch (start us, length us, event | category | flops | bytes accessed | tf_op | source)
XLA Modules:
  0.0 71.9 jit_solution(8685445976997424448)
XLA Ops:
  0.6 3.3 %route.1 = bf16[128,32,128]{2,1,0:T(8,128)(2,1)} custom-call(s32[1]{0:T(128)} %bitcast.late_ref, bf16[1024,128]{1,0:T(8,128)(2,1)} %features_hbm.1, s32[8,128]{1,0:T(8,128)} %bitcast.10), custom_call_target="tpu_custom_call" | custom-call | tf_op jit(solution)/shard_map/route/pallas_call | solution.py:70
  4.0 0.0 copy-start
  4.0 0.0 copy-start.1
  4.0 0.0 copy-start.2
  4.0 11.9 %all-to-all-start = ((bf16[128,32,128]{2,1,0:T(8,128)(2,1)}), bf16[128,32,128]{2,1,0:T(8,128)(2,1)}, u32[]{:S(2)}, u32[]{:S(2)}) async-start(bf16[128,32,128]{2,1,0:T(8,128)(2,1)} %route.1), calls=%async_computation | async-start | bytes 2097152 | tf_op jit(solution)/shard_map/all_to_all | solution.py:326
  16.0 0.0 copy-done
  16.0 0.0 copy-done.1
  16.0 0.0 copy-done.2
  16.0 0.5 prepare.1
  16.5 3.4 %collective-permute-start = (s32[27,256]{1,0:T(8,128)S(1)}, s32[27,256]{1,0:T(8,128)S(1)}, u32[]{:S(2)}, u32[]{:S(2)}) collective-permute-start(s32[27,256]{1,0:T(8,128)S(1)} %get-tuple-element.16), channel_id=1, source_target_pairs={{0,1},{1,2},{2,3},{3,4},{4,5},{5,6},{6,7},{7,8},{8,9},{9,10},{10,1... | collective-permute-start | bytes 82952 | tf_op jit(solution)/shard_map/ppermute | solution.py:330
  19.9 3.9 %collective-permute-start.1 = (s32[27,256]{1,0:T(8,128)S(1)}, s32[27,256]{1,0:T(8,128)S(1)}, u32[]{:S(2)}, u32[]{:S(2)}) collective-permute-start(s32[27,256]{1,0:T(8,128)S(1)} %get-tuple-element.17), channel_id=1, source_target_pairs={{1,0},{2,1},{3,2},{4,3},{5,4},{6,5},{7,6},{8,7},{9,8},{10,9},{11,1... | collective-permute-start | bytes 82952 | tf_op jit(solution)/shard_map/ppermute | solution.py:331
  23.8 11.2 %all-to-all-done.rows_ref = bf16[128,32,128]{2,1,0:T(8,128)(2,1)} async-done(((bf16[128,32,128]{2,1,0:T(8,128)(2,1)}), bf16[128,32,128]{2,1,0:T(8,128)(2,1)}, u32[]{:S(2)}, u32[]{:S(2)}) %all-to-all-start) | async-done | bytes 1048608 | tf_op jit(solution)/shard_map/all_to_all | solution.py:326
  35.0 18.7 %convolve.1 = (f32[1,2048]{1,0:T(1,128)S(1)}, f32[128,2048]{1,0:T(8,128)}, f32[128,2,128]{2,1,0:T(2,128)}) custom-call(bf16[128,32,128]{2,1,0:T(8,128)(2,1)} %all-to-all-done.rows_ref, s32[432,128]{1,0:T(8,128)S(1)} %get-tuple-element.13.index_hbm, bf16[128,3456]{1,0:T(8,128)(2,1)S(1)} %get-tuple-element.14.weights_hbm), custom_call_target="tpu_custom_call" | custom-call | flops 10871635968 | bytes 4194304 | tf_op jit(solution)/shard_map/convolve/pallas_call | solution.py:185
  53.7 4.0 %all-to-all-start.1 = ((f32[128,2,128]{2,1,0:T(2,128)}), f32[128,2,128]{2,1,0:T(2,128)S(1)}, u32[]{:S(2)}, u32[]{:S(2)}) async-start(f32[128,2,128]{2,1,0:T(2,128)} %get-tuple-element.15), calls=%async_computation.1 | async-start | bytes 262144 | tf_op jit(solution)/shard_map/all_to_all | solution.py:333
  57.8 0.0 collective-permute-done.before_ref
  57.8 0.0 collective-permute-done.1.after_ref
  57.8 0.0 copy-start.4
  57.8 0.0 copy-start.5
  57.8 0.6 copy-done.4
  58.5 0.0 copy-done.5
  58.5 5.2 %rims.1 = (f32[128,512]{1,0:T(8,128)S(1)}, f32[1,512]{1,0:T(1,128)S(1)}, f32[256,256]{1,0:T(8,128)S(1)}) custom-call(bf16[128,32,128]{2,1,0:T(8,128)(2,1)} %all-to-all-done.rows_ref, s32[27,256]{1,0:T(8,128)S(1)} %collective-permute-done.before_ref, s32[27,256]{1,0:T(8,128)S(1)} %collective-permute-done.1.after_ref, ...), custom_call_target="tpu_custom_call" | custom-call | flops 2717908992 | bytes 4194304 | tf_op jit(solution)/shard_map/rims/pallas_call | solution.py:237
  63.7 4.0 %all-to-all-done.1.sums_ref = f32[128,2,128]{2,1,0:T(2,128)S(1)} async-done(((f32[128,2,128]{2,1,0:T(2,128)}), f32[128,2,128]{2,1,0:T(2,128)S(1)}, u32[]{:S(2)}, u32[]{:S(2)}) %all-to-all-start.1) | async-done | bytes 131104 | tf_op jit(solution)/shard_map/all_to_all | solution.py:333
  67.7 0.0 copy-done.3
  67.7 4.2 %final.1 = (bf16[2048,128]{1,0:T(8,128)(2,1)}, bf16[512,256]{1,0:T(8,128)(2,1)}) custom-call(f32[128,2,128]{2,1,0:T(2,128)S(1)} %all-to-all-done.1.sums_ref, f32[256,256]{1,0:T(8,128)S(1)} %get-tuple-element.18.columns_ref, f32[128,512]{1,0:T(8,128)S(1)} %get-tuple-element.19.rims_ref, f32[1,512]{1,0:T(1,128)S(1)} %get-tuple-element.20.rims_filled_ref, ...), custom_call_target="tpu_custom_call" | custom-call | tf_op jit(solution)/shard_map/final/pallas_call | solution.py:300
  (1 shorter events, 0.0 us)
Async XLA Ops:
  4.0 12.0 %copy-start = (bf16[27,128,128]{2,1,0:T(8,128)(2,1)S(1)}, bf16[27,128,128]{2,1,0:T(8,128)(2,1)}, u32[]{:S(2)}) copy-start(bf16[27,128,128]{2,1,0:T(8,128)(2,1)} %weights_ref.1) | copy-start | bytes 2654212
  4.0 12.0 %copy-start.1 = (bf16[8,128,256]{2,1,0:T(8,128)(2,1)S(1)}, bf16[8,128,256]{2,1,0:T(8,128)(2,1)}, u32[]{:S(2)}) copy-start(bf16[8,128,256]{2,1,0:T(8,128)(2,1)} %down_ref.1) | copy-start | bytes 1572868
  4.0 12.0 %copy-start.2 = (s32[1,27,2048]{2,0,1:T(1,128)S(1)}, s32[1,27,2048]{2,0,1:T(1,128)}, u32[]{:S(2)}) copy-start(s32[1,27,2048]{2,0,1:T(1,128)} %param.10) | copy-start | bytes 663556
  4.0 31.0 %all-to-all-start = ((bf16[128,32,128]{2,1,0:T(8,128)(2,1)}), bf16[128,32,128]{2,1,0:T(8,128)(2,1)}, u32[]{:S(2)}, u32[]{:S(2)}) async-start(bf16[128,32,128]{2,1,0:T(8,128)(2,1)} %route.1), calls=%async_computation | async-start | bytes 2097152 | tf_op jit(solution)/shard_map/all_to_all | solution.py:326
  16.5 41.3 %collective-permute-start = (s32[27,256]{1,0:T(8,128)S(1)}, s32[27,256]{1,0:T(8,128)S(1)}, u32[]{:S(2)}, u32[]{:S(2)}) collective-permute-start(s32[27,256]{1,0:T(8,128)S(1)} %get-tuple-element.16), channel_id=1, source_target_pairs={{0,1},{1,2},{2,3},{3,4},{4,5},{5,6},{6,7},{7,8},{8,9},{9,10},{10,1... | collective-permute-start | bytes 82952 | tf_op jit(solution)/shard_map/ppermute | solution.py:330
  19.9 37.9 %collective-permute-start.1 = (s32[27,256]{1,0:T(8,128)S(1)}, s32[27,256]{1,0:T(8,128)S(1)}, u32[]{:S(2)}, u32[]{:S(2)}) collective-permute-start(s32[27,256]{1,0:T(8,128)S(1)} %get-tuple-element.17), channel_id=1, source_target_pairs={{1,0},{2,1},{3,2},{4,3},{5,4},{6,5},{7,6},{8,7},{9,8},{10,9},{11,1... | collective-permute-start | bytes 82952 | tf_op jit(solution)/shard_map/ppermute | solution.py:331
  53.7 14.0 %all-to-all-start.1 = ((f32[128,2,128]{2,1,0:T(2,128)}), f32[128,2,128]{2,1,0:T(2,128)S(1)}, u32[]{:S(2)}, u32[]{:S(2)}) async-start(f32[128,2,128]{2,1,0:T(2,128)} %get-tuple-element.15), calls=%async_computation.1 | async-start | bytes 262144 | tf_op jit(solution)/shard_map/all_to_all | solution.py:333
  57.8 0.7 copy-start.4
  57.8 0.7 copy-start.5
  58.5 9.2 %copy-start.3 = (s32[1,8,512]{2,1,0:T(8,128)S(1)}, s32[1,8,512]{2,1,0:T(8,128)}, u32[]{:S(2)}) copy-start(s32[1,8,512]{2,1,0:T(8,128)} %param.11) | copy-start | bytes 49156

commit v3 on v2

v3 whole, which is shorter than its diff:
```python
import jax
import jax.numpy as jnp
from jax import lax
from jax.experimental import pallas as pl
from jax.experimental.pallas import tpu as pltpu
from jax.sharding import PartitionSpec as P

AXES = ("blocks", "depth")
CH = 128
SEG = 256
SMEM = pl.BlockSpec(memory_space=pltpu.SMEM)
VMEM = pl.BlockSpec(memory_space=pltpu.VMEM)
HBM = pl.BlockSpec(memory_space=pltpu.HBM)
BF16 = jnp.bfloat16
F32 = jnp.float32


def params(mib):
    return pltpu.CompilerParams(vmem_limit_bytes=mib << 20)


def shape(dims, dtype):
    return jax.ShapeDtypeStruct(dims, dtype)


def onehot(where, size, first):
    rows = lax.broadcasted_iota(jnp.int16, (size, where.shape[1]), 0)
    local = jnp.broadcast_to((where - first).astype(jnp.int16), (size, where.shape[1]))
    return jnp.where(rows == local, BF16(1), BF16(0))


def route_body(late_ref, features_hbm, owners_hbm, out_ref, features_ref, owners_ref, sems):
    get_owners = pltpu.make_async_copy(owners_hbm, owners_ref, sems.at[0])
    get_features = pltpu.make_async_copy(features_hbm, features_ref, sems.at[1])
    get_owners.start()
    get_features.start()
    upper = (
        lax.broadcasted_iota(jnp.int32, (SEG, SEG), 0)
        < lax.broadcasted_iota(jnp.int32, (SEG, SEG), 1)
    ).astype(BF16)
    ones = jnp.ones((SEG, SEG), BF16)
    carry = jnp.zeros((128, SEG), F32)
    where = []
    get_owners.wait()
    for c in range(4):
        owners = jnp.concatenate(
            [owners_ref[2 * c : 2 * c + 1, :], owners_ref[2 * c + 1 : 2 * c + 2, :]], axis=1
        )
        hot = onehot(owners, 128, 0)
        before = jnp.dot(hot, upper, preferred_element_type=F32) + carry
        carry = carry + jnp.dot(hot, ones, preferred_element_type=F32)
        rank = jnp.sum(before * hot.astype(F32), axis=0, keepdims=True)
        where.append(owners * 16 + rank.astype(jnp.int32))
    get_features.wait()
    table = jnp.concatenate([features_ref[...], jnp.ones((1024, CH), BF16)], axis=1)
    for s in range(8):
        placed = jnp.concatenate([onehot(w, SEG, SEG * s) for w in where], axis=1)
        found = jnp.dot(placed, table, preferred_element_type=F32)
        rows = jnp.where(found[:, CH:] > 0.5, found[:, :CH], jnp.inf).astype(BF16)
        out_ref[16 * s : 16 * (s + 1), :16, :] = rows.reshape(16, 16, CH)
    late = late_ref[0] > 0

    @pl.when(late)
    def _():
        out_ref[1:, 16:, :] = out_ref[:127, :16, :]
        out_ref[:1, 16:, :] = jnp.full((1, 16, CH), jnp.inf, BF16)

    @pl.when(jnp.logical_not(late))
    def _():
        out_ref[:127, 16:, :] = out_ref[1:, :16, :]
        out_ref[127:, 16:, :] = jnp.full((1, 16, CH), jnp.inf, BF16)


def route(late, features, owners):
    return pl.pallas_call(
        route_body,
        name="route",
        out_shape=shape((128, 32, CH), BF16),
        in_specs=[SMEM] + [HBM] * 2,
        out_specs=VMEM,
        scratch_shapes=[
            pltpu.VMEM((1024, CH), BF16),
            pltpu.VMEM((8, 128), jnp.int32),
            pltpu.SemaphoreType.DMA((2,)),
        ],
        compiler_params=params(60),
    )(late, features, owners)


def prepare_body(index_ref, weights_ref, down_ref, head_ref, tail_ref, turned_ref, down_turned_ref):
    for k in range(27):
        for ref, first in ((head_ref, 0), (tail_ref, 14)):
            ref[k : k + 1, :] = jnp.concatenate(
                [index_ref[16 * k + t : 16 * k + t + 1, :] - CH * t for t in (first, first + 1)], axis=1
            )
        turned_ref[:, CH * k : CH * (k + 1)] = weights_ref[k].astype(F32).T.astype(BF16)
    for k in range(8):
        down_turned_ref[:, CH * k : CH * (k + 1)] = down_ref[k].astype(F32).T.astype(BF16)


def prepare(index, weights, down):
    return pl.pallas_call(
        prepare_body,
        name="prepare",
        out_shape=(
            shape((27, SEG), jnp.int32),
            shape((27, SEG), jnp.int32),
            shape((CH, 27 * CH), BF16),
            shape((2 * CH, 8 * CH), BF16),
        ),
        in_specs=[VMEM] * 3,
        out_specs=(VMEM,) * 4,
        compiler_params=params(16),
        cost_estimate=pl.CostEstimate(flops=0, bytes_accessed=8 << 20, transcendentals=0),
    )(index, weights, down)


LANE_OFFSETS = 5


def turn(raw):
    flat = raw.astype(F32).T
    filled = flat < jnp.inf
    return jnp.where(filled, flat, 0.0).astype(BF16), filled[:1].astype(F32)


def lanes_of(table, index):
    numbers = lax.GatherDimensionNumbers(
        offset_dims=(), collapsed_slice_dims=(1,), start_index_map=(1,),
        operand_batching_dims=(0,), start_indices_batching_dims=(0,),
    )
    return lax.gather(
        table, index[..., None], numbers, slice_sizes=(1, 1),
        mode=lax.GatherScatterMode.PROMISE_IN_BOUNDS,
    )


def put_tile(even_ref, odd_ref, tile, table):
    for ref, at in ((even_ref, tile), (odd_ref, tile - 1)):
        if 0 <= at < 2 * (ref.shape[0] // CH):
            part, half = divmod(at, 2)
            ref[CH * part : CH * (part + 1), CH * half : CH * (half + 1)] = table


def gather_block(even_ref, odd_ref, part, slots_of, gathered_ref):
    for half, ref in ((0, even_ref), (1, odd_ref)):
        rows = [pl.ds(pl.multiple_of(CH * (part + n), CH), CH) for n in range(3)]
        window = ref[pl.ds(pl.multiple_of(CH * part, CH), 2 * CH), :]
        tiles = [ref[rows[t // 2], CH * (t % 2) : CH * (t % 2 + 1)] for t in range(5)]

        def from_tiles(slots, out, kept):
            lane = jnp.broadcast_to((slots & 127).astype(jnp.int16), (CH, CH))
            where = jnp.broadcast_to((slots >> 7).astype(jnp.int16), (CH, CH))
            for t in kept:
                out = jnp.where(where == t, lanes_of(tiles[t], lane), out)
            return out

        def keep(k, value):
            gathered_ref[CH * k : CH * (k + 1), CH * half : CH * (half + 1)] = value

        def by_matmul(k):
            slots = [slots_of(k, half), slots_of(k + 1, half)]
            both = jnp.concatenate(slots, axis=1)
            low = jnp.where(both < 512, both & (SEG - 1), -1)
            found = jnp.dot(window, onehot(low, SEG, 0), preferred_element_type=F32)
            first = jnp.broadcast_to(both, (CH, SEG)) < SEG
            chosen = jnp.where(first, found[:CH], found[CH:]).astype(BF16)
            for n in range(2):
                keep(k + n, from_tiles(slots[n], chosen[:, CH * n : CH * (n + 1)], [4]))

        def by_lanes(k):
            keep(k, from_tiles(slots_of(k, half), jnp.zeros((CH, CH), BF16), range(5)))

        pairs = (27 - LANE_OFFSETS) // 2
        done = 2 * pairs
        for n in range(pairs):
            by_matmul(2 * n)
            while done < 27 and (done - 2 * pairs + 1) * pairs <= (n + 1) * (LANE_OFFSETS + 0.5):
                by_lanes(done)
                done += 1


def product(weights_ref, gathered_ref):
    return jnp.dot(weights_ref[...], gathered_ref[...], preferred_element_type=F32)


def conv_body(
    rows_hbm, index_hbm, weights_hbm, filled_ref, conv_hbm, send_ref,
    rows_ref, rims_ref, even_ref, odd_ref, conv_ref, sums_ref, first_ref, second_ref,
    index_ref, weights_ref, in_sems, out_sems,
):
    gets = [
        pltpu.make_async_copy(rows_hbm.at[112:, 16:], rims_ref.at[:16], in_sems.at[0]),
        pltpu.make_async_copy(rows_hbm.at[:16, 16:], rims_ref.at[16:], in_sems.at[1]),
    ] + [
        pltpu.make_async_copy(
            rows_hbm.at[32 * n : 32 * (n + 1), :16], rows_ref.at[32 * n : 32 * (n + 1)], in_sems.at[2 + n]
        )
        for n in range(4)
    ]
    get_index = pltpu.make_async_copy(index_hbm, index_ref, in_sems.at[6])
    get_weights = pltpu.make_async_copy(weights_hbm, weights_ref, in_sems.at[7])
    for get in gets + [get_index, get_weights]:
        get.start()
    sums_ref[...] = jnp.zeros_like(sums_ref)
    second_ref[...] = jnp.zeros_like(second_ref)
    gets[0].wait()
    gets[1].wait()
    for t in (0, 1, 18, 19):
        n = t if t < 2 else t - 16
        table, _ = turn(rims_ref[8 * n : 8 * (n + 1)].reshape(CH, CH))
        put_tile(even_ref, odd_ref, t, table)
    for t in range(2, 18):
        if t % 4 == 2:
            gets[2 + t // 4].wait()
        table, filled = turn(rows_ref[8 * (t - 2) : 8 * (t - 1)].reshape(CH, CH))
        put_tile(even_ref, odd_ref, t, table)
        filled_ref[:, CH * (t - 2) : CH * (t - 1)] = filled
    get_index.wait()
    get_weights.wait()

    def finish(conv, at, block):
        conv_ref[at] = conv
        weighted = conv * filled_ref[:, pl.ds(pl.multiple_of(SEG * block, SEG), SEG)]
        sums_ref[:CH] += weighted
        sums_ref[CH:] += weighted * conv
        pltpu.make_async_copy(conv_ref.at[at], conv_hbm.at[at], out_sems.at[at]).start()

    def step(block, own_ref, last_ref):
        conv = product(weights_ref, last_ref)

        def slots_of(k, half):
            tile = 2 * block + half
            return index_ref[pl.ds(16 * k + tile, 1), :] - CH * tile

        gather_block(even_ref, odd_ref, block, slots_of, own_ref)
        finish(conv, lax.rem(block + 8, 9), jnp.maximum(block - 1, 0))

    def two(j, _):
        step(2 * j, first_ref, second_ref)
        step(2 * j + 1, second_ref, first_ref)
        return 0

    lax.fori_loop(0, 4, two, 0)
    finish(product(weights_ref, second_ref), 7, 7)
    for n in range(2):
        total = sums_ref[CH * n : CH * (n + 1)]
        row = jnp.sum((total[:, :CH] + total[:, CH:]).T, axis=0, keepdims=True)
        send_ref[:, n : n + 1, :] = jnp.broadcast_to(row[None], (128, 1, CH))
    for n in range(9):
        pltpu.make_async_copy(conv_ref.at[n], conv_hbm.at[n], out_sems.at[n]).wait()


def convolve(rows, index, weights):
    return pl.pallas_call(
        conv_body,
        name="convolve",
        out_shape=(shape((1, 2048), F32), shape((9, CH, SEG), F32), shape((128, 2, CH), F32)),
        in_specs=[HBM] * 3,
        out_specs=(VMEM, HBM, VMEM),
        scratch_shapes=[
            pltpu.VMEM((128, 16, CH), BF16),
            pltpu.VMEM((32, 16, CH), BF16),
            pltpu.VMEM((10 * CH, SEG), BF16),
            pltpu.VMEM((10 * CH, SEG), BF16),
            pltpu.VMEM((9, CH, SEG), F32),
            pltpu.VMEM((2 * CH, SEG), F32),
            pltpu.VMEM((27 * CH, SEG), BF16),
            pltpu.VMEM((27 * CH, SEG), BF16),
            pltpu.VMEM((432, 128), jnp.int32),
            pltpu.VMEM((CH, 27 * CH), BF16),
            pltpu.SemaphoreType.DMA((8,)),
            pltpu.SemaphoreType.DMA((9,)),
        ],
        compiler_params=params(52),
        cost_estimate=pl.CostEstimate(
            flops=8 * 27 * 2 * 384 * 256 * 256, bytes_accessed=4 << 20, transcendentals=0
        ),
    )(rows, index, weights)


def column(row):
    flat = jnp.broadcast_to(row, (CH, CH)).T
    return jnp.concatenate([flat, flat], axis=1)


def rims_body(
    rows_hbm, before_ref, after_ref, weights_hbm, gain_ref, shift_ref,
    conv_ref, filled_ref, columns_ref,
    rows_ref, even_ref, odd_ref, first_ref, second_ref, weights_ref, sems,
):
    places = [
        (rows_hbm.at[96:, 16:], 0), (rows_hbm.at[:16, :16], 32),
        (rows_hbm.at[112:, :16], 48), (rows_hbm.at[:32, 16:], 64),
    ]
    gets = [
        pltpu.make_async_copy(src, rows_ref.at[at : at + src.shape[0]], sems.at[n])
        for n, (src, at) in enumerate(places)
    ]
    get_weights = pltpu.make_async_copy(weights_hbm, weights_ref, sems.at[4])
    for get in gets + [get_weights]:
        get.start()
    columns_ref[:CH] = column(gain_ref[...])
    columns_ref[CH:] = column(shift_ref[...])
    for get in gets:
        get.wait()
    for side, index_ref, gathered_ref in ((0, before_ref, first_ref), (1, after_ref, second_ref)):
        for n in range(6):
            at = 48 * side + 8 * n
            table, filled = turn(rows_ref[at : at + 8].reshape(CH, CH))
            put_tile(even_ref.at[side], odd_ref.at[side], n, table)
            if 2 <= n < 4:
                lanes = SEG * side + CH * (n - 2)
                filled_ref[:, lanes : lanes + CH] = filled

        def slots_of(k, half):
            return index_ref[k : k + 1, CH * half : CH * (half + 1)]

        gather_block(even_ref.at[side], odd_ref.at[side], 0, slots_of, gathered_ref)
        if side == 0:
            get_weights.wait()
        conv_ref[side] = product(weights_ref, gathered_ref)


def rims(rows, before, after, weights, gain, shift):
    return pl.pallas_call(
        rims_body,
        name="rims",
        out_shape=(shape((2, CH, SEG), F32), shape((1, 2 * SEG), F32), shape((2 * CH, SEG), F32)),
        in_specs=[HBM, VMEM, VMEM, HBM, VMEM, VMEM],
        out_specs=(VMEM,) * 3,
        scratch_shapes=[
            pltpu.VMEM((96, 16, CH), BF16),
            pltpu.VMEM((2, 3 * CH, SEG), BF16),
            pltpu.VMEM((2, 3 * CH, SEG), BF16),
            pltpu.VMEM((27 * CH, SEG), BF16),
            pltpu.VMEM((27 * CH, SEG), BF16),
            pltpu.VMEM((CH, 27 * CH), BF16),
            pltpu.SemaphoreType.DMA((5,)),
        ],
        compiler_params=params(52),
        cost_estimate=pl.CostEstimate(
            flops=2 * 27 * 2 * 384 * 256 * 256, bytes_accessed=4 << 20, transcendentals=0
        ),
    )(rows, before, after, weights, gain, shift)


def pick(window, local):
    low = jnp.dot(window, onehot(local & (SEG - 1), SEG, 0), preferred_element_type=F32)
    high = jnp.broadcast_to(local >> 8, (CH, SEG))
    out = jnp.zeros((CH, SEG), F32)
    for s in range(window.shape[0] // CH):
        out = jnp.where(high == s, low[CH * s : CH * (s + 1)], out)
    return out.astype(BF16)


def final_body(
    totals_ref, columns_ref, rims_ref, rims_filled_ref, conv_hbm, filled_ref, index_ref, weights_hbm,
    hidden_ref, coarse_ref, table_ref, gathered_ref, conv_ref, weights_ref, sems,
):
    gets = [pltpu.make_async_copy(conv_hbm.at[b], conv_ref.at[b], sems.at[b]) for b in range(8)]
    get_weights = pltpu.make_async_copy(weights_hbm, weights_ref, sems.at[8])
    for get in gets + [get_weights]:
        get.start()
    totals = jnp.sum(totals_ref[...], axis=0) / 131072.0
    mean = column(totals[:1])
    scale = columns_ref[:CH] / jnp.sqrt(column(totals[1:]) - mean * mean + 1e-05)
    shift = columns_ref[CH:]
    for c in (0, 9, 1, 2, 3, 4, 5, 6, 7, 8):
        own = slice(SEG * (c - 1), SEG * c)
        if c in (0, 9):
            conv = rims_ref[c // 9]
            filled = rims_filled_ref[:, SEG * (c // 9) : SEG * (c // 9 + 1)]
        else:
            gets[c - 1].wait()
            conv, filled = conv_ref[c - 1], filled_ref[:, own]
        hidden = filled * jnp.maximum((conv - mean) * scale + shift, 0.0)
        table_ref[CH * c : CH * (c + 1)] = hidden.astype(BF16)
        if 0 < c < 9:
            hidden_ref[own, :] = hidden.T.astype(BF16)
    for b in range(4):
        window = table_ref[2 * CH * b : 2 * CH * b + 4 * CH, :]
        for k in range(0, 8, 2):
            index = jnp.concatenate(
                [index_ref[k : k + 1, CH * b : CH * (b + 1)], index_ref[k + 1 : k + 2, CH * b : CH * (b + 1)]],
                axis=1,
            )
            chosen = pick(window, index - 2 * SEG * b)
            gathered_ref[CH * k : CH * (k + 1), CH * b : CH * (b + 1)] = chosen[:, :CH]
            gathered_ref[CH * (k + 1) : CH * (k + 2), CH * b : CH * (b + 1)] = chosen[:, CH:]
    get_weights.wait()
    for b in range(2):
        out = jnp.dot(
            weights_ref[...], gathered_ref[:, SEG * b : SEG * (b + 1)], preferred_element_type=F32
        )
        coarse_ref[SEG * b : SEG * (b + 1), :] = out.T.astype(BF16)


def final(totals, columns, rims_conv, rims_filled, conv, filled, index, weights):
    return pl.pallas_call(
        final_body,
        name="final",
        out_shape=(shape((2048, CH), BF16), shape((512, 2 * CH), BF16)),
        in_specs=[VMEM] * 4 + [HBM] + [VMEM] * 2 + [HBM],
        out_specs=(VMEM,) * 2,
        scratch_shapes=[
            pltpu.VMEM((10 * CH, SEG), BF16),
            pltpu.VMEM((8 * CH, 512), BF16),
            pltpu.VMEM((8, CH, SEG), F32),
            pltpu.VMEM((2 * CH, 8 * CH), BF16),
            pltpu.SemaphoreType.DMA((9,)),
        ],
        compiler_params=params(50),
    )(totals, columns, rims_conv, rims_filled, conv, filled, index, weights)


def exchange(rows):
    return lax.all_to_all(rows, AXES, split_axis=0, concat_axis=0, tiled=True)


def shards(features, owners, kernel_map, fine_slots, conv_weight, gain, shift, down_weight):
    ndev = lax.axis_size("blocks") * lax.axis_size("depth")
    late = (lax.axis_index("blocks") >= lax.axis_size("blocks") // 2).astype(jnp.int32)
    up = [(i, i + 1) for i in range(ndev - 1)]
    down = [(i + 1, i) for i in range(ndev - 1)]
    index = kernel_map.reshape(27 * 16, 128)

    rows = exchange(route(late[None], features, owners.reshape(8, 128)))
    head, tail, weights, down_weights = prepare(index, conv_weight, down_weight)
    before = lax.ppermute(tail, AXES, up)
    after = lax.ppermute(head, AXES, down)
    filled, conv, send = convolve(rows, index, weights)
    totals = exchange(send)
    rims_conv, rims_filled, columns = rims(
        rows, before, after, weights, gain.reshape(1, CH), shift.reshape(1, CH)
    )
    return final(
        totals, columns, rims_conv, rims_filled, conv, filled, fine_slots.reshape(8, 512), down_weights
    )


def solution(mesh):
    split = P(AXES, None)
    placed = (split, split, P(AXES, None, None), P(AXES, None, None), P(), P(), P(), P())
    return jax.shard_map(
        shards, mesh=mesh, in_specs=placed, out_specs=(split, split), check_vma=False
    )
```

time: 72.3 us -> 66.8 us (0.924)
  Pallas kernels: 31.9 us -> 25.5 us
  waiting for transfers between devices: 15.2 us -> 16.9 us
    pallas_call x5, Pallas kernels: 31.9 us -> 25.5 us  [the longest x1 12.5 us: convolve(): pl.pallas_call(conv_body, name='convolve', out_shape=(shape((1, 2048), F3...]
    all_to_all x2, waiting for transfers between devices: 15.2 us -> 16.9 us  [exchange(): return lax.all_to_all(rows, AXES, split_axis=0, concat_axis=0, tiled=True)]
  transfers between devices with their start and end apart: 4 -> 4, of which waited for: 2 -> 2; matrix products, arithmetic and copies ran while one was open for 0% -> 0% of each run, Pallas kernels for 34% -> 26%
where the time goes in v3:
time: 66.8 us; the launch traced here: 66.6 us
  Pallas kernels  25.5 us (38%)
  starting transfers between devices  23.3 us (35%)
  waiting for transfers between devices  16.9 us (25%)
  between operations  0.79 us (1%)
    all_to_all x2, waiting for transfers between devices, exchange(): return lax.all_to_all(rows, AXES, split_axis=0, concat_axis=0, tiled=True)  16.9 us
    all_to_all x2, starting transfers between devices, exchange(): return lax.all_to_all(rows, AXES, split_axis=0, concat_axis=0, tiled=True)  16 us
    pallas_call x1, Pallas kernels, convolve(): pl.pallas_call(conv_body, name='convolve', out_shape=(shape((1, 2048), F3...  12.5 us
    pallas_call x1, Pallas kernels, final(): pl.pallas_call(final_body, name='final', out_shape=(shape((2048, CH), BF1...  5.06 us
    pallas_call x1, Pallas kernels, rims(): pl.pallas_call(rims_body, name='rims', out_shape=(shape((2, CH, SEG), F32...  4.21 us
    ppermute x1, starting transfers between devices, shards(): after = lax.ppermute(head, AXES, down)  3.92 us
    ppermute x1, starting transfers between devices, shards(): before = lax.ppermute(tail, AXES, up)  3.42 us
    pallas_call x1, Pallas kernels, route(): pl.pallas_call(route_body, name='route', out_shape=shape((128, 32, CH), B...  3.3 us
  transfers between devices with their start and end apart: 4, of which 2 were waited for; matrix products, arithmetic and copies ran while one was open for 0% of the time, Pallas kernels for 26%

profile of v3, /device:TPU:1, one launch (start us, length us, event | category | flops | bytes accessed | tf_op | source)
XLA Modules:
  0.0 66.6 jit_solution(9831752094354041943)
XLA Ops:
  0.6 3.3 %route.1 = bf16[128,32,128]{2,1,0:T(8,128)(2,1)} custom-call(s32[1]{0:T(128)} %bitcast.late_ref, bf16[1024,128]{1,0:T(8,128)(2,1)} %features_hbm.1, s32[8,128]{1,0:T(8,128)} %bitcast.11), custom_call_target="tpu_custom_call" | custom-call | tf_op jit(solution)/shard_map/route/pallas_call | solution.py:75
  3.9 0.0 copy-start.1
  4.0 0.0 copy-start.2
  4.0 0.0 copy-start.3
  4.0 11.9 %all-to-all-start = ((bf16[128,32,128]{2,1,0:T(8,128)(2,1)}), bf16[128,32,128]{2,1,0:T(8,128)(2,1)}, u32[]{:S(2)}, u32[]{:S(2)}) async-start(bf16[128,32,128]{2,1,0:T(8,128)(2,1)} %route.1), calls=%async_computation | async-start | bytes 2097152 | tf_op jit(solution)/shard_map/all_to_all | solution.py:418
  15.9 0.0 copy-done.1
  15.9 0.0 copy-done.2
  16.0 0.0 copy-done.3
  16.0 0.5 prepare.1
  16.4 3.4 %collective-permute-start = (s32[27,256]{1,0:T(8,128)S(1)}, s32[27,256]{1,0:T(8,128)S(1)}, u32[]{:S(2)}, u32[]{:S(2)}) collective-permute-start(s32[27,256]{1,0:T(8,128)S(1)} %get-tuple-element.14), channel_id=1, source_target_pairs={{0,1},{1,2},{2,3},{3,4},{4,5},{5,6},{6,7},{7,8},{8,9},{9,10},{10,1... | collective-permute-start | bytes 82952 | tf_op jit(solution)/shard_map/ppermute | solution.py:430
  19.9 3.9 %collective-permute-start.1 = (s32[27,256]{1,0:T(8,128)S(1)}, s32[27,256]{1,0:T(8,128)S(1)}, u32[]{:S(2)}, u32[]{:S(2)}) collective-permute-start(s32[27,256]{1,0:T(8,128)S(1)} %get-tuple-element.15), channel_id=1, source_target_pairs={{1,0},{2,1},{3,2},{4,3},{5,4},{6,5},{7,6},{8,7},{9,8},{10,9},{11,1... | collective-permute-start | bytes 82952 | tf_op jit(solution)/shard_map/ppermute | solution.py:431
  23.8 11.2 %all-to-all-done.rows_hbm = bf16[128,32,128]{2,1,0:T(8,128)(2,1)} async-done(((bf16[128,32,128]{2,1,0:T(8,128)(2,1)}), bf16[128,32,128]{2,1,0:T(8,128)(2,1)}, u32[]{:S(2)}, u32[]{:S(2)}) %all-to-all-start) | async-done | bytes 1048608 | tf_op jit(solution)/shard_map/all_to_all | solution.py:418
  35.0 12.5 %convolve.1 = (f32[1,2048]{1,0:T(1,128)S(1)}, f32[9,128,256]{2,1,0:T(8,128)}, f32[128,2,128]{2,1,0:T(2,128)}) custom-call(bf16[128,32,128]{2,1,0:T(8,128)(2,1)} %all-to-all-done.rows_hbm, s32[432,128]{1,0:T(8,128)S(1)} %bitcast.7, bf16[128,3456]{1,0:T(8,128)(2,1)S(1)} %get-tuple-element.12.weights_hbm), custom_call_target="tpu_custom_call" | custom-call | flops 10871635968 | bytes 4194304 | tf_op jit(solution)/shard_map/convolve/pallas_call | solution.py:255
  47.5 4.1 %all-to-all-start.1 = ((f32[128,2,128]{2,1,0:T(2,128)}), f32[128,2,128]{2,1,0:T(2,128)S(1)}, u32[]{:S(2)}, u32[]{:S(2)}) async-start(f32[128,2,128]{2,1,0:T(2,128)} %get-tuple-element.13), calls=%async_computation.1 | async-start | bytes 262144 | tf_op jit(solution)/shard_map/all_to_all | solution.py:418
  51.6 0.0 collective-permute-done.before_ref
  51.6 0.0 collective-permute-done.1.after_ref
  51.6 0.0 copy-done.5
  51.6 0.0 copy-done.6
  51.6 0.0 copy-start
  51.6 0.0 copy-start.4
  51.6 4.2 %rims.1 = (f32[2,128,256]{2,1,0:T(8,128)S(1)}, f32[1,512]{1,0:T(1,128)S(1)}, f32[256,256]{1,0:T(8,128)S(1)}) custom-call(bf16[128,32,128]{2,1,0:T(8,128)(2,1)} %all-to-all-done.rows_hbm, s32[27,256]{1,0:T(8,128)S(1)} %collective-permute-done.before_ref, s32[27,256]{1,0:T(8,128)S(1)} %collective-permute-done.1.after_ref, ...), custom_call_target="tpu_custom_call" | custom-call | flops 2717908992 | bytes 4194304 | tf_op jit(solution)/shard_map/rims/pallas_call | solution.py:326
  55.8 5.7 %all-to-all-done.1.totals_ref = f32[128,2,128]{2,1,0:T(2,128)S(1)} async-done(((f32[128,2,128]{2,1,0:T(2,128)}), f32[128,2,128]{2,1,0:T(2,128)S(1)}, u32[]{:S(2)}, u32[]{:S(2)}) %all-to-all-start.1) | async-done | bytes 131104 | tf_op jit(solution)/shard_map/all_to_all | solution.py:418
  61.5 0.0 copy-done.4
  61.5 5.1 %final.1 = (bf16[2048,128]{1,0:T(8,128)(2,1)}, bf16[512,256]{1,0:T(8,128)(2,1)}) custom-call(f32[128,2,128]{2,1,0:T(2,128)S(1)} %all-to-all-done.1.totals_ref, f32[256,256]{1,0:T(8,128)S(1)} %get-tuple-element.16.columns_ref, f32[2,128,256]{2,1,0:T(8,128)S(1)} %get-tuple-element.17.rims_ref, f32[1,512]{1,0:T(1,128)S(1)} %get-tuple-element.18.rims_filled_ref, ...), custom_call_target="tpu_custom_call" | custom-call | tf_op jit(solution)/shard_map/final/pallas_call | solution.py:400
  (3 shorter events, 0.0 us)
Async XLA Ops:
  3.9 12.0 %copy-start.1 = (bf16[27,128,128]{2,1,0:T(8,128)(2,1)S(1)}, bf16[27,128,128]{2,1,0:T(8,128)(2,1)}, u32[]{:S(2)}) copy-start(bf16[27,128,128]{2,1,0:T(8,128)(2,1)} %weights_ref.1) | copy-start | bytes 2654212
  4.0 12.0 %copy-start.2 = (bf16[8,128,256]{2,1,0:T(8,128)(2,1)S(1)}, bf16[8,128,256]{2,1,0:T(8,128)(2,1)}, u32[]{:S(2)}) copy-start(bf16[8,128,256]{2,1,0:T(8,128)(2,1)} %down_ref.1) | copy-start | bytes 1572868
  4.0 12.0 %copy-start.3 = (s32[1,27,2048]{2,0,1:T(1,128)S(1)}, s32[1,27,2048]{2,0,1:T(1,128)}, u32[]{:S(2)}) copy-start(s32[1,27,2048]{2,0,1:T(1,128)} %param.10) | copy-start | bytes 663556
  4.0 31.0 %all-to-all-start = ((bf16[128,32,128]{2,1,0:T(8,128)(2,1)}), bf16[128,32,128]{2,1,0:T(8,128)(2,1)}, u32[]{:S(2)}, u32[]{:S(2)}) async-start(bf16[128,32,128]{2,1,0:T(8,128)(2,1)} %route.1), calls=%async_computation | async-start | bytes 2097152 | tf_op jit(solution)/shard_map/all_to_all | solution.py:418
  16.4 35.1 %collective-permute-start = (s32[27,256]{1,0:T(8,128)S(1)}, s32[27,256]{1,0:T(8,128)S(1)}, u32[]{:S(2)}, u32[]{:S(2)}) collective-permute-start(s32[27,256]{1,0:T(8,128)S(1)} %get-tuple-element.14), channel_id=1, source_target_pairs={{0,1},{1,2},{2,3},{3,4},{4,5},{5,6},{6,7},{7,8},{8,9},{9,10},{10,1... | collective-permute-start | bytes 82952 | tf_op jit(solution)/shard_map/ppermute | solution.py:430
  19.9 31.7 %collective-permute-start.1 = (s32[27,256]{1,0:T(8,128)S(1)}, s32[27,256]{1,0:T(8,128)S(1)}, u32[]{:S(2)}, u32[]{:S(2)}) collective-permute-start(s32[27,256]{1,0:T(8,128)S(1)} %get-tuple-element.15), channel_id=1, source_target_pairs={{1,0},{2,1},{3,2},{4,3},{5,4},{6,5},{7,6},{8,7},{9,8},{10,9},{11,1... | collective-permute-start | bytes 82952 | tf_op jit(solution)/shard_map/ppermute | solution.py:431
  35.0 16.6 %copy-start.5 = (f32[128]{0:T(128)S(1)}, f32[128]{0:T(128)}, u32[]{:S(2)}) copy-start(f32[128]{0:T(128)} %param.13) | copy-start | bytes 1540
  35.0 16.6 %copy-start.6 = (f32[128]{0:T(128)S(1)}, f32[128]{0:T(128)}, u32[]{:S(2)}) copy-start(f32[128]{0:T(128)} %param.14) | copy-start | bytes 1540
  47.5 14.0 %all-to-all-start.1 = ((f32[128,2,128]{2,1,0:T(2,128)}), f32[128,2,128]{2,1,0:T(2,128)S(1)}, u32[]{:S(2)}, u32[]{:S(2)}) async-start(f32[128,2,128]{2,1,0:T(2,128)} %get-tuple-element.13), calls=%async_computation.1 | async-start | bytes 262144 | tf_op jit(solution)/shard_map/all_to_all | solution.py:418
  51.6 9.9 %copy-start = (f32[9,128,256]{2,1,0:T(8,128)S(1)}, f32[9,128,256]{2,1,0:T(8,128)}, u32[]{:S(2)}) copy-start(f32[9,128,256]{2,1,0:T(8,128)} %get-tuple-element.19.conv_hbm) | copy-start | bytes 3538948
  51.6 9.9 %copy-start.4 = (s32[1,8,512]{2,1,0:T(8,128)S(1)}, s32[1,8,512]{2,1,0:T(8,128)}, u32[]{:S(2)}) copy-start(s32[1,8,512]{2,1,0:T(8,128)} %param.11) | copy-start | bytes 49156

commit v4 on v3

--- a/solution.py
+++ b/solution.py
@@ -29,11 +29,13 @@
     return jnp.where(rows == local, BF16(1), BF16(0))
 
 
-def route_body(late_ref, features_hbm, owners_hbm, out_ref, features_ref, owners_ref, sems):
+def route_body(late_ref, features_hbm, owners_hbm, out_hbm, features_ref, owners_ref, own_ref, empty_ref, sems):
     get_owners = pltpu.make_async_copy(owners_hbm, owners_ref, sems.at[0])
     get_features = pltpu.make_async_copy(features_hbm, features_ref, sems.at[1])
     get_owners.start()
     get_features.start()
+    empty_ref[...] = jnp.full((1, 16, CH), jnp.inf, BF16)
+    puts = []
     upper = (
         lax.broadcasted_iota(jnp.int32, (SEG, SEG), 0)
         < lax.broadcasted_iota(jnp.int32, (SEG, SEG), 1)
@@ -57,18 +59,33 @@
         placed = jnp.concatenate([onehot(w, SEG, SEG * s) for w in where], axis=1)
         found = jnp.dot(placed, table, preferred_element_type=F32)
         rows = jnp.where(found[:, CH:] > 0.5, found[:, :CH], jnp.inf).astype(BF16)
-        out_ref[16 * s : 16 * (s + 1), :16, :] = rows.reshape(16, 16, CH)
+        part = slice(16 * s, 16 * (s + 1))
+        own_ref[part] = rows.reshape(16, 16, CH)
+        put = pltpu.make_async_copy(own_ref.at[part], out_hbm.at[part, :16], sems.at[2 + s])
+        put.start()
+        puts.append(put)
     late = late_ref[0] > 0
+
+    def neighbours(first, skipped, source):
+        rest = pltpu.make_async_copy(
+            own_ref.at[source : source + 127], out_hbm.at[first : first + 127, 16:], sems.at[10]
+        )
+        edge = pltpu.make_async_copy(empty_ref, out_hbm.at[skipped : skipped + 1, 16:], sems.at[11])
+        rest.start()
+        edge.start()
+        rest.wait()
+        edge.wait()
 
     @pl.when(late)
     def _():
-        out_ref[1:, 16:, :] = out_ref[:127, :16, :]
-        out_ref[:1, 16:, :] = jnp.full((1, 16, CH), jnp.inf, BF16)
+        neighbours(1, 0, 0)
 
     @pl.when(jnp.logical_not(late))
     def _():
-        out_ref[:127, 16:, :] = out_ref[1:, :16, :]
-        out_ref[127:, 16:, :] = jnp.full((1, 16, CH), jnp.inf, BF16)
+        neighbours(0, 127, 1)
+
+    for put in puts:
+        put.wait()
 
 
 def route(late, features, owners):
@@ -77,11 +94,13 @@
         name="route",
         out_shape=shape((128, 32, CH), BF16),
         in_specs=[SMEM] + [HBM] * 2,
-        out_specs=VMEM,
+        out_specs=HBM,
         scratch_shapes=[
             pltpu.VMEM((1024, CH), BF16),
             pltpu.VMEM((8, 128), jnp.int32),
-            pltpu.SemaphoreType.DMA((2,)),
+            pltpu.VMEM((128, 16, CH), BF16),
+            pltpu.VMEM((1, 16, CH), BF16),
+            pltpu.SemaphoreType.DMA((12,)),
         ],
         compiler_params=params(60),
     )(late, features, owners)
@@ -280,13 +299,16 @@
 
 
 def column(row):
-    flat = jnp.broadcast_to(row, (CH, CH)).T
-    return jnp.concatenate([flat, flat], axis=1)
+    return jnp.broadcast_to(row, (CH, CH)).T
+
+
+def twice(block):
+    return jnp.concatenate([block, block], axis=1)
 
 
 def rims_body(
-    rows_hbm, before_ref, after_ref, weights_hbm, gain_ref, shift_ref,
-    conv_ref, filled_ref, columns_ref,
+    rows_hbm, before_ref, after_ref, weights_hbm, gain_ref, shift_ref, own_conv_ref, own_filled_ref,
+    conv_ref, filled_ref, columns_ref, flat_ref,
     rows_ref, even_ref, odd_ref, first_ref, second_ref, weights_ref, sems,
 ):
     places = [
@@ -320,15 +342,24 @@
         if side == 0:
             get_weights.wait()
         conv_ref[side] = product(weights_ref, gathered_ref)
-
-
-def rims(rows, before, after, weights, gain, shift):
+    for b in range(8):
+        lanes = slice(SEG * b, SEG * (b + 1))
+        kept = jnp.where(own_filled_ref[:, lanes] > 0, own_conv_ref[b], -jnp.inf)
+        flat_ref[lanes, :] = kept.T
+
+
+def rims(rows, before, after, weights, gain, shift, conv, filled):
     return pl.pallas_call(
         rims_body,
         name="rims",
-        out_shape=(shape((2, CH, SEG), F32), shape((1, 2 * SEG), F32), shape((2 * CH, SEG), F32)),
-        in_specs=[HBM, VMEM, VMEM, HBM, VMEM, VMEM],
-        out_specs=(VMEM,) * 3,
+        out_shape=(
+            shape((2, CH, SEG), F32),
+            shape((1, 2 * SEG), F32),
+            shape((2 * CH, CH), F32),
+            shape((2048, CH), F32),
+        ),
+        in_specs=[HBM, VMEM, VMEM, HBM] + [VMEM] * 4,
+        out_specs=(VMEM,) * 4,
         scratch_shapes=[
             pltpu.VMEM((96, 16, CH), BF16),
             pltpu.VMEM((2, 3 * CH, SEG), BF16),
@@ -342,7 +373,7 @@
         cost_estimate=pl.CostEstimate(
             flops=2 * 27 * 2 * 384 * 256 * 256, bytes_accessed=4 << 20, transcendentals=0
         ),
-    )(rows, before, after, weights, gain, shift)
+    )(rows, before, after, weights, gain, shift, conv, filled)
 
 
 def pick(window, local):
@@ -355,30 +386,48 @@
 
 
 def final_body(
-    totals_ref, columns_ref, rims_ref, rims_filled_ref, conv_hbm, filled_ref, index_ref, weights_hbm,
-    hidden_ref, coarse_ref, table_ref, gathered_ref, conv_ref, weights_ref, sems,
+    totals_ref, gain_ref, shift_ref, columns_ref, rims_ref, rims_filled_ref, conv_hbm, filled_ref,
+    flat_hbm, index_ref, weights_ref,
+    hidden_hbm, coarse_hbm, table_ref, gathered_ref, hidden_ref, coarse_ref, flat_ref, conv_ref, sems,
 ):
-    gets = [pltpu.make_async_copy(conv_hbm.at[b], conv_ref.at[b], sems.at[b]) for b in range(8)]
-    get_weights = pltpu.make_async_copy(weights_hbm, weights_ref, sems.at[8])
-    for get in gets + [get_weights]:
+    conv_gets = [
+        pltpu.make_async_copy(conv_hbm.at[b], conv_ref.at[b], sems.at[10 + b]) for b in range(8)
+    ]
+    gets = [
+        pltpu.make_async_copy(
+            flat_hbm.at[512 * b : 512 * (b + 1)], flat_ref.at[512 * b : 512 * (b + 1)], sems.at[6 + b]
+        )
+        for b in range(4)
+    ]
+    for get in conv_gets + gets:
         get.start()
     totals = jnp.sum(totals_ref[...], axis=0) / 131072.0
-    mean = column(totals[:1])
-    scale = columns_ref[:CH] / jnp.sqrt(column(totals[1:]) - mean * mean + 1e-05)
-    shift = columns_ref[CH:]
+    mean_row = totals[:1]
+    root_row = jnp.sqrt(totals[1:] - mean_row * mean_row + 1e-05)
+    mean = twice(column(mean_row))
+    scale = twice(columns_ref[:CH] / column(root_row))
+    shift = twice(columns_ref[CH:])
     for c in (0, 9, 1, 2, 3, 4, 5, 6, 7, 8):
         own = slice(SEG * (c - 1), SEG * c)
         if c in (0, 9):
             conv = rims_ref[c // 9]
             filled = rims_filled_ref[:, SEG * (c // 9) : SEG * (c // 9 + 1)]
         else:
-            gets[c - 1].wait()
+            conv_gets[c - 1].wait()
             conv, filled = conv_ref[c - 1], filled_ref[:, own]
         hidden = filled * jnp.maximum((conv - mean) * scale + shift, 0.0)
         table_ref[CH * c : CH * (c + 1)] = hidden.astype(BF16)
-        if 0 < c < 9:
-            hidden_ref[own, :] = hidden.T.astype(BF16)
+    scale_row = gain_ref[...] / root_row
+    puts = []
     for b in range(4):
+        own = slice(512 * b, 512 * (b + 1))
+        gets[b].wait()
+        flat = flat_ref[own, :]
+        hidden = jnp.maximum((flat - mean_row) * scale_row + shift_ref[...], 0.0)
+        hidden_ref[own, :] = jnp.where(flat > -jnp.inf, hidden, 0.0).astype(BF16)
+        put = pltpu.make_async_copy(hidden_ref.at[own], hidden_hbm.at[own], sems.at[b])
+        put.start()
+        puts.append(put)
         window = table_ref[2 * CH * b : 2 * CH * b + 4 * CH, :]
         for k in range(0, 8, 2):
             index = jnp.concatenate(
@@ -388,30 +437,38 @@
             chosen = pick(window, index - 2 * SEG * b)
             gathered_ref[CH * k : CH * (k + 1), CH * b : CH * (b + 1)] = chosen[:, :CH]
             gathered_ref[CH * (k + 1) : CH * (k + 2), CH * b : CH * (b + 1)] = chosen[:, CH:]
-    get_weights.wait()
-    for b in range(2):
-        out = jnp.dot(
-            weights_ref[...], gathered_ref[:, SEG * b : SEG * (b + 1)], preferred_element_type=F32
-        )
-        coarse_ref[SEG * b : SEG * (b + 1), :] = out.T.astype(BF16)
-
-
-def final(totals, columns, rims_conv, rims_filled, conv, filled, index, weights):
+        if b % 2:
+            out = jnp.dot(
+                weights_ref[...], gathered_ref[:, SEG * (b // 2) : SEG * (b // 2 + 1)],
+                preferred_element_type=F32,
+            )
+            part = slice(SEG * (b // 2), SEG * (b // 2 + 1))
+            coarse_ref[part, :] = out.T.astype(BF16)
+            put = pltpu.make_async_copy(coarse_ref.at[part], coarse_hbm.at[part], sems.at[4 + b // 2])
+            put.start()
+            puts.append(put)
+    for put in puts:
+        put.wait()
+
+
+def final(totals, gain, shift, columns, rims_conv, rims_filled, conv, filled, flat, index, weights):
     return pl.pallas_call(
         final_body,
         name="final",
         out_shape=(shape((2048, CH), BF16), shape((512, 2 * CH), BF16)),
-        in_specs=[VMEM] * 4 + [HBM] + [VMEM] * 2 + [HBM],
-        out_specs=(VMEM,) * 2,
+        in_specs=[VMEM] * 6 + [HBM, VMEM, HBM, VMEM, VMEM],
+        out_specs=(HBM, HBM),
         scratch_shapes=[
             pltpu.VMEM((10 * CH, SEG), BF16),
             pltpu.VMEM((8 * CH, 512), BF16),
+            pltpu.VMEM((2048, CH), BF16),
+            pltpu.VMEM((512, 2 * CH), BF16),
+            pltpu.VMEM((2048, CH), F32),
             pltpu.VMEM((8, CH, SEG), F32),
-            pltpu.VMEM((2 * CH, 8 * CH), BF16),
-            pltpu.SemaphoreType.DMA((9,)),
+            pltpu.SemaphoreType.DMA((18,)),
         ],
-        compiler_params=params(50),
-    )(totals, columns, rims_conv, rims_filled, conv, filled, index, weights)
+        compiler_params=params(52),
+    )(totals, gain, shift, columns, rims_conv, rims_filled, conv, filled, flat, index, weights)
 
 
 def exchange(rows):
@@ -431,11 +488,13 @@
     after = lax.ppermute(head, AXES, down)
     filled, conv, send = convolve(rows, index, weights)
     totals = exchange(send)
-    rims_conv, rims_filled, columns = rims(
-        rows, before, after, weights, gain.reshape(1, CH), shift.reshape(1, CH)
+    gain, shift = gain.reshape(1, CH), shift.reshape(1, CH)
+    rims_conv, rims_filled, columns, flat = rims(
+        rows, before, after, weights, gain, shift, conv, filled
     )
     return final(
-        totals, columns, rims_conv, rims_filled, conv, filled, fine_slots.reshape(8, 512), down_weights
+        totals, gain, shift, columns, rims_conv, rims_filled, conv, filled, flat,
+        fine_slots.reshape(8, 512), down_weights,
     )
 
 

time: 66.8 us -> 67.2 us (level)
  Pallas kernels: 25.5 us -> 27.8 us
  waiting for transfers between devices: 16.9 us -> 14.8 us
    pallas_call x1, Pallas kernels: 4.21 us -> 6.29 us  [rims(): pl.pallas_call(rims_body, name='rims', out_shape=(shape((2, CH, SEG), F32...]
    all_to_all x2, waiting for transfers between devices: 16.9 us -> 14.8 us  [exchange(): return lax.all_to_all(rows, AXES, split_axis=0, concat_axis=0, tiled=True)]
  transfers between devices with their start and end apart: 4 -> 4, of which waited for: 2 -> 2; matrix products, arithmetic and copies ran while one was open for 0% -> 0% of each run, Pallas kernels for 26% -> 29%
where the time goes in v4:
time: 67.2 us; the launch traced here: 66.9 us
  Pallas kernels  27.8 us (41%)
  starting transfers between devices  23.3 us (35%)
  waiting for transfers between devices  14.8 us (22%)
  between operations  0.95 us (1%)
    all_to_all x2, starting transfers between devices, exchange(): return lax.all_to_all(rows, AXES, split_axis=0, concat_axis=0, tiled=True)  16 us
    all_to_all x2, waiting for transfers between devices, exchange(): return lax.all_to_all(rows, AXES, split_axis=0, concat_axis=0, tiled=True)  14.8 us
    pallas_call x1, Pallas kernels, convolve(): pl.pallas_call(conv_body, name='convolve', out_shape=(shape((1, 2048), F3...  12.5 us
    pallas_call x1, Pallas kernels, rims(): pl.pallas_call(rims_body, name='rims', out_shape=(shape((2, CH, SEG), F32...  6.29 us
    pallas_call x1, Pallas kernels, final(): pl.pallas_call(final_body, name='final', out_shape=(shape((2048, CH), BF1...  5.26 us
    ppermute x1, starting transfers between devices, shards(): after = lax.ppermute(head, AXES, down)  3.92 us
    ppermute x1, starting transfers between devices, shards(): before = lax.ppermute(tail, AXES, up)  3.42 us
    pallas_call x1, Pallas kernels, route(): pl.pallas_call(route_body, name='route', out_shape=shape((128, 32, CH), B...  3.27 us
  transfers between devices with their start and end apart: 4, of which 2 were waited for; matrix products, arithmetic and copies ran while one was open for 0% of the time, Pallas kernels for 29%

profile of v4, /device:TPU:1, one launch (start us, length us, event | category | flops | bytes accessed | tf_op | source)
XLA Modules:
  0.0 66.9 jit_solution(2012580458960333441)
XLA Ops:
  0.6 3.3 %route.1 = bf16[128,32,128]{2,1,0:T(8,128)(2,1)} custom-call(s32[1]{0:T(128)} %bitcast.late_ref, bf16[1024,128]{1,0:T(8,128)(2,1)} %features_hbm.1, s32[8,128]{1,0:T(8,128)} %bitcast.13), custom_call_target="tpu_custom_call" | custom-call | tf_op jit(solution)/shard_map/route/pallas_call | solution.py:92
  3.9 0.0 copy-start
  3.9 0.0 copy-start.1
  3.9 0.0 copy-start.2
  3.9 12.0 %all-to-all-start = ((bf16[128,32,128]{2,1,0:T(8,128)(2,1)}), bf16[128,32,128]{2,1,0:T(8,128)(2,1)}, u32[]{:S(2)}, u32[]{:S(2)}) async-start(bf16[128,32,128]{2,1,0:T(8,128)(2,1)} %route.1), calls=%async_computation | async-start | bytes 2097152 | tf_op jit(solution)/shard_map/all_to_all | solution.py:475
  15.9 0.0 copy-done
  15.9 0.0 copy-done.1
  15.9 0.0 copy-done.2
  15.9 0.5 prepare.1
  16.4 3.4 %collective-permute-start = (s32[27,256]{1,0:T(8,128)S(1)}, s32[27,256]{1,0:T(8,128)S(1)}, u32[]{:S(2)}, u32[]{:S(2)}) collective-permute-start(s32[27,256]{1,0:T(8,128)S(1)} %get-tuple-element.15), channel_id=1, source_target_pairs={{0,1},{1,2},{2,3},{3,4},{4,5},{5,6},{6,7},{7,8},{8,9},{9,10},{10,1... | collective-permute-start | bytes 82952 | tf_op jit(solution)/shard_map/ppermute | solution.py:487
  19.8 3.9 %collective-permute-start.1 = (s32[27,256]{1,0:T(8,128)S(1)}, s32[27,256]{1,0:T(8,128)S(1)}, u32[]{:S(2)}, u32[]{:S(2)}) collective-permute-start(s32[27,256]{1,0:T(8,128)S(1)} %get-tuple-element.16), channel_id=1, source_target_pairs={{1,0},{2,1},{3,2},{4,3},{5,4},{6,5},{7,6},{8,7},{9,8},{10,9},{11,1... | collective-permute-start | bytes 82952 | tf_op jit(solution)/shard_map/ppermute | solution.py:488
  23.8 11.2 %all-to-all-done.rows_hbm = bf16[128,32,128]{2,1,0:T(8,128)(2,1)} async-done(((bf16[128,32,128]{2,1,0:T(8,128)(2,1)}), bf16[128,32,128]{2,1,0:T(8,128)(2,1)}, u32[]{:S(2)}, u32[]{:S(2)}) %all-to-all-start) | async-done | bytes 1048608 | tf_op jit(solution)/shard_map/all_to_all | solution.py:475
  35.0 0.0 copy-start.4
  35.0 12.5 %convolve.1 = (f32[1,2048]{1,0:T(1,128)S(1)}, f32[9,128,256]{2,1,0:T(8,128)}, f32[128,2,128]{2,1,0:T(2,128)}) custom-call(bf16[128,32,128]{2,1,0:T(8,128)(2,1)} %all-to-all-done.rows_hbm, s32[432,128]{1,0:T(8,128)S(1)} %bitcast.7, bf16[128,3456]{1,0:T(8,128)(2,1)S(1)} %get-tuple-element.13.weights_hbm), custom_call_target="tpu_custom_call" | custom-call | flops 10871635968 | bytes 4194304 | tf_op jit(solution)/shard_map/convolve/pallas_call | solution.py:274
  47.5 4.1 %all-to-all-start.1 = ((f32[128,2,128]{2,1,0:T(2,128)}), f32[128,2,128]{2,1,0:T(2,128)S(1)}, u32[]{:S(2)}, u32[]{:S(2)}) async-start(f32[128,2,128]{2,1,0:T(2,128)} %get-tuple-element.14), calls=%async_computation.1 | async-start | bytes 262144 | tf_op jit(solution)/shard_map/all_to_all | solution.py:475
  51.5 0.0 collective-permute-done.before_ref
  51.6 0.0 collective-permute-done.1.after_ref
  51.6 0.0 copy-done.4
  51.6 0.0 copy-done.5
  51.6 0.0 copy-start.3
  51.6 6.3 %rims.1 = (f32[2,128,256]{2,1,0:T(8,128)S(1)}, f32[1,512]{1,0:T(1,128)S(1)}, f32[256,128]{1,0:T(8,128)S(1)}, f32[2048,128]{1,0:T(8,128)}) custom-call(bf16[128,32,128]{2,1,0:T(8,128)(2,1)} %all-to-all-done.rows_hbm, s32[27,256]{1,0:T(8,128)S(1)} %collective-permute-done.before_ref, s32[27,256]{1,0:T(8,128)S(1)} %collective-permute-done.1.after_ref, ...), custom_call_target="tpu_custom_call" | custom-call | flops 2717908992 | bytes 4194304 | tf_op jit(solution)/shard_map/rims/pallas_call | solution.py:352
  57.9 3.6 %all-to-all-done.1.totals_ref = f32[128,2,128]{2,1,0:T(2,128)S(1)} async-done(((f32[128,2,128]{2,1,0:T(2,128)}), f32[128,2,128]{2,1,0:T(2,128)S(1)}, u32[]{:S(2)}, u32[]{:S(2)}) %all-to-all-start.1) | async-done | bytes 131104 | tf_op jit(solution)/shard_map/all_to_all | solution.py:475
  61.5 0.0 copy-done.3
  61.5 5.3 %final.1 = (bf16[2048,128]{1,0:T(8,128)(2,1)}, bf16[512,256]{1,0:T(8,128)(2,1)}) custom-call(f32[128,2,128]{2,1,0:T(2,128)S(1)} %all-to-all-done.1.totals_ref, f32[1,128]{1,0:T(1,128)S(1)} %bitcast.10, f32[1,128]{1,0:T(1,128)S(1)} %bitcast.12, f32[256,128]{1,0:T(8,128)S(1)} %get-tuple-element.19.columns_ref, f32[2,128,256]{2,1,0:T(8,128)S(1)} %get-tuple-element.20.rims_ref, ...), custom_call_target="tpu_custom_call" | custom-call | tf_op jit(solution)/shard_map/final/pallas_call | solution.py:455
  (1 shorter events, 0.0 us)
Async XLA Ops:
  3.9 12.0 %copy-start = (bf16[27,128,128]{2,1,0:T(8,128)(2,1)S(1)}, bf16[27,128,128]{2,1,0:T(8,128)(2,1)}, u32[]{:S(2)}) copy-start(bf16[27,128,128]{2,1,0:T(8,128)(2,1)} %weights_ref.1) | copy-start | bytes 2654212
  3.9 12.0 %copy-start.1 = (bf16[8,128,256]{2,1,0:T(8,128)(2,1)S(1)}, bf16[8,128,256]{2,1,0:T(8,128)(2,1)}, u32[]{:S(2)}) copy-start(bf16[8,128,256]{2,1,0:T(8,128)(2,1)} %down_ref.1) | copy-start | bytes 1572868
  3.9 12.0 %copy-start.2 = (s32[1,27,2048]{2,0,1:T(1,128)S(1)}, s32[1,27,2048]{2,0,1:T(1,128)}, u32[]{:S(2)}) copy-start(s32[1,27,2048]{2,0,1:T(1,128)} %param.10) | copy-start | bytes 663556
  3.9 31.0 %all-to-all-start = ((bf16[128,32,128]{2,1,0:T(8,128)(2,1)}), bf16[128,32,128]{2,1,0:T(8,128)(2,1)}, u32[]{:S(2)}, u32[]{:S(2)}) async-start(bf16[128,32,128]{2,1,0:T(8,128)(2,1)} %route.1), calls=%async_computation | async-start | bytes 2097152 | tf_op jit(solution)/shard_map/all_to_all | solution.py:475
  16.4 35.1 %collective-permute-start = (s32[27,256]{1,0:T(8,128)S(1)}, s32[27,256]{1,0:T(8,128)S(1)}, u32[]{:S(2)}, u32[]{:S(2)}) collective-permute-start(s32[27,256]{1,0:T(8,128)S(1)} %get-tuple-element.15), channel_id=1, source_target_pairs={{0,1},{1,2},{2,3},{3,4},{4,5},{5,6},{6,7},{7,8},{8,9},{9,10},{10,1... | collective-permute-start | bytes 82952 | tf_op jit(solution)/shard_map/ppermute | solution.py:487
  19.8 31.7 %collective-permute-start.1 = (s32[27,256]{1,0:T(8,128)S(1)}, s32[27,256]{1,0:T(8,128)S(1)}, u32[]{:S(2)}, u32[]{:S(2)}) collective-permute-start(s32[27,256]{1,0:T(8,128)S(1)} %get-tuple-element.16), channel_id=1, source_target_pairs={{1,0},{2,1},{3,2},{4,3},{5,4},{6,5},{7,6},{8,7},{9,8},{10,9},{11,1... | collective-permute-start | bytes 82952 | tf_op jit(solution)/shard_map/ppermute | solution.py:488
  35.0 16.6 %copy-start.4 = (f32[128]{0:T(128)S(1)}, f32[128]{0:T(128)}, u32[]{:S(2)}) copy-start(f32[128]{0:T(128)} %param.13) | copy-start | bytes 1540
  35.0 16.6 %copy-start.5 = (f32[128]{0:T(128)S(1)}, f32[128]{0:T(128)}, u32[]{:S(2)}) copy-start(f32[128]{0:T(128)} %param.14) | copy-start | bytes 1540
  47.5 14.0 %all-to-all-start.1 = ((f32[128,2,128]{2,1,0:T(2,128)}), f32[128,2,128]{2,1,0:T(2,128)S(1)}, u32[]{:S(2)}, u32[]{:S(2)}) async-start(f32[128,2,128]{2,1,0:T(2,128)} %get-tuple-element.14), calls=%async_computation.1 | async-start | bytes 262144 | tf_op jit(solution)/shard_map/all_to_all | solution.py:475
  51.6 9.9 %copy-start.3 = (s32[1,8,512]{2,1,0:T(8,128)S(1)}, s32[1,8,512]{2,1,0:T(8,128)}, u32[]{:S(2)}) copy-start(s32[1,8,512]{2,1,0:T(8,128)} %param.11) | copy-start | bytes 49156

commit v5 on v3

--- a/solution.py
+++ b/solution.py
@@ -29,11 +29,13 @@
     return jnp.where(rows == local, BF16(1), BF16(0))
 
 
-def route_body(late_ref, features_hbm, owners_hbm, out_ref, features_ref, owners_ref, sems):
+def route_body(late_ref, features_hbm, owners_hbm, out_hbm, features_ref, owners_ref, own_ref, empty_ref, sems):
     get_owners = pltpu.make_async_copy(owners_hbm, owners_ref, sems.at[0])
     get_features = pltpu.make_async_copy(features_hbm, features_ref, sems.at[1])
     get_owners.start()
     get_features.start()
+    empty_ref[...] = jnp.full((1, 16, CH), jnp.inf, BF16)
+    puts = []
     upper = (
         lax.broadcasted_iota(jnp.int32, (SEG, SEG), 0)
         < lax.broadcasted_iota(jnp.int32, (SEG, SEG), 1)
@@ -57,18 +59,33 @@
         placed = jnp.concatenate([onehot(w, SEG, SEG * s) for w in where], axis=1)
         found = jnp.dot(placed, table, preferred_element_type=F32)
         rows = jnp.where(found[:, CH:] > 0.5, found[:, :CH], jnp.inf).astype(BF16)
-        out_ref[16 * s : 16 * (s + 1), :16, :] = rows.reshape(16, 16, CH)
+        part = slice(16 * s, 16 * (s + 1))
+        own_ref[part] = rows.reshape(16, 16, CH)
+        put = pltpu.make_async_copy(own_ref.at[part], out_hbm.at[part, :16], sems.at[2 + s])
+        put.start()
+        puts.append(put)
     late = late_ref[0] > 0
+
+    def neighbours(first, skipped, source):
+        rest = pltpu.make_async_copy(
+            own_ref.at[source : source + 127], out_hbm.at[first : first + 127, 16:], sems.at[10]
+        )
+        edge = pltpu.make_async_copy(empty_ref, out_hbm.at[skipped : skipped + 1, 16:], sems.at[11])
+        rest.start()
+        edge.start()
+        rest.wait()
+        edge.wait()
 
     @pl.when(late)
     def _():
-        out_ref[1:, 16:, :] = out_ref[:127, :16, :]
-        out_ref[:1, 16:, :] = jnp.full((1, 16, CH), jnp.inf, BF16)
+        neighbours(1, 0, 0)
 
     @pl.when(jnp.logical_not(late))
     def _():
-        out_ref[:127, 16:, :] = out_ref[1:, :16, :]
-        out_ref[127:, 16:, :] = jnp.full((1, 16, CH), jnp.inf, BF16)
+        neighbours(0, 127, 1)
+
+    for put in puts:
+        put.wait()
 
 
 def route(late, features, owners):
@@ -77,11 +94,13 @@
         name="route",
         out_shape=shape((128, 32, CH), BF16),
         in_specs=[SMEM] + [HBM] * 2,
-        out_specs=VMEM,
+        out_specs=HBM,
         scratch_shapes=[
             pltpu.VMEM((1024, CH), BF16),
             pltpu.VMEM((8, 128), jnp.int32),
-            pltpu.SemaphoreType.DMA((2,)),
+            pltpu.VMEM((128, 16, CH), BF16),
+            pltpu.VMEM((1, 16, CH), BF16),
+            pltpu.SemaphoreType.DMA((12,)),
         ],
         compiler_params=params(60),
     )(late, features, owners)
@@ -355,29 +374,29 @@
 
 
 def final_body(
-    totals_ref, columns_ref, rims_ref, rims_filled_ref, conv_hbm, filled_ref, index_ref, weights_hbm,
-    hidden_ref, coarse_ref, table_ref, gathered_ref, conv_ref, weights_ref, sems,
+    totals_ref, columns_ref, rims_ref, rims_filled_ref, conv_ref, filled_ref, index_ref, weights_ref,
+    hidden_hbm, coarse_hbm, table_ref, gathered_ref, hidden_ref, coarse_ref, sems,
 ):
-    gets = [pltpu.make_async_copy(conv_hbm.at[b], conv_ref.at[b], sems.at[b]) for b in range(8)]
-    get_weights = pltpu.make_async_copy(weights_hbm, weights_ref, sems.at[8])
-    for get in gets + [get_weights]:
-        get.start()
     totals = jnp.sum(totals_ref[...], axis=0) / 131072.0
-    mean = column(totals[:1])
-    scale = columns_ref[:CH] / jnp.sqrt(column(totals[1:]) - mean * mean + 1e-05)
+    mean_row = totals[:1]
+    mean = column(mean_row)
+    scale = columns_ref[:CH] / column(jnp.sqrt(totals[1:] - mean_row * mean_row + 1e-05))
     shift = columns_ref[CH:]
-    for c in (0, 9, 1, 2, 3, 4, 5, 6, 7, 8):
+    puts = []
+    for c in range(10):
         own = slice(SEG * (c - 1), SEG * c)
         if c in (0, 9):
             conv = rims_ref[c // 9]
             filled = rims_filled_ref[:, SEG * (c // 9) : SEG * (c // 9 + 1)]
         else:
-            gets[c - 1].wait()
             conv, filled = conv_ref[c - 1], filled_ref[:, own]
         hidden = filled * jnp.maximum((conv - mean) * scale + shift, 0.0)
         table_ref[CH * c : CH * (c + 1)] = hidden.astype(BF16)
         if 0 < c < 9:
             hidden_ref[own, :] = hidden.T.astype(BF16)
+            put = pltpu.make_async_copy(hidden_ref.at[own], hidden_hbm.at[own], sems.at[c - 1])
+            put.start()
+            puts.append(put)
     for b in range(4):
         window = table_ref[2 * CH * b : 2 * CH * b + 4 * CH, :]
         for k in range(0, 8, 2):
@@ -388,12 +407,15 @@
             chosen = pick(window, index - 2 * SEG * b)
             gathered_ref[CH * k : CH * (k + 1), CH * b : CH * (b + 1)] = chosen[:, :CH]
             gathered_ref[CH * (k + 1) : CH * (k + 2), CH * b : CH * (b + 1)] = chosen[:, CH:]
-    get_weights.wait()
-    for b in range(2):
-        out = jnp.dot(
-            weights_ref[...], gathered_ref[:, SEG * b : SEG * (b + 1)], preferred_element_type=F32
-        )
-        coarse_ref[SEG * b : SEG * (b + 1), :] = out.T.astype(BF16)
+        if b % 2:
+            part = slice(SEG * (b // 2), SEG * (b // 2 + 1))
+            out = jnp.dot(weights_ref[...], gathered_ref[:, part], preferred_element_type=F32)
+            coarse_ref[part, :] = out.T.astype(BF16)
+            put = pltpu.make_async_copy(coarse_ref.at[part], coarse_hbm.at[part], sems.at[8 + b // 2])
+            put.start()
+            puts.append(put)
+    for put in puts:
+        put.wait()
 
 
 def final(totals, columns, rims_conv, rims_filled, conv, filled, index, weights):
@@ -401,14 +423,14 @@
         final_body,
         name="final",
         out_shape=(shape((2048, CH), BF16), shape((512, 2 * CH), BF16)),
-        in_specs=[VMEM] * 4 + [HBM] + [VMEM] * 2 + [HBM],
-        out_specs=(VMEM,) * 2,
+        in_specs=[VMEM] * 8,
+        out_specs=(HBM, HBM),
         scratch_shapes=[
             pltpu.VMEM((10 * CH, SEG), BF16),
             pltpu.VMEM((8 * CH, 512), BF16),
-            pltpu.VMEM((8, CH, SEG), F32),
-            pltpu.VMEM((2 * CH, 8 * CH), BF16),
-            pltpu.SemaphoreType.DMA((9,)),
+            pltpu.VMEM((2048, CH), BF16),
+            pltpu.VMEM((512, 2 * CH), BF16),
+            pltpu.SemaphoreType.DMA((10,)),
         ],
         compiler_params=params(50),
     )(totals, columns, rims_conv, rims_filled, conv, filled, index, weights)

time: 66.8 us -> 64.8 us (0.970)
  Pallas kernels: 25.5 us -> 23.5 us
    pallas_call x1, Pallas kernels: 5.06 us -> 3.03 us  [final(): pl.pallas_call(final_body, name='final', out_shape=(shape((2048, CH), BF1...]
  transfers between devices with their start and end apart: 4 -> 4, of which waited for: 2 -> 2; matrix products, arithmetic and copies ran while one was open for 0% -> 0% of each run, Pallas kernels for 26% -> 27%
where the time goes in v5:
time: 64.8 us; the launch traced here: 64.5 us
  Pallas kernels  23.5 us (36%)
  starting transfers between devices  23.3 us (36%)
  waiting for transfers between devices  16.9 us (26%)
  between operations  0.79 us (1%)
    all_to_all x2, waiting for transfers between devices, exchange(): return lax.all_to_all(rows, AXES, split_axis=0, concat_axis=0, tiled=True)  16.9 us
    all_to_all x2, starting transfers between devices, exchange(): return lax.all_to_all(rows, AXES, split_axis=0, concat_axis=0, tiled=True)  16 us
    pallas_call x1, Pallas kernels, convolve(): pl.pallas_call(conv_body, name='convolve', out_shape=(shape((1, 2048), F3...  12.5 us
    pallas_call x1, Pallas kernels, rims(): pl.pallas_call(rims_body, name='rims', out_shape=(shape((2, CH, SEG), F32...  4.21 us
    ppermute x1, starting transfers between devices, shards(): after = lax.ppermute(head, AXES, down)  3.92 us
    ppermute x1, starting transfers between devices, shards(): before = lax.ppermute(tail, AXES, up)  3.42 us
    pallas_call x1, Pallas kernels, route(): pl.pallas_call(route_body, name='route', out_shape=shape((128, 32, CH), B...  3.26 us
    pallas_call x1, Pallas kernels, final(): pl.pallas_call(final_body, name='final', out_shape=(shape((2048, CH), BF1...  3.03 us
  transfers between devices with their start and end apart: 4, of which 2 were waited for; matrix products, arithmetic and copies ran while one was open for 0% of the time, Pallas kernels for 27%

profile of v5, /device:TPU:1, one launch (start us, length us, event | category | flops | bytes accessed | tf_op | source)
XLA Modules:
  0.0 64.5 jit_solution(10722954720381906796)
XLA Ops:
  0.6 3.3 %route.1 = bf16[128,32,128]{2,1,0:T(8,128)(2,1)} custom-call(s32[1]{0:T(128)} %bitcast.late_ref, bf16[1024,128]{1,0:T(8,128)(2,1)} %features_hbm.1, s32[8,128]{1,0:T(8,128)} %bitcast.11), custom_call_target="tpu_custom_call" | custom-call | tf_op jit(solution)/shard_map/route/pallas_call | solution.py:92
  3.9 0.0 copy-start.1
  3.9 0.0 copy-start.2
  3.9 0.0 copy-start.3
  3.9 12.0 %all-to-all-start = ((bf16[128,32,128]{2,1,0:T(8,128)(2,1)}), bf16[128,32,128]{2,1,0:T(8,128)(2,1)}, u32[]{:S(2)}, u32[]{:S(2)}) async-start(bf16[128,32,128]{2,1,0:T(8,128)(2,1)} %route.1), calls=%async_computation | async-start | bytes 2097152 | tf_op jit(solution)/shard_map/all_to_all | solution.py:440
  15.9 0.0 copy-done.1
  15.9 0.0 copy-done.2
  15.9 0.0 copy-done.3
  15.9 0.5 prepare.1
  16.4 3.4 %collective-permute-start = (s32[27,256]{1,0:T(8,128)S(1)}, s32[27,256]{1,0:T(8,128)S(1)}, u32[]{:S(2)}, u32[]{:S(2)}) collective-permute-start(s32[27,256]{1,0:T(8,128)S(1)} %get-tuple-element.14), channel_id=1, source_target_pairs={{0,1},{1,2},{2,3},{3,4},{4,5},{5,6},{6,7},{7,8},{8,9},{9,10},{10,1... | collective-permute-start | bytes 82952 | tf_op jit(solution)/shard_map/ppermute | solution.py:452
  19.8 3.9 %collective-permute-start.1 = (s32[27,256]{1,0:T(8,128)S(1)}, s32[27,256]{1,0:T(8,128)S(1)}, u32[]{:S(2)}, u32[]{:S(2)}) collective-permute-start(s32[27,256]{1,0:T(8,128)S(1)} %get-tuple-element.15), channel_id=1, source_target_pairs={{1,0},{2,1},{3,2},{4,3},{5,4},{6,5},{7,6},{8,7},{9,8},{10,9},{11,1... | collective-permute-start | bytes 82952 | tf_op jit(solution)/shard_map/ppermute | solution.py:453
  23.8 11.2 %all-to-all-done.rows_hbm = bf16[128,32,128]{2,1,0:T(8,128)(2,1)} async-done(((bf16[128,32,128]{2,1,0:T(8,128)(2,1)}), bf16[128,32,128]{2,1,0:T(8,128)(2,1)}, u32[]{:S(2)}, u32[]{:S(2)}) %all-to-all-start) | async-done | bytes 1048608 | tf_op jit(solution)/shard_map/all_to_all | solution.py:440
  35.0 12.5 %convolve.1 = (f32[1,2048]{1,0:T(1,128)S(1)}, f32[9,128,256]{2,1,0:T(8,128)}, f32[128,2,128]{2,1,0:T(2,128)}) custom-call(bf16[128,32,128]{2,1,0:T(8,128)(2,1)} %all-to-all-done.rows_hbm, s32[432,128]{1,0:T(8,128)S(1)} %bitcast.7, bf16[128,3456]{1,0:T(8,128)(2,1)S(1)} %get-tuple-element.12.weights_hbm), custom_call_target="tpu_custom_call" | custom-call | flops 10871635968 | bytes 4194304 | tf_op jit(solution)/shard_map/convolve/pallas_call | solution.py:274
  47.5 4.0 %all-to-all-start.1 = ((f32[128,2,128]{2,1,0:T(2,128)}), f32[128,2,128]{2,1,0:T(2,128)S(1)}, u32[]{:S(2)}, u32[]{:S(2)}) async-start(f32[128,2,128]{2,1,0:T(2,128)} %get-tuple-element.13), calls=%async_computation.1 | async-start | bytes 262144 | tf_op jit(solution)/shard_map/all_to_all | solution.py:440
  51.5 0.0 collective-permute-done.before_ref
  51.5 0.0 collective-permute-done.1.after_ref
  51.6 0.0 copy-done.5
  51.6 0.0 copy-done.6
  51.6 0.0 copy-start
  51.6 0.0 copy-start.4
  51.6 4.2 %rims.1 = (f32[2,128,256]{2,1,0:T(8,128)S(1)}, f32[1,512]{1,0:T(1,128)S(1)}, f32[256,256]{1,0:T(8,128)S(1)}) custom-call(bf16[128,32,128]{2,1,0:T(8,128)(2,1)} %all-to-all-done.rows_hbm, s32[27,256]{1,0:T(8,128)S(1)} %collective-permute-done.before_ref, s32[27,256]{1,0:T(8,128)S(1)} %collective-permute-done.1.after_ref, ...), custom_call_target="tpu_custom_call" | custom-call | flops 2717908992 | bytes 4194304 | tf_op jit(solution)/shard_map/rims/pallas_call | solution.py:345
  55.8 5.7 %all-to-all-done.1.totals_ref = f32[128,2,128]{2,1,0:T(2,128)S(1)} async-done(((f32[128,2,128]{2,1,0:T(2,128)}), f32[128,2,128]{2,1,0:T(2,128)S(1)}, u32[]{:S(2)}, u32[]{:S(2)}) %all-to-all-start.1) | async-done | bytes 131104 | tf_op jit(solution)/shard_map/all_to_all | solution.py:440
  61.5 0.0 copy-done
  61.5 3.0 %final.1 = (bf16[2048,128]{1,0:T(8,128)(2,1)}, bf16[512,256]{1,0:T(8,128)(2,1)}) custom-call(f32[128,2,128]{2,1,0:T(2,128)S(1)} %all-to-all-done.1.totals_ref, f32[256,256]{1,0:T(8,128)S(1)} %get-tuple-element.16.columns_ref, f32[2,128,256]{2,1,0:T(8,128)S(1)} %get-tuple-element.17.rims_ref, f32[1,512]{1,0:T(1,128)S(1)} %get-tuple-element.18.rims_filled_ref, ...), custom_call_target="tpu_custom_call" | custom-call | tf_op jit(solution)/shard_map/final/pallas_call | solution.py:422
  (3 shorter events, 0.0 us)
Async XLA Ops:
  3.9 12.0 %copy-start.1 = (bf16[27,128,128]{2,1,0:T(8,128)(2,1)S(1)}, bf16[27,128,128]{2,1,0:T(8,128)(2,1)}, u32[]{:S(2)}) copy-start(bf16[27,128,128]{2,1,0:T(8,128)(2,1)} %weights_ref.1) | copy-start | bytes 2654212
  3.9 12.0 %copy-start.2 = (bf16[8,128,256]{2,1,0:T(8,128)(2,1)S(1)}, bf16[8,128,256]{2,1,0:T(8,128)(2,1)}, u32[]{:S(2)}) copy-start(bf16[8,128,256]{2,1,0:T(8,128)(2,1)} %down_ref.1) | copy-start | bytes 1572868
  3.9 12.0 %copy-start.3 = (s32[1,27,2048]{2,0,1:T(1,128)S(1)}, s32[1,27,2048]{2,0,1:T(1,128)}, u32[]{:S(2)}) copy-start(s32[1,27,2048]{2,0,1:T(1,128)} %param.10) | copy-start | bytes 663556
  3.9 31.0 %all-to-all-start = ((bf16[128,32,128]{2,1,0:T(8,128)(2,1)}), bf16[128,32,128]{2,1,0:T(8,128)(2,1)}, u32[]{:S(2)}, u32[]{:S(2)}) async-start(bf16[128,32,128]{2,1,0:T(8,128)(2,1)} %route.1), calls=%async_computation | async-start | bytes 2097152 | tf_op jit(solution)/shard_map/all_to_all | solution.py:440
  16.4 35.1 %collective-permute-start = (s32[27,256]{1,0:T(8,128)S(1)}, s32[27,256]{1,0:T(8,128)S(1)}, u32[]{:S(2)}, u32[]{:S(2)}) collective-permute-start(s32[27,256]{1,0:T(8,128)S(1)} %get-tuple-element.14), channel_id=1, source_target_pairs={{0,1},{1,2},{2,3},{3,4},{4,5},{5,6},{6,7},{7,8},{8,9},{9,10},{10,1... | collective-permute-start | bytes 82952 | tf_op jit(solution)/shard_map/ppermute | solution.py:452
  19.8 31.7 %collective-permute-start.1 = (s32[27,256]{1,0:T(8,128)S(1)}, s32[27,256]{1,0:T(8,128)S(1)}, u32[]{:S(2)}, u32[]{:S(2)}) collective-permute-start(s32[27,256]{1,0:T(8,128)S(1)} %get-tuple-element.15), channel_id=1, source_target_pairs={{1,0},{2,1},{3,2},{4,3},{5,4},{6,5},{7,6},{8,7},{9,8},{10,9},{11,1... | collective-permute-start | bytes 82952 | tf_op jit(solution)/shard_map/ppermute | solution.py:453
  35.0 16.6 %copy-start.5 = (f32[128]{0:T(128)S(1)}, f32[128]{0:T(128)}, u32[]{:S(2)}) copy-start(f32[128]{0:T(128)} %param.13) | copy-start | bytes 1540
  35.0 16.6 %copy-start.6 = (f32[128]{0:T(128)S(1)}, f32[128]{0:T(128)}, u32[]{:S(2)}) copy-start(f32[128]{0:T(128)} %param.14) | copy-start | bytes 1540
  47.5 14.0 %all-to-all-start.1 = ((f32[128,2,128]{2,1,0:T(2,128)}), f32[128,2,128]{2,1,0:T(2,128)S(1)}, u32[]{:S(2)}, u32[]{:S(2)}) async-start(f32[128,2,128]{2,1,0:T(2,128)} %get-tuple-element.13), calls=%async_computation.1 | async-start | bytes 262144 | tf_op jit(solution)/shard_map/all_to_all | solution.py:440
  51.6 9.9 %copy-start = (f32[9,128,256]{2,1,0:T(8,128)S(1)}, f32[9,128,256]{2,1,0:T(8,128)}, u32[]{:S(2)}) copy-start(f32[9,128,256]{2,1,0:T(8,128)} %get-tuple-element.19.conv_ref) | copy-start | bytes 3538948
  51.6 9.9 %copy-start.4 = (s32[1,8,512]{2,1,0:T(8,128)S(1)}, s32[1,8,512]{2,1,0:T(8,128)}, u32[]{:S(2)}) copy-start(s32[1,8,512]{2,1,0:T(8,128)} %param.11) | copy-start | bytes 49156

commit v6 on v5

--- a/solution.py
+++ b/solution.py
@@ -134,7 +134,7 @@
     )(index, weights, down)
 
 
-LANE_OFFSETS = 5
+LANE_OFFSETS = 6
 
 
 def turn(raw):
@@ -177,25 +177,27 @@
         def keep(k, value):
             gathered_ref[CH * k : CH * (k + 1), CH * half : CH * (half + 1)] = value
 
-        def by_matmul(k):
-            slots = [slots_of(k, half), slots_of(k + 1, half)]
+        def by_matmul(*pair):
+            slots = [slots_of(k, half) for k in pair]
             both = jnp.concatenate(slots, axis=1)
             low = jnp.where(both < 512, both & (SEG - 1), -1)
             found = jnp.dot(window, onehot(low, SEG, 0), preferred_element_type=F32)
             first = jnp.broadcast_to(both, (CH, SEG)) < SEG
             chosen = jnp.where(first, found[:CH], found[CH:]).astype(BF16)
             for n in range(2):
-                keep(k + n, from_tiles(slots[n], chosen[:, CH * n : CH * (n + 1)], [4]))
+                keep(pair[n], from_tiles(slots[n], chosen[:, CH * n : CH * (n + 1)], [4]))
 
         def by_lanes(k):
             keep(k, from_tiles(slots_of(k, half), jnp.zeros((CH, CH), BF16), range(5)))
 
-        pairs = (27 - LANE_OFFSETS) // 2
+        keep(13, tiles[2])
+        offsets = [k for k in range(27) if k != 13]
+        pairs = (26 - LANE_OFFSETS) // 2
         done = 2 * pairs
         for n in range(pairs):
-            by_matmul(2 * n)
-            while done < 27 and (done - 2 * pairs + 1) * pairs <= (n + 1) * (LANE_OFFSETS + 0.5):
-                by_lanes(done)
+            by_matmul(offsets[2 * n], offsets[2 * n + 1])
+            while done < 26 and (done - 2 * pairs + 1) * pairs <= (n + 1) * (LANE_OFFSETS + 0.5):
+                by_lanes(offsets[done])
                 done += 1
 
 
@@ -204,9 +206,9 @@
 
 
 def conv_body(
-    rows_hbm, index_hbm, weights_hbm, filled_ref, conv_hbm, send_ref,
+    rows_hbm, index_ref, weights_ref, filled_ref, conv_hbm, send_hbm,
     rows_ref, rims_ref, even_ref, odd_ref, conv_ref, sums_ref, first_ref, second_ref,
-    index_ref, weights_ref, in_sems, out_sems,
+    send_ref, in_sems, out_sems,
 ):
     gets = [
         pltpu.make_async_copy(rows_hbm.at[112:, 16:], rims_ref.at[:16], in_sems.at[0]),
@@ -217,9 +219,7 @@
         )
         for n in range(4)
     ]
-    get_index = pltpu.make_async_copy(index_hbm, index_ref, in_sems.at[6])
-    get_weights = pltpu.make_async_copy(weights_hbm, weights_ref, in_sems.at[7])
-    for get in gets + [get_index, get_weights]:
+    for get in gets:
         get.start()
     sums_ref[...] = jnp.zeros_like(sums_ref)
     second_ref[...] = jnp.zeros_like(second_ref)
@@ -235,8 +235,6 @@
         table, filled = turn(rows_ref[8 * (t - 2) : 8 * (t - 1)].reshape(CH, CH))
         put_tile(even_ref, odd_ref, t, table)
         filled_ref[:, CH * (t - 2) : CH * (t - 1)] = filled
-    get_index.wait()
-    get_weights.wait()
 
     def finish(conv, at, block):
         conv_ref[at] = conv
@@ -266,8 +264,11 @@
         total = sums_ref[CH * n : CH * (n + 1)]
         row = jnp.sum((total[:, :CH] + total[:, CH:]).T, axis=0, keepdims=True)
         send_ref[:, n : n + 1, :] = jnp.broadcast_to(row[None], (128, 1, CH))
+    send = pltpu.make_async_copy(send_ref, send_hbm, out_sems.at[9])
+    send.start()
     for n in range(9):
         pltpu.make_async_copy(conv_ref.at[n], conv_hbm.at[n], out_sems.at[n]).wait()
+    send.wait()
 
 
 def convolve(rows, index, weights):
@@ -275,8 +276,8 @@
         conv_body,
         name="convolve",
         out_shape=(shape((1, 2048), F32), shape((9, CH, SEG), F32), shape((128, 2, CH), F32)),
-        in_specs=[HBM] * 3,
-        out_specs=(VMEM, HBM, VMEM),
+        in_specs=[HBM, VMEM, VMEM],
+        out_specs=(VMEM, HBM, HBM),
         scratch_shapes=[
             pltpu.VMEM((128, 16, CH), BF16),
             pltpu.VMEM((32, 16, CH), BF16),
@@ -286,10 +287,9 @@
             pltpu.VMEM((2 * CH, SEG), F32),
             pltpu.VMEM((27 * CH, SEG), BF16),
             pltpu.VMEM((27 * CH, SEG), BF16),
-            pltpu.VMEM((432, 128), jnp.int32),
-            pltpu.VMEM((CH, 27 * CH), BF16),
-            pltpu.SemaphoreType.DMA((8,)),
-            pltpu.SemaphoreType.DMA((9,)),
+            pltpu.VMEM((128, 2, CH), F32),
+            pltpu.SemaphoreType.DMA((6,)),
+            pltpu.SemaphoreType.DMA((10,)),
         ],
         compiler_params=params(52),
         cost_estimate=pl.CostEstimate(
@@ -304,9 +304,9 @@
 
 
 def rims_body(
-    rows_hbm, before_ref, after_ref, weights_hbm, gain_ref, shift_ref,
+    rows_hbm, before_ref, after_ref, weights_ref, gain_ref, shift_ref,
     conv_ref, filled_ref, columns_ref,
-    rows_ref, even_ref, odd_ref, first_ref, second_ref, weights_ref, sems,
+    rows_ref, even_ref, odd_ref, first_ref, second_ref, sems,
 ):
     places = [
         (rows_hbm.at[96:, 16:], 0), (rows_hbm.at[:16, :16], 32),
@@ -316,8 +316,7 @@
         pltpu.make_async_copy(src, rows_ref.at[at : at + src.shape[0]], sems.at[n])
         for n, (src, at) in enumerate(places)
     ]
-    get_weights = pltpu.make_async_copy(weights_hbm, weights_ref, sems.at[4])
-    for get in gets + [get_weights]:
+    for get in gets:
         get.start()
     columns_ref[:CH] = column(gain_ref[...])
     columns_ref[CH:] = column(shift_ref[...])
@@ -336,8 +335,6 @@
             return index_ref[k : k + 1, CH * half : CH * (half + 1)]
 
         gather_block(even_ref.at[side], odd_ref.at[side], 0, slots_of, gathered_ref)
-        if side == 0:
-            get_weights.wait()
         conv_ref[side] = product(weights_ref, gathered_ref)
 
 
@@ -346,7 +343,7 @@
         rims_body,
         name="rims",
         out_shape=(shape((2, CH, SEG), F32), shape((1, 2 * SEG), F32), shape((2 * CH, SEG), F32)),
-        in_specs=[HBM, VMEM, VMEM, HBM, VMEM, VMEM],
+        in_specs=[HBM] + [VMEM] * 5,
         out_specs=(VMEM,) * 3,
         scratch_shapes=[
             pltpu.VMEM((96, 16, CH), BF16),
@@ -354,8 +351,7 @@
             pltpu.VMEM((2, 3 * CH, SEG), BF16),
             pltpu.VMEM((27 * CH, SEG), BF16),
             pltpu.VMEM((27 * CH, SEG), BF16),
-            pltpu.VMEM((CH, 27 * CH), BF16),
-            pltpu.SemaphoreType.DMA((5,)),
+            pltpu.SemaphoreType.DMA((4,)),
         ],
         compiler_params=params(52),
         cost_estimate=pl.CostEstimate(
@@ -364,13 +360,21 @@
     )(rows, before, after, weights, gain, shift)
 
 
-def pick(window, local):
-    low = jnp.dot(window, onehot(local & (SEG - 1), SEG, 0), preferred_element_type=F32)
-    high = jnp.broadcast_to(local >> 8, (CH, SEG))
-    out = jnp.zeros((CH, SEG), F32)
-    for s in range(window.shape[0] // CH):
-        out = jnp.where(high == s, low[CH * s : CH * (s + 1)], out)
-    return out.astype(BF16)
+def pick_both(window, tiles, slots):
+    both = jnp.concatenate(slots, axis=1)
+    low = jnp.where(both < 768, both & (SEG - 1), -1)
+    found = jnp.dot(window, onehot(low, SEG, 0), preferred_element_type=F32)
+    high = jnp.broadcast_to(both >> 8, (CH, SEG))
+    out = jnp.where(high == 0, found[:CH], jnp.where(high == 1, found[CH : 2 * CH], found[2 * CH :])).astype(BF16)
+    outs = []
+    for n in range(2):
+        lane = jnp.broadcast_to((slots[n] & 127).astype(jnp.int16), (CH, CH))
+        where = jnp.broadcast_to((slots[n] >> 7).astype(jnp.int16), (CH, CH))
+        value = out[:, CH * n : CH * (n + 1)]
+        for t in range(2):
+            value = jnp.where(where == 6 + t, lanes_of(tiles[t], lane), value)
+        outs.append(value)
+    return outs
 
 
 def final_body(
@@ -398,15 +402,13 @@
             put.start()
             puts.append(put)
     for b in range(4):
-        window = table_ref[2 * CH * b : 2 * CH * b + 4 * CH, :]
+        window = table_ref[2 * CH * b : 2 * CH * b + 3 * CH, :]
+        last = table_ref[2 * CH * b + 3 * CH : 2 * CH * b + 4 * CH, :]
         for k in range(0, 8, 2):
-            index = jnp.concatenate(
-                [index_ref[k : k + 1, CH * b : CH * (b + 1)], index_ref[k + 1 : k + 2, CH * b : CH * (b + 1)]],
-                axis=1,
-            )
-            chosen = pick(window, index - 2 * SEG * b)
-            gathered_ref[CH * k : CH * (k + 1), CH * b : CH * (b + 1)] = chosen[:, :CH]
-            gathered_ref[CH * (k + 1) : CH * (k + 2), CH * b : CH * (b + 1)] = chosen[:, CH:]
+            slots = [index_ref[k + n : k + n + 1, CH * b : CH * (b + 1)] - 2 * SEG * b for n in range(2)]
+            chosen = pick_both(window, [last[:, :CH], last[:, CH:]], slots)
+            for n in range(2):
+                gathered_ref[CH * (k + n) : CH * (k + n + 1), CH * b : CH * (b + 1)] = chosen[n]
         if b % 2:
             part = slice(SEG * (b // 2), SEG * (b // 2 + 1))
             out = jnp.dot(weights_ref[...], gathered_ref[:, part], preferred_element_type=F32)

time: 64.8 us -> 64.5 us (level)
  transfers between devices with their start and end apart: 4 -> 4, of which waited for: 2 -> 2; matrix products, arithmetic and copies ran while one was open for 0% -> 0% of each run, Pallas kernels for 27% -> 26%
where the time goes in v6:
time: 64.5 us; the launch traced here: 64.2 us
  starting transfers between devices  23.3 us (36%)
  Pallas kernels  22.9 us (36%)
  waiting for transfers between devices  17.1 us (27%)
  between operations  0.79 us (1%)
    all_to_all x2, waiting for transfers between devices, exchange(): return lax.all_to_all(rows, AXES, split_axis=0, concat_axis=0, tiled=True)  17.1 us
    all_to_all x2, starting transfers between devices, exchange(): return lax.all_to_all(rows, AXES, split_axis=0, concat_axis=0, tiled=True)  16 us
    pallas_call x1, Pallas kernels, convolve(): pl.pallas_call(conv_body, name='convolve', out_shape=(shape((1, 2048), F3...  12.4 us
    pallas_call x1, Pallas kernels, rims(): pl.pallas_call(rims_body, name='rims', out_shape=(shape((2, CH, SEG), F32...  3.96 us
    ppermute x1, starting transfers between devices, shards(): after = lax.ppermute(head, AXES, down)  3.92 us
    ppermute x1, starting transfers between devices, shards(): before = lax.ppermute(tail, AXES, up)  3.42 us
    pallas_call x1, Pallas kernels, route(): pl.pallas_call(route_body, name='route', out_shape=shape((128, 32, CH), B...  3.26 us
    pallas_call x1, Pallas kernels, final(): pl.pallas_call(final_body, name='final', out_shape=(shape((2048, CH), BF1...  2.82 us
  transfers between devices with their start and end apart: 4, of which 2 were waited for; matrix products, arithmetic and copies ran while one was open for 0% of the time, Pallas kernels for 26%

profile of v6, /device:TPU:1, one launch (start us, length us, event | category | flops | bytes accessed | tf_op | source)
XLA Modules:
  0.0 64.2 jit_solution(5262599019657616758)
XLA Ops:
  0.6 3.3 %route.1 = bf16[128,32,128]{2,1,0:T(8,128)(2,1)} custom-call(s32[1]{0:T(128)} %bitcast.late_ref, bf16[1024,128]{1,0:T(8,128)(2,1)} %features_hbm.1, s32[8,128]{1,0:T(8,128)} %bitcast.11), custom_call_target="tpu_custom_call" | custom-call | tf_op jit(solution)/shard_map/route/pallas_call | solution.py:92
  3.9 0.0 copy-start.1
  3.9 0.0 copy-start.2
  3.9 0.0 copy-start.3
  3.9 12.0 %all-to-all-start = ((bf16[128,32,128]{2,1,0:T(8,128)(2,1)}), bf16[128,32,128]{2,1,0:T(8,128)(2,1)}, u32[]{:S(2)}, u32[]{:S(2)}) async-start(bf16[128,32,128]{2,1,0:T(8,128)(2,1)} %route.1), calls=%async_computation | async-start | bytes 2097152 | tf_op jit(solution)/shard_map/all_to_all | solution.py:442
  15.9 0.0 copy-done.1
  15.9 0.0 copy-done.2
  15.9 0.0 copy-done.3
  15.9 0.5 prepare.1
  16.4 3.4 %collective-permute-start = (s32[27,256]{1,0:T(8,128)S(1)}, s32[27,256]{1,0:T(8,128)S(1)}, u32[]{:S(2)}, u32[]{:S(2)}) collective-permute-start(s32[27,256]{1,0:T(8,128)S(1)} %get-tuple-element.14), channel_id=1, source_target_pairs={{0,1},{1,2},{2,3},{3,4},{4,5},{5,6},{6,7},{7,8},{8,9},{9,10},{10,1... | collective-permute-start | bytes 82952 | tf_op jit(solution)/shard_map/ppermute | solution.py:454
  19.8 3.9 %collective-permute-start.1 = (s32[27,256]{1,0:T(8,128)S(1)}, s32[27,256]{1,0:T(8,128)S(1)}, u32[]{:S(2)}, u32[]{:S(2)}) collective-permute-start(s32[27,256]{1,0:T(8,128)S(1)} %get-tuple-element.15), channel_id=1, source_target_pairs={{1,0},{2,1},{3,2},{4,3},{5,4},{6,5},{7,6},{8,7},{9,8},{10,9},{11,1... | collective-permute-start | bytes 82952 | tf_op jit(solution)/shard_map/ppermute | solution.py:455
  23.8 11.2 %all-to-all-done.rows_hbm = bf16[128,32,128]{2,1,0:T(8,128)(2,1)} async-done(((bf16[128,32,128]{2,1,0:T(8,128)(2,1)}), bf16[128,32,128]{2,1,0:T(8,128)(2,1)}, u32[]{:S(2)}, u32[]{:S(2)}) %all-to-all-start) | async-done | bytes 1048608 | tf_op jit(solution)/shard_map/all_to_all | solution.py:442
  35.0 12.4 %convolve.1 = (f32[1,2048]{1,0:T(1,128)S(1)}, f32[9,128,256]{2,1,0:T(8,128)}, f32[128,2,128]{2,1,0:T(2,128)}) custom-call(bf16[128,32,128]{2,1,0:T(8,128)(2,1)} %all-to-all-done.rows_hbm, s32[432,128]{1,0:T(8,128)S(1)} %bitcast.7, bf16[128,3456]{1,0:T(8,128)(2,1)S(1)} %get-tuple-element.12.weights_ref), custom_call_target="tpu_custom_call" | custom-call | flops 10871635968 | bytes 4194304 | tf_op jit(solution)/shard_map/convolve/pallas_call | solution.py:275
  47.4 4.0 %all-to-all-start.1 = ((f32[128,2,128]{2,1,0:T(2,128)}), f32[128,2,128]{2,1,0:T(2,128)S(1)}, u32[]{:S(2)}, u32[]{:S(2)}) async-start(f32[128,2,128]{2,1,0:T(2,128)} %get-tuple-element.13), calls=%async_computation.1 | async-start | bytes 262144 | tf_op jit(solution)/shard_map/all_to_all | solution.py:442
  51.4 0.0 collective-permute-done.before_ref
  51.4 0.0 collective-permute-done.1.after_ref
  51.4 0.0 copy-done.5
  51.4 0.0 copy-done.6
  51.5 0.0 copy-start
  51.5 0.0 copy-start.4
  51.5 4.0 %rims.1 = (f32[2,128,256]{2,1,0:T(8,128)S(1)}, f32[1,512]{1,0:T(1,128)S(1)}, f32[256,256]{1,0:T(8,128)S(1)}) custom-call(bf16[128,32,128]{2,1,0:T(8,128)(2,1)} %all-to-all-done.rows_hbm, s32[27,256]{1,0:T(8,128)S(1)} %collective-permute-done.before_ref, s32[27,256]{1,0:T(8,128)S(1)} %collective-permute-done.1.after_ref, ...), custom_call_target="tpu_custom_call" | custom-call | flops 2717908992 | bytes 4194304 | tf_op jit(solution)/shard_map/rims/pallas_call | solution.py:342
  55.5 5.9 %all-to-all-done.1.totals_ref = f32[128,2,128]{2,1,0:T(2,128)S(1)} async-done(((f32[128,2,128]{2,1,0:T(2,128)}), f32[128,2,128]{2,1,0:T(2,128)S(1)}, u32[]{:S(2)}, u32[]{:S(2)}) %all-to-all-start.1) | async-done | bytes 131104 | tf_op jit(solution)/shard_map/all_to_all | solution.py:442
  61.4 0.0 copy-done.4
  61.4 2.8 %final.1 = (bf16[2048,128]{1,0:T(8,128)(2,1)}, bf16[512,256]{1,0:T(8,128)(2,1)}) custom-call(f32[128,2,128]{2,1,0:T(2,128)S(1)} %all-to-all-done.1.totals_ref, f32[256,256]{1,0:T(8,128)S(1)} %get-tuple-element.16.columns_ref, f32[2,128,256]{2,1,0:T(8,128)S(1)} %get-tuple-element.17.rims_ref, f32[1,512]{1,0:T(1,128)S(1)} %get-tuple-element.18.rims_filled_ref, ...), custom_call_target="tpu_custom_call" | custom-call | tf_op jit(solution)/shard_map/final/pallas_call | solution.py:424
  (3 shorter events, 0.0 us)
Async XLA Ops:
  3.9 12.0 %copy-start.1 = (bf16[27,128,128]{2,1,0:T(8,128)(2,1)S(1)}, bf16[27,128,128]{2,1,0:T(8,128)(2,1)}, u32[]{:S(2)}) copy-start(bf16[27,128,128]{2,1,0:T(8,128)(2,1)} %weights_ref.1) | copy-start | bytes 2654212
  3.9 12.0 %copy-start.2 = (bf16[8,128,256]{2,1,0:T(8,128)(2,1)S(1)}, bf16[8,128,256]{2,1,0:T(8,128)(2,1)}, u32[]{:S(2)}) copy-start(bf16[8,128,256]{2,1,0:T(8,128)(2,1)} %down_ref.1) | copy-start | bytes 1572868
  3.9 12.0 %copy-start.3 = (s32[1,27,2048]{2,0,1:T(1,128)S(1)}, s32[1,27,2048]{2,0,1:T(1,128)}, u32[]{:S(2)}) copy-start(s32[1,27,2048]{2,0,1:T(1,128)} %param.10) | copy-start | bytes 663556
  3.9 31.0 %all-to-all-start = ((bf16[128,32,128]{2,1,0:T(8,128)(2,1)}), bf16[128,32,128]{2,1,0:T(8,128)(2,1)}, u32[]{:S(2)}, u32[]{:S(2)}) async-start(bf16[128,32,128]{2,1,0:T(8,128)(2,1)} %route.1), calls=%async_computation | async-start | bytes 2097152 | tf_op jit(solution)/shard_map/all_to_all | solution.py:442
  16.4 35.0 %collective-permute-start = (s32[27,256]{1,0:T(8,128)S(1)}, s32[27,256]{1,0:T(8,128)S(1)}, u32[]{:S(2)}, u32[]{:S(2)}) collective-permute-start(s32[27,256]{1,0:T(8,128)S(1)} %get-tuple-element.14), channel_id=1, source_target_pairs={{0,1},{1,2},{2,3},{3,4},{4,5},{5,6},{6,7},{7,8},{8,9},{9,10},{10,1... | collective-permute-start | bytes 82952 | tf_op jit(solution)/shard_map/ppermute | solution.py:454
  19.8 31.6 %collective-permute-start.1 = (s32[27,256]{1,0:T(8,128)S(1)}, s32[27,256]{1,0:T(8,128)S(1)}, u32[]{:S(2)}, u32[]{:S(2)}) collective-permute-start(s32[27,256]{1,0:T(8,128)S(1)} %get-tuple-element.15), channel_id=1, source_target_pairs={{1,0},{2,1},{3,2},{4,3},{5,4},{6,5},{7,6},{8,7},{9,8},{10,9},{11,1... | collective-permute-start | bytes 82952 | tf_op jit(solution)/shard_map/ppermute | solution.py:455
  35.0 16.5 %copy-start.5 = (f32[128]{0:T(128)S(1)}, f32[128]{0:T(128)}, u32[]{:S(2)}) copy-start(f32[128]{0:T(128)} %param.13) | copy-start | bytes 1540
  35.0 16.5 %copy-start.6 = (f32[128]{0:T(128)S(1)}, f32[128]{0:T(128)}, u32[]{:S(2)}) copy-start(f32[128]{0:T(128)} %param.14) | copy-start | bytes 1540
  47.4 14.0 %all-to-all-start.1 = ((f32[128,2,128]{2,1,0:T(2,128)}), f32[128,2,128]{2,1,0:T(2,128)S(1)}, u32[]{:S(2)}, u32[]{:S(2)}) async-start(f32[128,2,128]{2,1,0:T(2,128)} %get-tuple-element.13), calls=%async_computation.1 | async-start | bytes 262144 | tf_op jit(solution)/shard_map/all_to_all | solution.py:442
  51.5 9.9 %copy-start = (f32[9,128,256]{2,1,0:T(8,128)S(1)}, f32[9,128,256]{2,1,0:T(8,128)}, u32[]{:S(2)}) copy-start(f32[9,128,256]{2,1,0:T(8,128)} %get-tuple-element.19.conv_ref) | copy-start | bytes 3538948
  51.5 9.9 %copy-start.4 = (s32[1,8,512]{2,1,0:T(8,128)S(1)}, s32[1,8,512]{2,1,0:T(8,128)}, u32[]{:S(2)}) copy-start(s32[1,8,512]{2,1,0:T(8,128)} %param.11) | copy-start | bytes 49156

commit v7 on v6

--- a/solution.py
+++ b/solution.py
@@ -215,9 +215,9 @@
         pltpu.make_async_copy(rows_hbm.at[:16, 16:], rims_ref.at[16:], in_sems.at[1]),
     ] + [
         pltpu.make_async_copy(
-            rows_hbm.at[32 * n : 32 * (n + 1), :16], rows_ref.at[32 * n : 32 * (n + 1)], in_sems.at[2 + n]
+            rows_hbm.at[64 * n : 64 * (n + 1), :16], rows_ref.at[64 * n : 64 * (n + 1)], in_sems.at[2 + n]
         )
-        for n in range(4)
+        for n in range(2)
     ]
     for get in gets:
         get.start()
@@ -230,8 +230,8 @@
         table, _ = turn(rims_ref[8 * n : 8 * (n + 1)].reshape(CH, CH))
         put_tile(even_ref, odd_ref, t, table)
     for t in range(2, 18):
-        if t % 4 == 2:
-            gets[2 + t // 4].wait()
+        if t % 8 == 2:
+            gets[2 + t // 8].wait()
         table, filled = turn(rows_ref[8 * (t - 2) : 8 * (t - 1)].reshape(CH, CH))
         put_tile(even_ref, odd_ref, t, table)
         filled_ref[:, CH * (t - 2) : CH * (t - 1)] = filled

time: 64.5 us -> 64.4 us (level)
  no operation moved by 1% of the time
where the time goes in v7:
time: 64.4 us; the launch traced here: 64.1 us
  starting transfers between devices  23.3 us (36%)
  Pallas kernels  22.8 us (35%)
  waiting for transfers between devices  17.1 us (27%)
  between operations  0.79 us (1%)
    all_to_all x2, waiting for transfers between devices, exchange(): return lax.all_to_all(rows, AXES, split_axis=0, concat_axis=0, tiled=True)  17.1 us
    all_to_all x2, starting transfers between devices, exchange(): return lax.all_to_all(rows, AXES, split_axis=0, concat_axis=0, tiled=True)  16 us
    pallas_call x1, Pallas kernels, convolve(): pl.pallas_call(conv_body, name='convolve', out_shape=(shape((1, 2048), F3...  12.3 us
    pallas_call x1, Pallas kernels, rims(): pl.pallas_call(rims_body, name='rims', out_shape=(shape((2, CH, SEG), F32...  3.97 us
    ppermute x1, starting transfers between devices, shards(): after = lax.ppermute(head, AXES, down)  3.92 us
    ppermute x1, starting transfers between devices, shards(): before = lax.ppermute(tail, AXES, up)  3.42 us
    pallas_call x1, Pallas kernels, route(): pl.pallas_call(route_body, name='route', out_shape=shape((128, 32, CH), B...  3.26 us
    pallas_call x1, Pallas kernels, final(): pl.pallas_call(final_body, name='final', out_shape=(shape((2048, CH), BF1...  2.82 us
  transfers between devices with their start and end apart: 4, of which 2 were waited for; matrix products, arithmetic and copies ran while one was open for 0% of the time, Pallas kernels for 26%

profile of v7, /device:TPU:1, one launch (start us, length us, event | category | flops | bytes accessed | tf_op | source)
XLA Modules:
  0.0 64.1 jit_solution(436334665888050706)
XLA Ops:
  0.6 3.3 %route.1 = bf16[128,32,128]{2,1,0:T(8,128)(2,1)} custom-call(s32[1]{0:T(128)} %bitcast.late_ref, bf16[1024,128]{1,0:T(8,128)(2,1)} %features_hbm.1, s32[8,128]{1,0:T(8,128)} %bitcast.11), custom_call_target="tpu_custom_call" | custom-call | tf_op jit(solution)/shard_map/route/pallas_call | solution.py:92
  3.9 0.0 copy-start.1
  3.9 0.0 copy-start.2
  3.9 0.0 copy-start.3
  3.9 12.0 %all-to-all-start = ((bf16[128,32,128]{2,1,0:T(8,128)(2,1)}), bf16[128,32,128]{2,1,0:T(8,128)(2,1)}, u32[]{:S(2)}, u32[]{:S(2)}) async-start(bf16[128,32,128]{2,1,0:T(8,128)(2,1)} %route.1), calls=%async_computation | async-start | bytes 2097152 | tf_op jit(solution)/shard_map/all_to_all | solution.py:442
  15.9 0.0 copy-done.1
  15.9 0.0 copy-done.2
  15.9 0.0 copy-done.3
  15.9 0.5 prepare.1
  16.4 3.4 %collective-permute-start = (s32[27,256]{1,0:T(8,128)S(1)}, s32[27,256]{1,0:T(8,128)S(1)}, u32[]{:S(2)}, u32[]{:S(2)}) collective-permute-start(s32[27,256]{1,0:T(8,128)S(1)} %get-tuple-element.14), channel_id=1, source_target_pairs={{0,1},{1,2},{2,3},{3,4},{4,5},{5,6},{6,7},{7,8},{8,9},{9,10},{10,1... | collective-permute-start | bytes 82952 | tf_op jit(solution)/shard_map/ppermute | solution.py:454
  19.8 3.9 %collective-permute-start.1 = (s32[27,256]{1,0:T(8,128)S(1)}, s32[27,256]{1,0:T(8,128)S(1)}, u32[]{:S(2)}, u32[]{:S(2)}) collective-permute-start(s32[27,256]{1,0:T(8,128)S(1)} %get-tuple-element.15), channel_id=1, source_target_pairs={{1,0},{2,1},{3,2},{4,3},{5,4},{6,5},{7,6},{8,7},{9,8},{10,9},{11,1... | collective-permute-start | bytes 82952 | tf_op jit(solution)/shard_map/ppermute | solution.py:455
  23.8 11.2 %all-to-all-done.rows_hbm = bf16[128,32,128]{2,1,0:T(8,128)(2,1)} async-done(((bf16[128,32,128]{2,1,0:T(8,128)(2,1)}), bf16[128,32,128]{2,1,0:T(8,128)(2,1)}, u32[]{:S(2)}, u32[]{:S(2)}) %all-to-all-start) | async-done | bytes 1048608 | tf_op jit(solution)/shard_map/all_to_all | solution.py:442
  35.0 12.3 %convolve.1 = (f32[1,2048]{1,0:T(1,128)S(1)}, f32[9,128,256]{2,1,0:T(8,128)}, f32[128,2,128]{2,1,0:T(2,128)}) custom-call(bf16[128,32,128]{2,1,0:T(8,128)(2,1)} %all-to-all-done.rows_hbm, s32[432,128]{1,0:T(8,128)S(1)} %bitcast.7, bf16[128,3456]{1,0:T(8,128)(2,1)S(1)} %get-tuple-element.12.weights_ref), custom_call_target="tpu_custom_call" | custom-call | flops 10871635968 | bytes 4194304 | tf_op jit(solution)/shard_map/convolve/pallas_call | solution.py:275
  47.3 4.1 %all-to-all-start.1 = ((f32[128,2,128]{2,1,0:T(2,128)}), f32[128,2,128]{2,1,0:T(2,128)S(1)}, u32[]{:S(2)}, u32[]{:S(2)}) async-start(f32[128,2,128]{2,1,0:T(2,128)} %get-tuple-element.13), calls=%async_computation.1 | async-start | bytes 262144 | tf_op jit(solution)/shard_map/all_to_all | solution.py:442
  51.3 0.0 collective-permute-done.before_ref
  51.3 0.0 collective-permute-done.1.after_ref
  51.3 0.0 copy-done.5
  51.3 0.0 copy-done.6
  51.4 0.0 copy-start
  51.4 0.0 copy-start.4
  51.4 4.0 %rims.1 = (f32[2,128,256]{2,1,0:T(8,128)S(1)}, f32[1,512]{1,0:T(1,128)S(1)}, f32[256,256]{1,0:T(8,128)S(1)}) custom-call(bf16[128,32,128]{2,1,0:T(8,128)(2,1)} %all-to-all-done.rows_hbm, s32[27,256]{1,0:T(8,128)S(1)} %collective-permute-done.before_ref, s32[27,256]{1,0:T(8,128)S(1)} %collective-permute-done.1.after_ref, ...), custom_call_target="tpu_custom_call" | custom-call | flops 2717908992 | bytes 4194304 | tf_op jit(solution)/shard_map/rims/pallas_call | solution.py:342
  55.4 5.9 %all-to-all-done.1.totals_ref = f32[128,2,128]{2,1,0:T(2,128)S(1)} async-done(((f32[128,2,128]{2,1,0:T(2,128)}), f32[128,2,128]{2,1,0:T(2,128)S(1)}, u32[]{:S(2)}, u32[]{:S(2)}) %all-to-all-start.1) | async-done | bytes 131104 | tf_op jit(solution)/shard_map/all_to_all | solution.py:442
  61.3 0.0 copy-done
  61.3 2.8 %final.1 = (bf16[2048,128]{1,0:T(8,128)(2,1)}, bf16[512,256]{1,0:T(8,128)(2,1)}) custom-call(f32[128,2,128]{2,1,0:T(2,128)S(1)} %all-to-all-done.1.totals_ref, f32[256,256]{1,0:T(8,128)S(1)} %get-tuple-element.16.columns_ref, f32[2,128,256]{2,1,0:T(8,128)S(1)} %get-tuple-element.17.rims_ref, f32[1,512]{1,0:T(1,128)S(1)} %get-tuple-element.18.rims_filled_ref, ...), custom_call_target="tpu_custom_call" | custom-call | tf_op jit(solution)/shard_map/final/pallas_call | solution.py:424
  (3 shorter events, 0.0 us)
Async XLA Ops:
  3.9 12.0 %copy-start.1 = (bf16[27,128,128]{2,1,0:T(8,128)(2,1)S(1)}, bf16[27,128,128]{2,1,0:T(8,128)(2,1)}, u32[]{:S(2)}) copy-start(bf16[27,128,128]{2,1,0:T(8,128)(2,1)} %weights_ref.1) | copy-start | bytes 2654212
  3.9 12.0 %copy-start.2 = (bf16[8,128,256]{2,1,0:T(8,128)(2,1)S(1)}, bf16[8,128,256]{2,1,0:T(8,128)(2,1)}, u32[]{:S(2)}) copy-start(bf16[8,128,256]{2,1,0:T(8,128)(2,1)} %down_ref.1) | copy-start | bytes 1572868
  3.9 12.0 %copy-start.3 = (s32[1,27,2048]{2,0,1:T(1,128)S(1)}, s32[1,27,2048]{2,0,1:T(1,128)}, u32[]{:S(2)}) copy-start(s32[1,27,2048]{2,0,1:T(1,128)} %param.10) | copy-start | bytes 663556
  3.9 31.0 %all-to-all-start = ((bf16[128,32,128]{2,1,0:T(8,128)(2,1)}), bf16[128,32,128]{2,1,0:T(8,128)(2,1)}, u32[]{:S(2)}, u32[]{:S(2)}) async-start(bf16[128,32,128]{2,1,0:T(8,128)(2,1)} %route.1), calls=%async_computation | async-start | bytes 2097152 | tf_op jit(solution)/shard_map/all_to_all | solution.py:442
  16.4 34.9 %collective-permute-start = (s32[27,256]{1,0:T(8,128)S(1)}, s32[27,256]{1,0:T(8,128)S(1)}, u32[]{:S(2)}, u32[]{:S(2)}) collective-permute-start(s32[27,256]{1,0:T(8,128)S(1)} %get-tuple-element.14), channel_id=1, source_target_pairs={{0,1},{1,2},{2,3},{3,4},{4,5},{5,6},{6,7},{7,8},{8,9},{9,10},{10,1... | collective-permute-start | bytes 82952 | tf_op jit(solution)/shard_map/ppermute | solution.py:454
  19.8 31.5 %collective-permute-start.1 = (s32[27,256]{1,0:T(8,128)S(1)}, s32[27,256]{1,0:T(8,128)S(1)}, u32[]{:S(2)}, u32[]{:S(2)}) collective-permute-start(s32[27,256]{1,0:T(8,128)S(1)} %get-tuple-element.15), channel_id=1, source_target_pairs={{1,0},{2,1},{3,2},{4,3},{5,4},{6,5},{7,6},{8,7},{9,8},{10,9},{11,1... | collective-permute-start | bytes 82952 | tf_op jit(solution)/shard_map/ppermute | solution.py:455
  35.0 16.4 %copy-start.5 = (f32[128]{0:T(128)S(1)}, f32[128]{0:T(128)}, u32[]{:S(2)}) copy-start(f32[128]{0:T(128)} %param.13) | copy-start | bytes 1540
  35.0 16.4 %copy-start.6 = (f32[128]{0:T(128)S(1)}, f32[128]{0:T(128)}, u32[]{:S(2)}) copy-start(f32[128]{0:T(128)} %param.14) | copy-start | bytes 1540
  47.3 14.0 %all-to-all-start.1 = ((f32[128,2,128]{2,1,0:T(2,128)}), f32[128,2,128]{2,1,0:T(2,128)S(1)}, u32[]{:S(2)}, u32[]{:S(2)}) async-start(f32[128,2,128]{2,1,0:T(2,128)} %get-tuple-element.13), calls=%async_computation.1 | async-start | bytes 262144 | tf_op jit(solution)/shard_map/all_to_all | solution.py:442
  51.4 9.9 %copy-start = (f32[9,128,256]{2,1,0:T(8,128)S(1)}, f32[9,128,256]{2,1,0:T(8,128)}, u32[]{:S(2)}) copy-start(f32[9,128,256]{2,1,0:T(8,128)} %get-tuple-element.19.conv_ref) | copy-start | bytes 3538948
  51.4 9.9 %copy-start.4 = (s32[1,8,512]{2,1,0:T(8,128)S(1)}, s32[1,8,512]{2,1,0:T(8,128)}, u32[]{:S(2)}) copy-start(s32[1,8,512]{2,1,0:T(8,128)} %param.11) | copy-start | bytes 49156
